TPU v7x, 512 devices: a whole 4x8x8 slice. The times are simulated.
512 devices in a mesh: seq: 64 (over z, x, core), chan: 8 (over y).
Axes of the slice: x: 4, y: 8, z: 8, core: 2. Of those that a mesh axis runs over, the one named last changes fastest.
Arguments:
- key_branch: bfloat16 [8192, 4096], P('seq', 'chan'), may hold values from -6 to 6
- value_branch: bfloat16 [8192, 4096], P('seq', 'chan'), may hold values from -6 to 6
- query_branch: bfloat16 [8192, 4096], P('seq', 'chan'), may hold values from -6 to 6
- long_filter: bfloat16 [8192, 4096], P('seq', 'chan'), may hold values from -1.1 to 1.1
- skip_scale: float32 [4096], P('chan'), may hold values from -1 to 1
- out_weight: bfloat16 [4096, 4096], P('chan'), may hold values from -0.125 to 0.125
Outputs:
- operator_out: bfloat16 [8192, 4096], P('seq', 'chan')
- projected: bfloat16 [8192, 4096], P('seq', 'chan')
All inputs are finite; a program needn't handle non-finite values.
Results may differ from a plain program's by a relative error of at most 0.02.
Values may be sent and summed in bfloat16 or wider, within the bound.
No kernel may reach another device: no remote copies, remote signals or barrier semaphores. Data moves between devices by JAX's collectives and lax.ppermute only.
A program may use at most 64 MiB of HBM per device.

v0:
```python
import jax
import jax.numpy as jnp
from jax import lax
from jax.sharding import PartitionSpec as P

highest = lax.Precision.HIGHEST


def phases(numerator, denominator):
    return 2.0 * jnp.pi / denominator * (numerator % denominator).astype(jnp.float32)


def product(matrix, operand, pattern):
    return jnp.einsum(
        pattern, matrix, operand, precision=highest, preferred_element_type=jnp.float32
    )


def spectra(real_part, imag_part, freq_rows, row_count, length_all):
    offsets = jnp.arange(row_count, dtype=jnp.int32)
    twist = phases(freq_rows[:, None] * offsets[None, :], length_all)[:, :, None]
    cos_twist = jnp.cos(twist)
    sin_twist = jnp.sin(twist)
    shifted_re = real_part * cos_twist + imag_part * sin_twist
    shifted_im = imag_part * cos_twist - real_part * sin_twist
    lattice = phases(offsets[:, None] * offsets[None, :], row_count)
    cos_lattice = jnp.cos(lattice)
    sin_lattice = jnp.sin(lattice)
    spec_re = product(cos_lattice, shifted_re, "kr,aeri->aeki") + product(
        sin_lattice, shifted_im, "kr,aeri->aeki"
    )
    spec_im = product(cos_lattice, shifted_im, "kr,aeri->aeki") - product(
        sin_lattice, shifted_re, "kr,aeri->aeki"
    )
    prod_re = spec_re[0] * spec_re[1] - spec_im[0] * spec_im[1]
    prod_im = spec_re[0] * spec_im[1] + spec_im[0] * spec_re[1]
    back_re = product(cos_lattice, prod_re, "kr,eki->eri") - product(
        sin_lattice, prod_im, "kr,eki->eri"
    )
    back_im = product(cos_lattice, prod_im, "kr,eki->eri") + product(
        sin_lattice, prod_re, "kr,eki->eri"
    )
    out_re = back_re * cos_twist - back_im * sin_twist
    out_im = back_re * sin_twist + back_im * cos_twist
    return (out_re, out_im)


def shards(key_branch, value_branch, query_branch, long_filter, skip_scale, out_weight):
    seq_count = lax.axis_size("seq")
    seq_index = lax.axis_index("seq")
    row_count, chan_local = key_branch.shape
    block_rows = row_count // seq_count
    length_all = 2 * seq_count * row_count
    ordinal = jnp.arange(seq_count, dtype=jnp.int32)
    products = (key_branch.astype(jnp.float32) * value_branch.astype(jnp.float32)).astype(
        jnp.bfloat16
    )
    blocks = (
        products.reshape(seq_count, block_rows, chan_local),
        long_filter.reshape(seq_count, block_rows, chan_local),
    )
    stacked = jnp.stack(
        (
            lax.all_to_all(blocks[0], "seq", split_axis=0, concat_axis=0, tiled=True),
            lax.all_to_all(blocks[1], "seq", split_axis=0, concat_axis=0, tiled=True),
        )
    ).astype(jnp.float32)
    frequency = jnp.arange(2 * seq_count, dtype=jnp.int32)
    angles = phases(frequency[:, None] * ordinal[None, :], 2 * seq_count)
    part_re = product(jnp.cos(angles), stacked, "kd,adji->akji")
    part_im = -product(jnp.sin(angles), stacked, "kd,adji->akji")
    layout = (2, seq_count, 2, block_rows, stacked.shape[3])
    front_re = part_re.reshape(layout)
    front_im = part_im.reshape(layout)
    received = (
        lax.all_to_all(front_re, "seq", split_axis=1, concat_axis=3, tiled=True),
        lax.all_to_all(front_im, "seq", split_axis=1, concat_axis=3, tiled=True),
    )
    freq_rows = 2 * seq_index + jnp.arange(2, dtype=jnp.int32)
    middle_re, middle_im = spectra(
        received[0][:, 0], received[1][:, 0], freq_rows, row_count, length_all
    )
    classes = middle_re.shape[0]
    layout = (classes, seq_count, block_rows, chan_local)
    received = (
        lax.all_to_all(
            middle_re.reshape(layout).astype(jnp.bfloat16),
            "seq",
            split_axis=1,
            concat_axis=0,
            tiled=True,
        ).astype(jnp.float32),
        lax.all_to_all(
            middle_im.reshape(layout).astype(jnp.bfloat16),
            "seq",
            split_axis=1,
            concat_axis=0,
            tiled=True,
        ).astype(jnp.float32),
    )
    frequency = jnp.arange(2 * seq_count, dtype=jnp.int32)
    angles = phases(ordinal[:, None] * frequency[None, :], 2 * seq_count)
    summed = product(jnp.cos(angles), received[0][:, 0], "dk,kji->dji") - product(
        jnp.sin(angles), received[1][:, 0], "dk,kji->dji"
    )
    rear_out = summed / length_all
    convolved = lax.all_to_all(rear_out, "seq", split_axis=0, concat_axis=1, tiled=True).reshape(
        row_count, chan_local
    )
    direct = skip_scale[None, :] * products.astype(jnp.float32)
    operator_out = (query_branch.astype(jnp.float32) * (convolved + direct)).astype(jnp.bfloat16)
    partial_sums = jnp.dot(operator_out, out_weight, preferred_element_type=jnp.float32)
    projected = lax.psum_scatter(
        partial_sums.astype(jnp.bfloat16), "chan", scatter_dimension=1, tiled=True
    )
    return (operator_out, projected)


def solution(mesh):
    placed = (
        P("seq", "chan"),
        P("seq", "chan"),
        P("seq", "chan"),
        P("seq", "chan"),
        P("chan"),
        P("chan", None),
    )
    return jax.shard_map(
        shards,
        mesh=mesh,
        in_specs=placed,
        out_specs=(P("seq", "chan"), P("seq", "chan")),
        check_vma=False,
    )
```

profile of v0, /device:TPU:1, one launch (start us, length us, event | category | flops | bytes accessed | tf_op | source)
XLA Modules:
  0.0 234.0 jit_solution(5625377843351801142)
XLA Ops:
  7.2 1.0 multiply_convert_fusion.1
  8.2 0.7 reshape.146
  8.9 14.8 %all-to-all-start = ((bf16[64,2,512]{2,1,0:T(2,128)(2,1)}), bf16[64,2,512]{2,1,0:T(2,128)(2,1)S(1)}, u32[]{:S(2)}, u32[]{:S(2)}) async-start(bf16[64,2,512]{2,1,0:T(2,128)(2,1)} %reshape.146), calls=%async_computation | async-start | bytes 262144 | tf_op jit(solution)/shard_map/all_to_all | solution.py:64
  23.7 1.6 reshape.147
  25.3 9.5 %all-to-all-done = bf16[64,2,512]{2,1,0:T(2,128)(2,1)S(1)} async-done(((bf16[64,2,512]{2,1,0:T(2,128)(2,1)}), bf16[64,2,512]{2,1,0:T(2,128)(2,1)S(1)}, u32[]{:S(2)}, u32[]{:S(2)}) %all-to-all-start) | async-done | bytes 131104 | tf_op jit(solution)/shard_map/all_to_all | solution.py:64
  34.8 4.4 %all-to-all-start.1 = ((bf16[64,2,512]{2,1,0:T(2,128)(2,1)}), bf16[64,2,512]{2,1,0:T(2,128)(2,1)S(1)}, u32[]{:S(2)}, u32[]{:S(2)}) async-start(bf16[64,2,512]{2,1,0:T(2,128)(2,1)} %reshape.147), calls=%async_computation.1 | async-start | bytes 262144 | tf_op jit(solution)/shard_map/all_to_all | solution.py:65
  39.3 11.3 %all-to-all-done.1 = bf16[64,2,512]{2,1,0:T(2,128)(2,1)S(1)} async-done(((bf16[64,2,512]{2,1,0:T(2,128)(2,1)}), bf16[64,2,512]{2,1,0:T(2,128)(2,1)S(1)}, u32[]{:S(2)}, u32[]{:S(2)}) %all-to-all-start.1) | async-done | bytes 131104 | tf_op jit(solution)/shard_map/all_to_all | solution.py:65
  50.7 0.8 fusion.2
  51.5 0.6 reshape.149
  52.1 1.6 copy.46
  53.7 4.5 %all-to-all-start.3 = ((f32[2,64,2,2,512]{4,2,3,0,1:T(2,128)}), f32[2,64,2,2,512]{4,2,3,0,1:T(2,128)S(1)}, u32[]{:S(2)}, u32[]{:S(2)}) async-start(f32[2,64,2,2,512]{4,2,3,0,1:T(2,128)} %copy.46), calls=%async_computation.3 | async-start | bytes 2097152 | tf_op jit(solution)/shard_map/all_to_all | solution.py:77
  58.2 0.8 convolution_bitcast_fusion
  59.0 0.6 reshape.148
  59.6 1.6 copy.43
  61.3 25.1 %all-to-all-done.3 = f32[2,64,2,2,512]{4,2,3,0,1:T(2,128)S(1)} async-done(((f32[2,64,2,2,512]{4,2,3,0,1:T(2,128)}), f32[2,64,2,2,512]{4,2,3,0,1:T(2,128)S(1)}, u32[]{:S(2)}, u32[]{:S(2)}) %all-to-all-start.3) | async-done | bytes 1048608 | tf_op jit(solution)/shard_map/all_to_all | solution.py:77
  86.4 6.4 %all-to-all-start.2 = ((f32[2,64,2,2,512]{4,2,3,0,1:T(2,128)}), f32[2,64,2,2,512]{4,2,3,0,1:T(2,128)S(1)}, u32[]{:S(2)}, u32[]{:S(2)}) async-start(f32[2,64,2,2,512]{4,2,3,0,1:T(2,128)} %copy.43), calls=%async_computation.2 | async-start | bytes 2097152 | tf_op jit(solution)/shard_map/all_to_all | solution.py:76
  92.8 0.1 fusion.69
  92.9 0.1 copy.45
  93.0 0.1 copy.48
  93.2 0.4 copy.47
  93.5 27.2 %all-to-all-done.2 = f32[2,64,2,2,512]{4,2,3,0,1:T(2,128)S(1)} async-done(((f32[2,64,2,2,512]{4,2,3,0,1:T(2,128)}), f32[2,64,2,2,512]{4,2,3,0,1:T(2,128)S(1)}, u32[]{:S(2)}, u32[]{:S(2)}) %all-to-all-start.2) | async-done | bytes 1048608 | tf_op jit(solution)/shard_map/all_to_all | solution.py:76
  120.8 0.4 copy.44
  121.1 1.9 multiply_add_fusion
  123.0 0.5 copy.49
  123.6 1.5 copy.51
  125.0 1.2 fusion.24
  126.3 1.2 fusion.26
  127.5 1.2 fusion
  128.7 1.2 fusion.1
  129.9 0.1 multiply_subtract_fusion.1
  130.1 0.9 fusion.8
  130.9 0.9 fusion.4
  131.8 0.9 convolution_add_fusion.1
  132.8 1.0 fusion.11
  133.8 0.9 copy.61
  134.7 6.5 %all-to-all-start.4 = ((bf16[2,64,2,512]{3,2,0,1:T(2,128)(2,1)}), bf16[2,64,2,512]{3,2,0,1:T(2,128)(2,1)S(1)}, u32[]{:S(2)}, u32[]{:S(2)}) async-start(bf16[2,64,2,512]{3,2,0,1:T(2,128)(2,1)} %copy.61), calls=%async_computation.4 | async-start | bytes 524288 | tf_op jit(solution)/shard_map/all_to_all | solution.py:86
  141.2 0.1 convert_element_type.99
  141.3 0.9 copy.63
  142.2 12.2 %all-to-all-done.4 = bf16[2,64,2,512]{3,2,0,1:T(2,128)(2,1)S(1)} async-done(((bf16[2,64,2,512]{3,2,0,1:T(2,128)(2,1)}), bf16[2,64,2,512]{3,2,0,1:T(2,128)(2,1)S(1)}, u32[]{:S(2)}, u32[]{:S(2)}) %all-to-all-start.4) | async-done | bytes 262176 | tf_op jit(solution)/shard_map/all_to_all | solution.py:86
  154.3 4.9 %all-to-all-start.5 = ((bf16[2,64,2,512]{3,2,0,1:T(2,128)(2,1)}), bf16[2,64,2,512]{3,2,0,1:T(2,128)(2,1)S(1)}, u32[]{:S(2)}, u32[]{:S(2)}) async-start(bf16[2,64,2,512]{3,2,0,1:T(2,128)(2,1)} %copy.63), calls=%async_computation.5 | async-start | bytes 524288 | tf_op jit(solution)/shard_map/all_to_all | solution.py:93
  159.3 0.4 fusion.13
  159.7 12.7 %all-to-all-done.5 = bf16[2,64,2,512]{3,2,0,1:T(2,128)(2,1)S(1)} async-done(((bf16[2,64,2,512]{3,2,0,1:T(2,128)(2,1)}), bf16[2,64,2,512]{3,2,0,1:T(2,128)(2,1)S(1)}, u32[]{:S(2)}, u32[]{:S(2)}) %all-to-all-start.5) | async-done | bytes 262176 | tf_op jit(solution)/shard_map/all_to_all | solution.py:93
  172.4 0.4 fusion.3
  172.9 0.2 copy.65
  173.1 17.7 %all_to_all.79 = f32[64,2,512]{2,1,0:T(2,128)S(1)} all-to-all(f32[64,2,512]{2,1,0:T(2,128)S(1)} %copy.65), channel_id=1, replica_groups=mesh['seq'=64,'chan'=8] {'seq'}, dimensions={0} | all-to-all | bytes 524288 | tf_op jit(solution)/shard_map/all_to_all | solution.py:107
  190.7 0.2 reshape.150
  191.0 3.9 %convolution_convert_fusion = bf16[128,4096]{1,0:T(8,128)(2,1)} fusion(bf16[128,512]{1,0:T(8,128)(2,1)S(1)} %multiply_convert_fusion, bf16[512,4096]{1,0:T(8,128)(2,1)} %param.11), kind=kOutput, calls=%fused_computation | convolution fusion | flops 537395200 | bytes 5373952 | tf_op jit(solution)/shard_map/dot_general | solution.py:112
  195.0 32.2 %reduce-scatter.2.cloned.1.call-done = bf16[128,512]{1,0:T(8,128)(2,1)} async-done(((bf16[128,4096]{1,0:T(8,128)(2,1)}), bf16[128,512]{1,0:T(8,128)(2,1)}) %reduce-scatter.2.cloned.1.call-update) | async-done | bytes 131088 | tf_op jit(solution)/shard_map/reduce_scatter | solution.py:113
  (13 shorter events, 0.3 us)
Async XLA Ops:
  8.9 26.0 %all-to-all-start = ((bf16[64,2,512]{2,1,0:T(2,128)(2,1)}), bf16[64,2,512]{2,1,0:T(2,128)(2,1)S(1)}, u32[]{:S(2)}, u32[]{:S(2)}) async-start(bf16[64,2,512]{2,1,0:T(2,128)(2,1)} %reshape.146), calls=%async_computation | async-start | bytes 262144 | tf_op jit(solution)/shard_map/all_to_all | solution.py:64
  34.8 15.8 %all-to-all-start.1 = ((bf16[64,2,512]{2,1,0:T(2,128)(2,1)}), bf16[64,2,512]{2,1,0:T(2,128)(2,1)S(1)}, u32[]{:S(2)}, u32[]{:S(2)}) async-start(bf16[64,2,512]{2,1,0:T(2,128)(2,1)} %reshape.147), calls=%async_computation.1 | async-start | bytes 262144 | tf_op jit(solution)/shard_map/all_to_all | solution.py:65
  53.7 32.6 %all-to-all-start.3 = ((f32[2,64,2,2,512]{4,2,3,0,1:T(2,128)}), f32[2,64,2,2,512]{4,2,3,0,1:T(2,128)S(1)}, u32[]{:S(2)}, u32[]{:S(2)}) async-start(f32[2,64,2,2,512]{4,2,3,0,1:T(2,128)} %copy.46), calls=%async_computation.3 | async-start | bytes 2097152 | tf_op jit(solution)/shard_map/all_to_all | solution.py:77
  86.4 34.4 %all-to-all-start.2 = ((f32[2,64,2,2,512]{4,2,3,0,1:T(2,128)}), f32[2,64,2,2,512]{4,2,3,0,1:T(2,128)S(1)}, u32[]{:S(2)}, u32[]{:S(2)}) async-start(f32[2,64,2,2,512]{4,2,3,0,1:T(2,128)} %copy.43), calls=%async_computation.2 | async-start | bytes 2097152 | tf_op jit(solution)/shard_map/all_to_all | solution.py:76
  132.7 58.2 %copy-start.1 = (bf16[128,512]{1,0:T(8,128)(2,1)S(1)}, bf16[128,512]{1,0:T(8,128)(2,1)}, u32[]{:S(2)}) copy-start(bf16[128,512]{1,0:T(8,128)(2,1)} %param.8) | copy-start | bytes 393220
  132.7 58.2 %copy-start.2 = (f32[512]{0:T(512)S(1)}, f32[512]{0:T(512)}, u32[]{:S(2)}) copy-start(f32[512]{0:T(512)} %param.10) | copy-start | bytes 6148
  134.7 19.6 %all-to-all-start.4 = ((bf16[2,64,2,512]{3,2,0,1:T(2,128)(2,1)}), bf16[2,64,2,512]{3,2,0,1:T(2,128)(2,1)S(1)}, u32[]{:S(2)}, u32[]{:S(2)}) async-start(bf16[2,64,2,512]{3,2,0,1:T(2,128)(2,1)} %copy.61), calls=%async_computation.4 | async-start | bytes 524288 | tf_op jit(solution)/shard_map/all_to_all | solution.py:86
  154.3 18.1 %all-to-all-start.5 = ((bf16[2,64,2,512]{3,2,0,1:T(2,128)(2,1)}), bf16[2,64,2,512]{3,2,0,1:T(2,128)(2,1)S(1)}, u32[]{:S(2)}, u32[]{:S(2)}) async-start(bf16[2,64,2,512]{3,2,0,1:T(2,128)(2,1)} %copy.63), calls=%async_computation.5 | async-start | bytes 524288 | tf_op jit(solution)/shard_map/all_to_all | solution.py:93
  159.3 67.9 %reduce-scatter.2.cloned.1.call-start = ((), (), s32[]{:S(2)}) async-start(), calls=%async_computation.8 | async-start | bytes 1179648 | tf_op jit(solution)/shard_map/reduce_scatter | solution.py:113
  191.0 36.1 %copy-start = (bf16[128,512]{1,0:T(8,128)(2,1)}, bf16[128,512]{1,0:T(8,128)(2,1)S(1)}, u32[]{:S(2)}) copy-start(bf16[128,512]{1,0:T(8,128)(2,1)S(1)} %multiply_convert_fusion) | copy-start | bytes 393220
Sparse Core Ops, SparseCore 0:
  195.1 31.9 reduce-scatter.1
where the time goes:
time: 238 us; the launch traced here: 234 us
  waiting for transfers between devices  130 us (55%)
  starting transfers between devices  41.6 us (17%)
  blocking collectives  17.7 us (7%)
  matrix products  14.8 us (6%)
  between operations  14.3 us (6%)
  local copies, waits for them, and re-layouts  12.2 us (5%)
  other arithmetic  3.2 us (1%)
    reduce_scatter x1, waiting for transfers between devices, shards(): lax.psum_scatter(partial_sums.astype(jnp.bfloat16), 'chan', scatter_dimen...  32.2 us
    all_to_all x1, waiting for transfers between devices, shards(): lax.all_to_all(front_re, 'seq', split_axis=1, concat_axis=3, tiled=True)  27.2 us
    all_to_all x1, waiting for transfers between devices, shards(): lax.all_to_all(front_im, 'seq', split_axis=1, concat_axis=3, tiled=True)  25.1 us
    all_to_all x1, blocking collectives, shards(): lax.all_to_all(rear_out, 'seq', split_axis=0, concat_axis=1, tiled=True)  17.7 us
    all_to_all x1, starting transfers between devices, shards(): lax.all_to_all(blocks[0], 'seq', split_axis=0, concat_axis=0, tiled=True)  14.8 us
    all_to_all x1, waiting for transfers between devices, shards(): lax.all_to_all(middle_im.reshape(layout).astype(jnp.bfloat16), 'seq', spl...  12.7 us
    all_to_all x1, waiting for transfers between devices, shards(): lax.all_to_all(middle_re.reshape(layout).astype(jnp.bfloat16), 'seq', spl...  12.2 us
    all_to_all x1, waiting for transfers between devices, shards(): lax.all_to_all(blocks[1], 'seq', split_axis=0, concat_axis=0, tiled=True)  11.3 us
  transfers between devices with their start and end apart: 7, of which 7 were waited for; matrix products, arithmetic and copies ran while one was open for 3% of the time, Pallas kernels for 0%

commit v1 on v0

v1 whole, which is shorter than its diff:
```python
import functools

import jax
import jax.numpy as jnp
import numpy as np
from jax import lax
from jax.experimental import pallas as pl
from jax.experimental.pallas import tpu as pltpu
from jax.sharding import PartitionSpec as P

f32 = jnp.float32
bf16 = jnp.bfloat16


def split(values, parts):
    pieces = []
    rest = np.asarray(values, np.float64)
    for _ in range(parts):
        piece = rest.astype(bf16)
        pieces.append(piece)
        rest = rest - piece.astype(np.float64)
    return pieces


def transform_tables(outer, inner):
    length = outer * inner
    row = np.arange(outer, dtype=np.float64)
    lane = np.arange(inner, dtype=np.float64)
    angle = 2.0 * np.pi * np.outer(row + 0.25, row) / outer
    first = np.concatenate([np.cos(angle), -np.sin(angle)], axis=0)
    twist = 2.0 * np.pi * np.outer(row + 0.25, lane) / length
    angle = 2.0 * np.pi * np.outer(lane, lane) / inner
    cos, sin = np.cos(angle), np.sin(angle)
    second = np.block([[cos, -sin], [sin, cos]])
    angle = 2.0 * np.pi * np.outer(row, row + 0.25) / outer
    last = np.concatenate([np.cos(angle), -np.sin(angle)], axis=1) / length
    first_parts = np.concatenate(split(first, 3), axis=1)
    second_parts = split(second, 2)
    back_parts = split(second.T, 2)
    last_high, last_low = split(last, 2)
    last_parts = np.concatenate([last_high, last_low, last_high], axis=1)
    return (
        first_parts,
        np.cos(twist).astype(np.float32),
        np.sin(twist).astype(np.float32),
        second_parts[0],
        second_parts[1],
        back_parts[0],
        back_parts[1],
        last_parts,
    )


def dot(a, b):
    return jnp.dot(a, b, preferred_element_type=f32)


def halves(values):
    high = values.astype(bf16)
    return high, (values - high.astype(f32)).astype(bf16)


def pack_kernel(shares, key_ref, value_ref, filter_ref, query_ref, out_ref):
    rows, chans = key_ref.shape
    group = chans // shares
    products = (key_ref[...].astype(f32) * value_ref[...].astype(f32)).astype(bf16).astype(f32)
    pieces = (products, filter_ref[...].astype(f32), query_ref[...].astype(f32))
    turned = [piece.T.reshape(shares, group, rows) for piece in pieces]
    out_ref[...] = jnp.concatenate(turned, axis=1).reshape(out_ref.shape).astype(bf16)


def convolve_kernel(
    group,
    outer,
    skip_ref,
    packed_ref,
    first_ref,
    cos_ref,
    sin_ref,
    second_high,
    second_low,
    back_high,
    back_low,
    last_ref,
    out_ref,
    wide,
    gated,
):
    inner = packed_ref.shape[1]
    signals = 2 * group
    step = 3 * group
    wide[...] = packed_ref[...].astype(f32)
    cos, sin = cos_ref[...], sin_ref[...]
    taken = [wide[pl.ds(i, outer, stride=step), :] for i in range(signals)]
    stacked = jnp.concatenate([t.astype(bf16) for t in taken], axis=1)
    front = dot(first_ref[...], jnp.concatenate([stacked] * 3, axis=0))
    rows = []
    for i in range(signals):
        re = front[:outer, i * inner : (i + 1) * inner]
        im = front[outer:, i * inner : (i + 1) * inner]
        rows.append(jnp.concatenate([re * cos + im * sin, im * cos - re * sin], axis=1))
    high, low = halves(jnp.concatenate(rows, axis=0))
    spec = dot(high, second_high[...]) + dot(low, second_high[...]) + dot(high, second_low[...])
    half = group * outer
    a_re, a_im = spec[:half, :inner], spec[:half, inner:]
    b_re, b_im = spec[half:, :inner], spec[half:, inner:]
    prod = jnp.concatenate([a_re * b_re - a_im * b_im, a_re * b_im + a_im * b_re], axis=1)
    high, low = halves(prod)
    back = dot(high, back_high[...]) + dot(low, back_high[...]) + dot(high, back_low[...])
    columns = []
    for i in range(group):
        re = back[i * outer : (i + 1) * outer, :inner]
        im = back[i * outer : (i + 1) * outer, inner:]
        columns.append(jnp.concatenate([re * cos - im * sin, re * sin + im * cos], axis=0))
    high, low = halves(jnp.concatenate(columns, axis=1))
    result = dot(last_ref[...], jnp.concatenate([high, high, low], axis=0))
    for i in range(group):
        conv = result[:, i * inner : (i + 1) * inner]
        query = wide[pl.ds(signals + i, outer, stride=step), :]
        gated[pl.ds(i, outer, stride=group), :] = query * (conv + skip_ref[i] * taken[i])
    out_ref[...] = gated[...].astype(bf16)


def project_kernel(turned_ref, weight_ref, out_ref, partial_ref):
    @pl.when(pl.program_id(0) == 0)
    def _():
        out_ref[...] = turned_ref[...].astype(f32).T.astype(bf16)

    partial_ref[0] = dot(out_ref[...], weight_ref[...]).astype(bf16)


VMEM = pl.BlockSpec(memory_space=pltpu.VMEM)
SMEM = pl.BlockSpec(memory_space=pltpu.SMEM)
params = pltpu.CompilerParams(vmem_limit_bytes=48 * 1024 * 1024)


def shards(key_branch, value_branch, query_branch, long_filter, skip_scale, out_weight):
    seq_count = lax.axis_size("seq")
    chan_count = lax.axis_size("chan")
    seq_index = lax.axis_index("seq")
    rows, chans = key_branch.shape
    group = chans // seq_count
    tables = transform_tables(seq_count, rows)
    packed = pl.pallas_call(
        functools.partial(pack_kernel, seq_count),
        out_shape=jax.ShapeDtypeStruct((3 * chans, rows), bf16),
        in_specs=[VMEM] * 4,
        out_specs=VMEM,
        compiler_params=params,
        name="pack",
    )(key_branch, value_branch, long_filter, query_branch)
    packed = lax.all_to_all(
        packed.reshape(seq_count, 3 * group, rows), "seq", split_axis=0, concat_axis=0, tiled=True
    ).reshape(3 * chans, rows)
    skip = lax.dynamic_slice(skip_scale, (seq_index * group,), (group,))
    turned = pl.pallas_call(
        functools.partial(convolve_kernel, group, seq_count),
        out_shape=jax.ShapeDtypeStruct((chans, rows), bf16),
        in_specs=[SMEM] + [VMEM] * (1 + len(tables)),
        out_specs=VMEM,
        scratch_shapes=[pltpu.VMEM((3 * chans, rows), f32), pltpu.VMEM((chans, rows), f32)],
        compiler_params=params,
        name="convolve",
    )(skip, packed, *[jnp.asarray(t) for t in tables])
    turned = lax.all_to_all(
        turned.reshape(seq_count, group, rows), "seq", split_axis=0, concat_axis=0, tiled=True
    ).reshape(chans, rows)
    width = out_weight.shape[1] // chan_count
    operator_out, partial = pl.pallas_call(
        project_kernel,
        grid=(chan_count,),
        out_shape=(
            jax.ShapeDtypeStruct((rows, chans), bf16),
            jax.ShapeDtypeStruct((chan_count, rows, width), bf16),
        ),
        in_specs=[
            pl.BlockSpec((chans, rows), lambda i: (0, 0)),
            pl.BlockSpec((chans, width), lambda i: (0, i)),
        ],
        out_specs=(
            pl.BlockSpec((rows, chans), lambda i: (0, 0)),
            pl.BlockSpec((1, rows, width), lambda i: (i, 0, 0)),
        ),
        compiler_params=params,
        name="project",
    )(turned, out_weight)
    partial = lax.all_to_all(partial, "chan", split_axis=0, concat_axis=0, tiled=True)
    projected = jnp.sum(partial.astype(f32), axis=0).astype(bf16)
    return (operator_out, projected)


def solution(mesh):
    placed = (
        P("seq", "chan"),
        P("seq", "chan"),
        P("seq", "chan"),
        P("seq", "chan"),
        P("chan"),
        P("chan", None),
    )
    return jax.shard_map(
        shards,
        mesh=mesh,
        in_specs=placed,
        out_specs=(P("seq", "chan"), P("seq", "chan")),
        check_vma=False,
    )
```

time: 238 us -> 102 us (0.43); the launches traced: 234 us -> 101 us
  waiting for transfers between devices: 130 us -> 14.3 us
  blocking collectives: 17.7 us -> 50.9 us
  starting transfers between devices: 41.6 us -> 14.8 us
  matrix products: 14.8 us -> 0 us
  between operations: 14.3 us -> 0.67 us
  Pallas kernels: 0 us -> 5.98 us
  other arithmetic: 3.2 us -> 0.81 us
    all_to_all x6 -> x1, waiting for transfers between devices: 98 us -> 14.3 us  [shards(): lax.all_to_all(packed.reshape(seq_count, 3 * group, rows), 'seq', split_a...]
    all_to_all x1 -> x2, blocking collectives: 17.7 us -> 50.9 us  [the longest x1 34.4 us: shards(): lax.all_to_all(partial, 'chan', split_axis=0, concat_axis=0, tiled=True)]
    reduce_scatter x1 -> x0, waiting for transfers between devices: 32.2 us -> none  [shards(): lax.psum_scatter(partial_sums.astype(jnp.bfloat16), 'chan', scatter_dimen...]
    all_to_all x6 -> x1, starting transfers between devices: 41.6 us -> 14.8 us  [shards(): lax.all_to_all(packed.reshape(seq_count, 3 * group, rows), 'seq', split_a...]
    dot_general x13 -> x0, matrix products: 14.8 us -> none  [the longest x12 10.9 us: product(): jnp.einsum(pattern, matrix, operand, precision=highest, preferred_element...]
    unnamed x6 -> x26, local copies, waits for them, and re-layouts: 0.02 us -> 12.6 us
    reshape x7 -> x0, local copies, waits for them, and re-layouts: 7.01 us -> none  [the longest x2 2.25 us: shards(): front_re = part_re.reshape(layout)]
    pallas_call x0 -> x3, Pallas kernels: none -> 5.98 us  [the longest x1 2.8 us: shards(): pl.pallas_call(project_kernel, grid=(chan_count,), out_shape=(jax.ShapeDt...]
  transfers between devices with their start and end apart: 7 -> 1, of which waited for: 7 -> 1; matrix products, arithmetic and copies ran while one was open for 3% -> 1% of each run, Pallas kernels for 0% -> 0%
where the time goes in v1:
time: 102 us; the launch traced here: 101 us
  blocking collectives  50.9 us (50%)
  starting transfers between devices  14.8 us (15%)
  waiting for transfers between devices  14.3 us (14%)
  local copies, waits for them, and re-layouts  13.3 us (13%)
  Pallas kernels  5.98 us (6%)
    all_to_all x1, blocking collectives, shards(): lax.all_to_all(partial, 'chan', split_axis=0, concat_axis=0, tiled=True)  34.4 us
    all_to_all x1, blocking collectives, shards(): lax.all_to_all(turned.reshape(seq_count, group, rows), 'seq', split_axis=...  16.5 us
    all_to_all x1, starting transfers between devices, shards(): lax.all_to_all(packed.reshape(seq_count, 3 * group, rows), 'seq', split_a...  14.8 us
    all_to_all x1, waiting for transfers between devices, shards(): lax.all_to_all(packed.reshape(seq_count, 3 * group, rows), 'seq', split_a...  14.3 us
    unnamed x26, local copies, waits for them, and re-layouts  12.6 us
    pallas_call x1, Pallas kernels, shards(): pl.pallas_call(project_kernel, grid=(chan_count,), out_shape=(jax.ShapeDt...  2.8 us
    pallas_call x1, Pallas kernels, shards(): pl.pallas_call(functools.partial(convolve_kernel, group, seq_count), out_...  2.26 us
  transfers between devices with their start and end apart: 1, of which 1 were waited for; matrix products, arithmetic and copies ran while one was open for 1% of the time, Pallas kernels for 0%

profile of v1, /device:TPU:1, one launch (start us, length us, event | category | flops | bytes accessed | tf_op | source)
XLA Modules:
  0.0 100.8 jit_solution(9330706705561885211)
XLA Ops:
  0.6 0.0 copy-start.1
  0.6 0.9 copy-done.1
  1.5 0.0 copy-start.2
  1.5 0.9 copy-done.2
  2.4 0.0 copy-start.3
  2.4 0.9 copy-done.3
  3.3 0.0 copy-start.4
  3.3 0.9 copy-done.4
  4.2 0.9 pack.1
  5.2 14.8 %all-to-all-start = ((bf16[64,24,128]{2,1,0:T(8,128)(2,1)}), bf16[64,24,128]{2,1,0:T(8,128)(2,1)S(1)}, u32[]{:S(2)}, u32[]{:S(2)}) async-start(bf16[64,24,128]{2,1,0:T(8,128)(2,1)} %bitcast), calls=%async_computation | async-start | bytes 786432 | tf_op jit(solution)/shard_map/all_to_all | solution.py:152
  20.0 0.8 dynamic_slice.3.skip_ref
  20.8 14.3 %all-to-all-done = bf16[64,24,128]{2,1,0:T(8,128)(2,1)S(1)} async-done(((bf16[64,24,128]{2,1,0:T(8,128)(2,1)}), bf16[64,24,128]{2,1,0:T(8,128)(2,1)S(1)}, u32[]{:S(2)}, u32[]{:S(2)}) %all-to-all-start) | async-done | bytes 393248 | tf_op jit(solution)/shard_map/all_to_all | solution.py:152
  35.1 0.0 copy-start.5
  35.1 0.9 copy-done.5
  36.0 0.0 copy-start.6
  36.0 0.9 copy-done.6
  36.9 0.0 copy-start.7
  36.9 0.9 copy-done.7
  37.8 0.0 copy-start.8
  37.8 0.9 copy-done.8
  38.7 0.0 copy-start.9
  38.7 0.8 copy-done.9
  39.5 0.0 copy-start.10
  39.5 0.8 copy-done.10
  40.3 0.0 copy-start.11
  40.3 0.8 copy-done.11
  41.1 0.0 copy-start.12
  41.1 0.8 copy-done.12
  41.8 2.3 %convolve.1 = bf16[512,128]{1,0:T(8,128)(2,1)S(1)} custom-call(f32[8]{0:T(128)S(1)} %dynamic_slice.3.skip_ref, bf16[1536,128]{1,0:T(8,128)(2,1)S(1)} %bitcast.4, bf16[128,192]{1,0:T(8,128)(2,1)S(1)} %copy-done.9, f32[64,128]{1,0:T(8,128)S(1)} %copy-done.12, f32[64,128]{1,0:T(8,128)S(1)} %copy-done.11, bf16[256,256]{1,0:T(8,128)(2,1)S(1)} %copy-done.8, ...), custom_call_target="tpu_custom_call" | custom-call | tf_op jit(solution)/shard_map/convolve/pallas_call | solution.py:156
  44.1 16.5 %all_to_all.15 = bf16[64,8,128]{2,1,0:T(8,128)(2,1)S(1)} all-to-all(bf16[64,8,128]{2,1,0:T(8,128)(2,1)S(1)} %bitcast.5), channel_id=1, replica_groups=mesh['seq'=64,'chan'=8] {'seq'}, dimensions={0} | all-to-all | bytes 262144 | tf_op jit(solution)/shard_map/all_to_all | solution.py:165
  60.6 0.0 copy-start
  60.6 2.2 %copy-done = bf16[512,4096]{1,0:T(8,128)(2,1)S(1)} copy-done((bf16[512,4096]{1,0:T(8,128)(2,1)S(1)}, bf16[512,4096]{1,0:T(8,128)(2,1)}, u32[]{:S(2)}) %copy-start) | copy-done | bytes 4194328
  62.8 2.8 %project.1 = (bf16[128,512]{1,0:T(8,128)(2,1)}, bf16[8,128,512]{2,1,0:T(8,128)(2,1)S(1)}) custom-call(bf16[512,128]{1,0:T(8,128)(2,1)S(1)} %bitcast.6, bf16[512,4096]{1,0:T(8,128)(2,1)S(1)} %copy-done), custom_call_target="tpu_custom_call" | custom-call | tf_op jit(solution)/shard_map/project/pallas_call | solution.py:169
  65.6 34.4 %all_to_all.16 = bf16[8,128,512]{2,1,0:T(8,128)(2,1)S(1)} all-to-all(bf16[8,128,512]{2,1,0:T(8,128)(2,1)S(1)} %get-tuple-element.5), channel_id=1, replica_groups=mesh['seq'=64,'chan'=8] {'chan'}, dimensions={0} | all-to-all | bytes 2097152 | tf_op jit(solution)/shard_map/all_to_all | solution.py:187
  100.0 0.8 reduce_sum.12
Async XLA Ops:
  0.6 0.9 copy-start.1
  1.5 0.9 copy-start.2
  2.4 0.9 copy-start.3
  3.3 0.9 copy-start.4
  5.2 29.9 %all-to-all-start = ((bf16[64,24,128]{2,1,0:T(8,128)(2,1)}), bf16[64,24,128]{2,1,0:T(8,128)(2,1)S(1)}, u32[]{:S(2)}, u32[]{:S(2)}) async-start(bf16[64,24,128]{2,1,0:T(8,128)(2,1)} %bitcast), calls=%async_computation | async-start | bytes 786432 | tf_op jit(solution)/shard_map/all_to_all | solution.py:152
  35.1 0.9 copy-start.5
  36.0 0.9 copy-start.6
  36.9 0.9 copy-start.7
  37.8 0.9 copy-start.8
  38.7 0.8 copy-start.9
  39.5 0.8 copy-start.10
  40.3 0.8 copy-start.11
  41.1 0.8 copy-start.12
  60.6 2.2 %copy-start = (bf16[512,4096]{1,0:T(8,128)(2,1)S(1)}, bf16[512,4096]{1,0:T(8,128)(2,1)}, u32[]{:S(2)}) copy-start(bf16[512,4096]{1,0:T(8,128)(2,1)} %weight_ref.1) | copy-start | bytes 12582916

commit v2 on v1

v2 whole, which is shorter than its diff:
```python
import functools

import jax
import jax.numpy as jnp
import numpy as np
from jax import lax
from jax.experimental import pallas as pl
from jax.experimental.pallas import tpu as pltpu
from jax.sharding import Mesh
from jax.sharding import PartitionSpec as P

f32 = jnp.float32
bf16 = jnp.bfloat16


def split(values, parts):
    pieces = []
    rest = np.asarray(values, np.float64)
    for _ in range(parts):
        piece = rest.astype(bf16)
        pieces.append(piece)
        rest = rest - piece.astype(np.float64)
    return pieces


def transform_tables(outer, inner):
    length = outer * inner
    row = np.arange(outer, dtype=np.float64)
    lane = np.arange(inner, dtype=np.float64)
    angle = 2.0 * np.pi * np.outer(row + 0.25, row) / outer
    first = np.concatenate([np.cos(angle), -np.sin(angle)], axis=0)
    twist = 2.0 * np.pi * np.outer(row + 0.25, lane) / length
    angle = 2.0 * np.pi * np.outer(lane, lane) / inner
    cos, sin = np.cos(angle), np.sin(angle)
    second = np.block([[cos, -sin], [sin, cos]])
    angle = 2.0 * np.pi * np.outer(row, row + 0.25) / outer
    last = np.concatenate([np.cos(angle), -np.sin(angle)], axis=1) / length
    first_parts = np.concatenate(split(first, 3), axis=1)
    second_parts = split(second, 2)
    back_parts = split(second.T, 2)
    last_high, last_low = split(last, 2)
    last_parts = np.concatenate([last_high, last_low, last_high], axis=1)
    return (
        first_parts,
        np.cos(twist).astype(np.float32),
        np.sin(twist).astype(np.float32),
        second_parts[0],
        second_parts[1],
        back_parts[0],
        back_parts[1],
        last_parts,
    )


def dot(a, b):
    return jnp.dot(a, b, preferred_element_type=f32)


def halves(values):
    high = values.astype(bf16)
    return high, (values - high.astype(f32)).astype(bf16)


PAIR = 2


def served(plane, step, planes):
    return lax.rem(plane + planes + step * (PAIR * lax.rem(plane, PAIR) - 1), planes)


def place():
    plane = PAIR * lax.axis_index("quad") + lax.axis_index("side")
    return plane, plane + 1 - PAIR * lax.axis_index("side")


def columns_of(plane, width):
    return pl.ds(pl.multiple_of(plane * width, width), width)


def fetch(pairs, sems):
    copies = [pltpu.make_async_copy(src, dst, sems.at[i]) for i, (src, dst) in enumerate(pairs)]
    for copy in copies:
        copy.start()
    return copies


def wait_all(copies):
    for copy in copies:
        copy.wait()


def pack_kernel(shares, key_ref, value_ref, filter_ref, out_ref, held, sems):
    rows, chans = key_ref.shape
    group = chans // shares
    wait_all(fetch([(ref, held.at[i]) for i, ref in enumerate((key_ref, value_ref, filter_ref))], sems))
    products = (held[0].astype(f32) * held[1].astype(f32)).astype(bf16).astype(f32)
    turned = [piece.T.reshape(shares, group, rows) for piece in (products, held[2].astype(f32))]
    out_ref[...] = jnp.concatenate(turned, axis=1).reshape(out_ref.shape).astype(bf16)


def convolve_kernel(
    group,
    outer,
    skip,
    packed,
    first_ref,
    cos_ref,
    sin_ref,
    second_high,
    second_low,
    back_high,
    back_low,
    last_ref,
    out_ref,
    wide,
    turned,
):
    inner = packed.shape[1]
    signals = 2 * group
    step = 2 * group
    wide[...] = packed[...].astype(f32)
    cos, sin = cos_ref[...], sin_ref[...]
    taken = [wide[pl.ds(i, outer, stride=step), :] for i in range(signals)]
    stacked = jnp.concatenate([t.astype(bf16) for t in taken], axis=1)
    front = dot(first_ref[...], jnp.concatenate([stacked] * 3, axis=0))
    rows = []
    for i in range(signals):
        re = front[:outer, i * inner : (i + 1) * inner]
        im = front[outer:, i * inner : (i + 1) * inner]
        rows.append(jnp.concatenate([re * cos + im * sin, im * cos - re * sin], axis=1))
    high, low = halves(jnp.concatenate(rows, axis=0))
    spec = dot(high, second_high[...]) + dot(low, second_high[...]) + dot(high, second_low[...])
    half = group * outer
    a_re, a_im = spec[:half, :inner], spec[:half, inner:]
    b_re, b_im = spec[half:, :inner], spec[half:, inner:]
    prod = jnp.concatenate([a_re * b_re - a_im * b_im, a_re * b_im + a_im * b_re], axis=1)
    high, low = halves(prod)
    back = dot(high, back_high[...]) + dot(low, back_high[...]) + dot(high, back_low[...])
    columns = []
    for i in range(group):
        re = back[i * outer : (i + 1) * outer, :inner]
        im = back[i * outer : (i + 1) * outer, inner:]
        columns.append(jnp.concatenate([re * cos - im * sin, re * sin + im * cos], axis=0))
    high, low = halves(jnp.concatenate(columns, axis=1))
    result = dot(last_ref[...], jnp.concatenate([high, high, low], axis=0))
    base = (lax.axis_index("zx") * 2 + lax.axis_index("core")) * group
    for i in range(group):
        summed = result[:, i * inner : (i + 1) * inner] + skip[base + i] * taken[i]
        turned[pl.ds(i, outer, stride=group), :] = summed
    out = turned[...].astype(bf16)
    for i in range(PAIR):
        out_ref[i] = out


def ship_kernel(steps, planes, query_ref, weight_ref, packed_ref, *rest):
    del packed_ref
    *out_refs, sems = rest
    partner = place()[1]
    count, width = out_refs[0].shape
    rows = pl.ds(pl.multiple_of(lax.axis_index("core") * count, count), count)
    pairs = [(query_ref, out_refs[-1].at[pl.ds(count, query_ref.shape[0])])]
    for step, out_ref in zip(steps, out_refs, strict=True):
        columns = columns_of(served(partner, step, planes), width)
        pairs.append((weight_ref.at[rows, columns], out_ref.at[pl.ds(0, count)]))
    wait_all(fetch(pairs, sems))


def hold_kernel(*refs):
    del refs


def stage_kernel(query_ref, *rest):
    *piece_refs, weight_ref, queries_ref, sems = rest
    count = len(piece_refs) // 2
    near_refs, far_refs = piece_refs[:count], piece_refs[count:]
    core = lax.axis_index("core")
    half = weight_ref.shape[1] // 2
    near = pl.ds(pl.multiple_of(core * half, half), half)
    far = pl.ds(pl.multiple_of((1 - core) * half, half), half)
    rows = pl.ds(half, query_ref.shape[0])
    pairs = [(query_ref, queries_ref.at[0]), (near_refs[-1].at[rows], queries_ref.at[1])]
    for i in range(count):
        pairs.append((near_refs[i].at[pl.ds(0, half)], weight_ref.at[i, near]))
        pairs.append((far_refs[i].at[pl.ds(0, half)], weight_ref.at[i, far]))
    wait_all(fetch(pairs, sems))


def gate_kernel(steps, planes, turned_ref, queries_ref, other_weight, weight_ref, own_ref, *rest):
    *partial_refs, partner_ref, held, sems = rest
    plane, partner = place()
    width = held.shape[2]
    targets = [served(plane, step, planes) for step in steps] + [partner]
    copies = fetch([(weight_ref.at[:, columns_of(t, width)], held.at[i]) for i, t in enumerate(targets)], sems)
    side = lax.axis_index("side")
    other = (queries_ref[1].astype(f32) * turned_ref[1 - side].astype(f32).T).astype(bf16)
    own = (queries_ref[0].astype(f32) * turned_ref[side].astype(f32).T).astype(bf16)
    own_ref[...] = own
    across = [dot(other, other_weight[i]) for i in range(len(steps))]
    for i, partial_ref in enumerate(partial_refs):
        copies[i].wait()
        partial_ref[...] = (dot(own, held[i]) + across[i]).astype(bf16)
    copies[-1].wait()
    partner_ref[...] = dot(own, held[len(steps)]).astype(bf16)


def keep_kernel(own_ref, weight_ref, out_ref, kept_ref, held, sems):
    copies = fetch([(weight_ref.at[:, columns_of(place()[0], held.shape[1])], held)], sems)
    own = own_ref[...]
    out_ref[...] = own
    wait_all(copies)
    kept_ref[...] = dot(own, held[...])


def sum_kernel(*refs):
    *parts, out_ref = refs
    total = parts[0][...]
    for part in parts[1:]:
        total = total + part[...].astype(f32)
    out_ref[...] = total.astype(out_ref.dtype)


ANY = pl.BlockSpec(memory_space=pl.ANY)
VMEM = pl.BlockSpec(memory_space=pltpu.VMEM)
SMEM = pl.BlockSpec(memory_space=pltpu.SMEM)
params = pltpu.CompilerParams(vmem_limit_bytes=32 * 1024 * 1024)
dma = pltpu.SemaphoreType.DMA


def call(kernel, name, out_shape, in_specs, scratch=(), **options):
    options.setdefault("out_specs", [VMEM] * len(out_shape))
    return pl.pallas_call(
        kernel,
        out_shape=out_shape,
        in_specs=in_specs,
        scratch_shapes=list(scratch),
        compiler_params=params,
        name=name,
        **options,
    )


def in_vmem(*arrays):
    return [pltpu.with_memory_space_constraint(x, pltpu.VMEM) for x in arrays]


def permuted_after(arrays, after, axis, pairs):
    count = len(arrays)
    arrays = call(
        hold_kernel,
        "hold",
        [jax.ShapeDtypeStruct(x.shape, x.dtype) for x in arrays],
        [ANY] * (count + 1),
        out_specs=[ANY] * count,
        input_output_aliases={i: i for i in range(count)},
    )(*arrays, after)
    return arrays, [lax.ppermute(x, axis, pairs) for x in arrays]


def shards(key_branch, value_branch, query_branch, long_filter, skip_scale, out_weight):
    seq, chan = ("zx", "core"), ("quad", "side")
    seq_count = lax.axis_size("zx") * lax.axis_size("core")
    planes = PAIR * lax.axis_size("quad")
    steps = tuple(range(planes // PAIR - 1, 0, -1))
    rows, chans = key_branch.shape
    group = chans // seq_count
    width = out_weight.shape[1] // planes
    tables = transform_tables(seq_count, rows)
    key_branch, value_branch, query_branch, long_filter, out_weight = [
        pltpu.with_memory_space_constraint(x, pltpu.HBM)
        for x in (key_branch, value_branch, query_branch, long_filter, out_weight)
    ]
    (packed,) = call(
        functools.partial(pack_kernel, seq_count),
        "pack",
        [pltpu.VMEM((2 * chans, rows), bf16)],
        [ANY] * 3,
        [pltpu.VMEM((3, rows, chans), bf16), dma((3,))],
    )(key_branch, value_branch, long_filter)
    arrived = lax.all_to_all(
        packed.reshape(seq_count, 2 * group, rows), seq, split_axis=0, concat_axis=0, tiled=True
    ).reshape(2 * chans, rows)
    swap = [(0, 1), (1, 0)]
    half = chans // 2
    piece_rows = [half] * (len(steps) - 1) + [half + rows]
    near = call(
        functools.partial(ship_kernel, steps, planes),
        "ship",
        [pltpu.VMEM((count, width), bf16) for count in piece_rows],
        [ANY] * 3,
        [dma((1 + len(steps),))],
    )(query_branch, out_weight, packed)
    near = [lax.ppermute(x, "side", swap) for x in near]
    (turned,) = call(
        functools.partial(convolve_kernel, group, seq_count),
        "convolve",
        [pltpu.VMEM((PAIR, chans, rows), bf16)],
        [SMEM] + [VMEM] * (1 + len(tables)),
        [pltpu.VMEM((2 * chans, rows), f32), pltpu.VMEM((chans, rows), f32)],
    )(skip_scale, arrived, *[jnp.asarray(t) for t in tables])
    near, far = permuted_after(near, turned, "core", swap)
    staged = call(
        stage_kernel,
        "stage",
        [pltpu.VMEM((len(steps), chans, width), bf16), pltpu.VMEM((PAIR, rows, chans), bf16)],
        [ANY] * (1 + 2 * len(steps)),
        [dma((2 * len(steps) + 2,))],
    )(query_branch, *near, *far)
    other_weight, queries = in_vmem(*staged)
    turned = lax.all_to_all(
        turned.reshape(PAIR * seq_count, group, rows), ("side",) + seq, split_axis=0, concat_axis=0, tiled=True
    ).reshape(PAIR, chans, rows)
    block = pltpu.VMEM((rows, width), bf16)
    own, *sent, partner = call(
        functools.partial(gate_kernel, steps, planes),
        "gate",
        [pltpu.VMEM((rows, chans), bf16)] + [block] * (len(steps) + 1),
        [VMEM] * 3 + [ANY],
        [pltpu.VMEM((len(steps) + 1, chans, width), bf16), dma((len(steps) + 1,))],
    )(turned, queries, other_weight, out_weight)
    operator_out, kept = call(
        keep_kernel,
        "keep",
        [jax.ShapeDtypeStruct((rows, chans), bf16), pltpu.VMEM((rows, width), f32)],
        [VMEM, ANY],
        [pltpu.VMEM((chans, width), bf16), dma((1,))],
    )(own, out_weight)
    parts = [kept]
    for part, step in zip(sent, steps, strict=True):
        pairs = [(i, (i + (step if i % PAIR else planes - step)) % planes) for i in range(planes)]
        parts.append(lax.ppermute(part, chan, pairs))
    parts.append(lax.ppermute(partner, "side", swap))
    (projected,) = call(sum_kernel, "sum", [jax.ShapeDtypeStruct((rows, width), bf16)], [VMEM] * len(parts))(*parts)
    return (operator_out, projected)


def solution(mesh):
    seq_count, chan_count = mesh.shape["seq"], mesh.shape["chan"]
    shape = (seq_count // 2, 2, chan_count // PAIR, PAIR)
    paired = Mesh(mesh.devices.reshape(shape), ("zx", "core", "quad", "side"))
    seq, chan = ("zx", "core"), ("quad", "side")
    placed = (
        P(seq, chan),
        P(seq, chan),
        P(seq, chan),
        P(seq, chan),
        P(chan),
        P(chan, None),
    )
    return jax.shard_map(
        shards,
        mesh=paired,
        in_specs=placed,
        out_specs=(P(seq, chan), P(seq, chan)),
        check_vma=False,
    )
```

time: 102 us -> 79.3 us (0.78)
  blocking collectives: 50.9 us -> 0 us
  starting transfers between devices: 14.8 us -> 54.9 us
  local copies, waits for them, and re-layouts: 13.3 us -> 0.06 us
  Pallas kernels: 5.98 us -> 11.8 us
  waiting for transfers between devices: 14.3 us -> 10.7 us
    all_to_all x2 -> x0, blocking collectives: 50.9 us -> none  [the longest x1 34.4 us: shards(): lax.all_to_all(partial, 'chan', split_axis=0, concat_axis=0, tiled=True)]
    ppermute x0 -> x10, starting transfers between devices: none -> 31.5 us  [the longest x3 13.8 us: shards(): parts.append(lax.ppermute(part, chan, pairs))]
    unnamed x26 -> x18, local copies, waits for them, and re-layouts: 12.6 us -> 0.06 us
    all_to_all x1 -> x2, starting transfers between devices: 14.8 us -> 23.4 us  [the longest x1 14.8 us: shards(): lax.all_to_all(packed.reshape(seq_count, 2 * group, rows), seq, split_axi...]
    all_to_all x1 -> x2, waiting for transfers between devices: 14.3 us -> 7.48 us  [the longest x1 4.06 us: shards(): lax.all_to_all(turned.reshape(PAIR * seq_count, group, rows), ('side',) +...]
    pallas_call x3 -> x8, Pallas kernels: 5.98 us -> 11.8 us  [the longest x1 3.01 us: shards(): call(functools.partial(convolve_kernel, group, seq_count), 'convolve', [p...]
    ppermute x0 -> x10, waiting for transfers between devices: none -> 3.18 us  [the longest x1 1.51 us: shards(): parts.append(lax.ppermute(partner, 'side', swap))]
  transfers between devices with their start and end apart: 1 -> 12, of which waited for: 1 -> 5; matrix products, arithmetic and copies ran while one was open for 1% -> 0% of each run, Pallas kernels for 0% -> 9%
where the time goes in v2:
time: 79.3 us; the launch traced here: 78.3 us
  starting transfers between devices  54.9 us (69%)
  Pallas kernels  11.8 us (15%)
  waiting for transfers between devices  10.7 us (13%)
  between operations  0.95 us (1%)
    all_to_all x1, starting transfers between devices, shards(): lax.all_to_all(packed.reshape(seq_count, 2 * group, rows), seq, split_axi...  14.8 us
    ppermute x3, starting transfers between devices, shards(): parts.append(lax.ppermute(part, chan, pairs))  13.8 us
    all_to_all x1, starting transfers between devices, shards(): lax.all_to_all(turned.reshape(PAIR * seq_count, group, rows), ('side',) +...  8.53 us
    ppermute x3, starting transfers between devices, shards(): near = [lax.ppermute(x, 'side', swap) for x in near]  8.49 us
    ppermute x3, starting transfers between devices, permuted_after(): return (arrays, [lax.ppermute(x, axis, pairs) for x in arrays])  7.3 us
    all_to_all x1, waiting for transfers between devices, shards(): lax.all_to_all(turned.reshape(PAIR * seq_count, group, rows), ('side',) +...  4.06 us
    all_to_all x1, waiting for transfers between devices, shards(): lax.all_to_all(packed.reshape(seq_count, 2 * group, rows), seq, split_axi...  3.42 us
    pallas_call x1, Pallas kernels, shards(): call(functools.partial(convolve_kernel, group, seq_count), 'convolve', [p...  3.01 us
  transfers between devices with their start and end apart: 12, of which 5 were waited for; matrix products, arithmetic and copies ran while one was open for 0% of the time, Pallas kernels for 9%

profile of v2, /device:TPU:1, one launch (start us, length us, event | category | flops | bytes accessed | tf_op | source)
XLA Modules:
  0.0 78.3 jit_solution(11264904918973672665)
XLA Ops:
  0.6 0.0 copy-start.5
  0.6 0.0 copy-start
  0.7 0.0 copy-start.1
  0.7 0.0 copy-start.2
  0.7 0.0 copy-start.3
  0.7 0.0 copy-start.6
  0.7 0.0 copy-start.7
  0.7 0.0 copy-start.4
  0.7 0.0 copy-start.8
  0.7 2.0 %pack.1.packed_ref = bf16[1024,128]{1,0:T(8,128)(2,1)} custom-call(bf16[128,512]{1,0:T(8,128)(2,1)} %key_ref.1, bf16[128,512]{1,0:T(8,128)(2,1)} %value_ref.1, bf16[128,512]{1,0:T(8,128)(2,1)} %filter_ref.1), custom_call_target="tpu_custom_call" | custom-call | tf_op jit(solution)/shard_map/pack/pallas_call | solution.py:272
  2.8 14.8 %all-to-all-start = ((bf16[64,16,128]{2,1,0:T(8,128)(2,1)}), bf16[64,16,128]{2,1,0:T(8,128)(2,1)S(1)}, u32[]{:S(2)}, u32[]{:S(2)}) async-start(bf16[64,16,128]{2,1,0:T(8,128)(2,1)} %bitcast), calls=%async_computation | async-start | bytes 524288 | tf_op jit(solution)/shard_map/all_to_all | solution.py:279
  17.6 1.2 %ship.1 = (bf16[256,512]{1,0:T(8,128)(2,1)S(1)}, bf16[256,512]{1,0:T(8,128)(2,1)S(1)}, bf16[384,512]{1,0:T(8,128)(2,1)S(1)}) custom-call(bf16[128,512]{1,0:T(8,128)(2,1)} %query_ref.3, bf16[512,4096]{1,0:T(8,128)(2,1)} %weight_ref.5, bf16[1024,128]{1,0:T(8,128)(2,1)} %pack.1.packed_ref), custom_call_target="tpu_custom_call" | custom-call | tf_op jit(solution)/shard_map/ship/pallas_call | solution.py:285
  18.9 3.2 %collective-permute-start.2 = (bf16[384,512]{1,0:T(8,128)(2,1)S(1)}, bf16[384,512]{1,0:T(8,128)(2,1)S(1)}, u32[]{:S(2)}, u32[]{:S(2)}) collective-permute-start(bf16[384,512]{1,0:T(8,128)(2,1)S(1)} %get-tuple-element.19), channel_id=1, source_target_pairs={{0,1},{1,0},{2,3},{3,2},{4,5},{5,4},{6,7},{7,6},{8,9},{9,8},{10,11... | collective-permute-start | bytes 1179656 | tf_op jit(solution)/shard_map/ppermute | solution.py:292
  22.1 2.1 %collective-permute-start = (bf16[256,512]{1,0:T(8,128)(2,1)S(1)}, bf16[256,512]{1,0:T(8,128)(2,1)S(1)}, u32[]{:S(2)}, u32[]{:S(2)}) collective-permute-start(bf16[256,512]{1,0:T(8,128)(2,1)S(1)} %get-tuple-element.17), channel_id=1, source_target_pairs={{0,1},{1,0},{2,3},{3,2},{4,5},{5,4},{6,7},{7,6},{8,9},{9,8},{10,11... | collective-permute-start | bytes 786440 | tf_op jit(solution)/shard_map/ppermute | solution.py:292
  24.2 3.2 %collective-permute-start.1 = (bf16[256,512]{1,0:T(8,128)(2,1)S(1)}, bf16[256,512]{1,0:T(8,128)(2,1)S(1)}, u32[]{:S(2)}, u32[]{:S(2)}) collective-permute-start(bf16[256,512]{1,0:T(8,128)(2,1)S(1)} %get-tuple-element.18), channel_id=1, source_target_pairs={{0,1},{1,0},{2,3},{3,2},{4,5},{5,4},{6,7},{7,6},{8,9},{9,8},{10,11... | collective-permute-start | bytes 786440 | tf_op jit(solution)/shard_map/ppermute | solution.py:292
  27.4 3.4 %all-to-all-done = bf16[64,16,128]{2,1,0:T(8,128)(2,1)S(1)} async-done(((bf16[64,16,128]{2,1,0:T(8,128)(2,1)}), bf16[64,16,128]{2,1,0:T(8,128)(2,1)S(1)}, u32[]{:S(2)}, u32[]{:S(2)}) %all-to-all-start) | async-done | bytes 262176 | tf_op jit(solution)/shard_map/all_to_all | solution.py:279
  30.8 0.0 copy-done.5
  30.8 0.0 copy-done.1
  30.8 0.0 copy-done.2
  30.8 0.0 copy-done.3
  30.8 0.0 copy-done.6
  30.8 0.0 copy-done.7
  30.9 0.0 copy-done.4
  30.9 0.0 copy-done.8
  30.9 3.0 %convolve.1.refs_3_ = bf16[2,512,128]{2,1,0:T(8,128)(2,1)} custom-call(f32[512]{0:T(512)S(1)} %copy-done.8, bf16[1024,128]{1,0:T(8,128)(2,1)S(1)} %bitcast.5, bf16[128,192]{1,0:T(8,128)(2,1)S(1)} %copy-done.4, f32[64,128]{1,0:T(8,128)S(1)} %copy-done.7, f32[64,128]{1,0:T(8,128)S(1)} %copy-done.6, bf16[256,256]{1,0:T(8,128)(2,1)S(1)} %copy-done.3, ...), custom_call_target="tpu_custom_call" | custom-call | tf_op jit(solution)/shard_map/convolve/pallas_call | solution.py:293
  33.9 8.5 %all-to-all-start.1 = ((bf16[128,8,128]{2,1,0:T(8,128)(2,1)}), bf16[128,8,128]{2,1,0:T(8,128)(2,1)S(1)}, u32[]{:S(2)}, u32[]{:S(2)}) async-start(bf16[128,8,128]{2,1,0:T(8,128)(2,1)} %bitcast.2), calls=%async_computation.1 | async-start | bytes 524288 | tf_op jit(solution)/shard_map/all_to_all | solution.py:309
  42.4 0.0 collective-permute-done.refs_0_
  42.4 0.0 collective-permute-done.1.refs_1_
  42.4 0.0 collective-permute-done.2.refs_2_
  42.5 3.0 %collective-permute-start.5 = (bf16[384,512]{1,0:T(8,128)(2,1)S(1)}, bf16[384,512]{1,0:T(8,128)(2,1)S(1)}, u32[]{:S(2)}, u32[]{:S(2)}) collective-permute-start(bf16[384,512]{1,0:T(8,128)(2,1)S(1)} %get-tuple-element.22.rest_2_), channel_id=1, source_target_pairs={{0,8},{8,0},{1,9},{9,1},{2,10},{10,2},{3,11},{11,3},{4,12},{12,4},... | collective-permute-start | bytes 1179656 | tf_op jit(solution)/shard_map/ppermute | solution.py:256
  45.4 1.9 %collective-permute-start.3 = (bf16[256,512]{1,0:T(8,128)(2,1)S(1)}, bf16[256,512]{1,0:T(8,128)(2,1)S(1)}, u32[]{:S(2)}, u32[]{:S(2)}) collective-permute-start(bf16[256,512]{1,0:T(8,128)(2,1)S(1)} %get-tuple-element.20.rest_0_), channel_id=1, source_target_pairs={{0,8},{8,0},{1,9},{9,1},{2,10},{10,2},{3,11},{11,3},{4,12},{12,4},... | collective-permute-start | bytes 786440 | tf_op jit(solution)/shard_map/ppermute | solution.py:256
  47.4 2.4 %collective-permute-start.4 = (bf16[256,512]{1,0:T(8,128)(2,1)S(1)}, bf16[256,512]{1,0:T(8,128)(2,1)S(1)}, u32[]{:S(2)}, u32[]{:S(2)}) collective-permute-start(bf16[256,512]{1,0:T(8,128)(2,1)S(1)} %get-tuple-element.21.rest_1_), channel_id=1, source_target_pairs={{0,8},{8,0},{1,9},{9,1},{2,10},{10,2},{3,11},{11,3},{4,12},{12,4},... | collective-permute-start | bytes 786440 | tf_op jit(solution)/shard_map/ppermute | solution.py:256
  49.8 0.0 collective-permute-done.3.rest_3_
  49.8 1.1 %collective-permute-done.4.rest_4_ = bf16[256,512]{1,0:T(8,128)(2,1)S(1)} collective-permute-done((bf16[256,512]{1,0:T(8,128)(2,1)S(1)}, bf16[256,512]{1,0:T(8,128)(2,1)S(1)}, u32[]{:S(2)}, u32[]{:S(2)}) %collective-permute-start.4) | collective-permute-done | bytes 262176 | tf_op jit(solution)/shard_map/ppermute | solution.py:256
  50.9 0.0 collective-permute-done.5.rest_5_
  50.9 1.0 %stage.1 = (bf16[3,512,512]{2,1,0:T(8,128)(2,1)S(1)}, bf16[2,128,512]{2,1,0:T(8,128)(2,1)S(1)}) custom-call(bf16[128,512]{1,0:T(8,128)(2,1)} %query_ref.3, bf16[256,512]{1,0:T(8,128)(2,1)S(1)} %get-tuple-element.20.rest_0_, bf16[256,512]{1,0:T(8,128)(2,1)S(1)} %get-tuple-element.21.rest_1_, bf16[384,512]{1,0:T(8,128)(2,1)S(1)} %get-tuple-element.22.rest_2_, ...), custom_call_target="tpu_custom_call" | custom-call | tf_op jit(solution)/shard_map/stage/pallas_call | solution.py:301
  51.9 4.1 %all-to-all-done.1 = bf16[128,8,128]{2,1,0:T(8,128)(2,1)S(1)} async-done(((bf16[128,8,128]{2,1,0:T(8,128)(2,1)}), bf16[128,8,128]{2,1,0:T(8,128)(2,1)S(1)}, u32[]{:S(2)}, u32[]{:S(2)}) %all-to-all-start.1) | async-done | bytes 262176 | tf_op jit(solution)/shard_map/all_to_all | solution.py:309
  56.0 2.1 %gate.1 = (bf16[128,512]{1,0:T(8,128)(2,1)S(1)}, bf16[128,512]{1,0:T(8,128)(2,1)S(1)}, bf16[128,512]{1,0:T(8,128)(2,1)S(1)}, bf16[128,512]{1,0:T(8,128)(2,1)S(1)}, bf16[128,512]{1,0:T(8,128)(2,1)S(1)}) custom-call(bf16[2,512,128]{2,1,0:T(8,128)(2,1)S(1)} %bitcast.4, bf16[2,128,512]{2,1,0:T(8,128)(2,1)S(1)} %get-tuple-element.23.queries_ref, ...), custom_call_target="tpu_custom_call" | custom-call | tf_op jit(solution)/shard_map/gate/pallas_call | solution.py:313
  58.0 7.3 %collective-permute-start.6 = (bf16[128,512]{1,0:T(8,128)(2,1)S(1)}, bf16[128,512]{1,0:T(8,128)(2,1)S(1)}, u32[]{:S(2)}, u32[]{:S(2)}) collective-permute-start(bf16[128,512]{1,0:T(8,128)(2,1)S(1)} %get-tuple-element.28), channel_id=1, source_target_pairs={{0,5},{1,4},{2,7},{3,6},{4,1},{5,0},{6,3},{7,2},{8,13},{9,12},{10,... | collective-permute-start | bytes 393224 | tf_op jit(solution)/shard_map/ppermute | solution.py:330
  65.3 2.1 %collective-permute-start.7 = (bf16[128,512]{1,0:T(8,128)(2,1)S(1)}, bf16[128,512]{1,0:T(8,128)(2,1)S(1)}, u32[]{:S(2)}, u32[]{:S(2)}) collective-permute-start(bf16[128,512]{1,0:T(8,128)(2,1)S(1)} %get-tuple-element.29), channel_id=1, source_target_pairs={{0,6},{1,3},{2,0},{3,5},{4,2},{5,7},{6,4},{7,1},{8,14},{9,11},{10,... | collective-permute-start | bytes 393224 | tf_op jit(solution)/shard_map/ppermute | solution.py:330
  67.4 4.5 %collective-permute-start.8 = (bf16[128,512]{1,0:T(8,128)(2,1)S(1)}, bf16[128,512]{1,0:T(8,128)(2,1)S(1)}, u32[]{:S(2)}, u32[]{:S(2)}) collective-permute-start(bf16[128,512]{1,0:T(8,128)(2,1)S(1)} %get-tuple-element.30), channel_id=1, source_target_pairs={{0,7},{1,2},{2,1},{3,4},{4,3},{5,6},{6,5},{7,0},{8,15},{9,10},{10,... | collective-permute-start | bytes 393224 | tf_op jit(solution)/shard_map/ppermute | solution.py:330
  71.9 1.9 %collective-permute-start.9 = (bf16[128,512]{1,0:T(8,128)(2,1)S(1)}, bf16[128,512]{1,0:T(8,128)(2,1)S(1)}, u32[]{:S(2)}, u32[]{:S(2)}) collective-permute-start(bf16[128,512]{1,0:T(8,128)(2,1)S(1)} %get-tuple-element.31), channel_id=1, source_target_pairs={{0,1},{1,0},{2,3},{3,2},{4,5},{5,4},{6,7},{7,6},{8,9},{9,8},{10,11... | collective-permute-start | bytes 393224 | tf_op jit(solution)/shard_map/ppermute | solution.py:331
  73.8 1.7 %keep.1 = (bf16[128,512]{1,0:T(8,128)(2,1)}, f32[128,512]{1,0:T(8,128)S(1)}) custom-call(bf16[128,512]{1,0:T(8,128)(2,1)S(1)} %get-tuple-element.25.own_ref, bf16[512,4096]{1,0:T(8,128)(2,1)} %weight_ref.5), custom_call_target="tpu_custom_call" | custom-call | tf_op jit(solution)/shard_map/keep/pallas_call | solution.py:320
  75.6 0.0 collective-permute-done.6.refs_1_
  75.6 0.0 collective-permute-done.7.refs_2_
  75.6 0.5 collective-permute-done.8.refs_3_
  76.1 1.5 %collective-permute-done.9.refs_4_ = bf16[128,512]{1,0:T(8,128)(2,1)S(1)} collective-permute-done((bf16[128,512]{1,0:T(8,128)(2,1)S(1)}, bf16[128,512]{1,0:T(8,128)(2,1)S(1)}, u32[]{:S(2)}, u32[]{:S(2)}) %collective-permute-start.9) | collective-permute-done | bytes 131104 | tf_op jit(solution)/shard_map/ppermute | solution.py:331
  77.6 0.7 sum.1
  (2 shorter events, 0.0 us)
Async XLA Ops:
  0.6 30.2 %copy-start.5 = (bf16[64,384]{1,0:T(8,128)(2,1)S(1)}, bf16[64,384]{1,0:T(8,128)(2,1)}, u32[]{:S(2)}) copy-start(bf16[64,384]{1,0:T(8,128)(2,1)} %constant.23.clone.last_ref) | copy-start | bytes 147460
  0.6 30.2 %copy-start = (bf16[256,256]{1,0:T(8,128)(2,1)S(1)}, bf16[256,256]{1,0:T(8,128)(2,1)}, u32[]{:S(2)}) copy-start(bf16[256,256]{1,0:T(8,128)(2,1)} %constant.22.clone.back_low) | copy-start | bytes 393220
  0.7 30.2 %copy-start.1 = (bf16[256,256]{1,0:T(8,128)(2,1)S(1)}, bf16[256,256]{1,0:T(8,128)(2,1)}, u32[]{:S(2)}) copy-start(bf16[256,256]{1,0:T(8,128)(2,1)} %constant.21.clone.back_high) | copy-start | bytes 393220
  0.7 30.1 %copy-start.2 = (bf16[256,256]{1,0:T(8,128)(2,1)S(1)}, bf16[256,256]{1,0:T(8,128)(2,1)}, u32[]{:S(2)}) copy-start(bf16[256,256]{1,0:T(8,128)(2,1)} %constant.20.clone.second_low) | copy-start | bytes 393220
  0.7 30.1 %copy-start.3 = (bf16[256,256]{1,0:T(8,128)(2,1)S(1)}, bf16[256,256]{1,0:T(8,128)(2,1)}, u32[]{:S(2)}) copy-start(bf16[256,256]{1,0:T(8,128)(2,1)} %constant.19.clone.second_high) | copy-start | bytes 393220
  0.7 30.1 %copy-start.6 = (f32[64,128]{1,0:T(8,128)S(1)}, f32[64,128]{1,0:T(8,128)}, u32[]{:S(2)}) copy-start(f32[64,128]{1,0:T(8,128)} %constant.18.clone.sin_ref) | copy-start | bytes 98308
  0.7 30.1 %copy-start.7 = (f32[64,128]{1,0:T(8,128)S(1)}, f32[64,128]{1,0:T(8,128)}, u32[]{:S(2)}) copy-start(f32[64,128]{1,0:T(8,128)} %constant.17.clone.cos_ref) | copy-start | bytes 98308
  0.7 30.1 %copy-start.4 = (bf16[128,192]{1,0:T(8,128)(2,1)S(1)}, bf16[128,192]{1,0:T(8,128)(2,1)}, u32[]{:S(2)}) copy-start(bf16[128,192]{1,0:T(8,128)(2,1)} %constant.16.clone.first_ref) | copy-start | bytes 147460
  0.7 30.1 %copy-start.8 = (f32[512]{0:T(512)S(1)}, f32[512]{0:T(512)}, u32[]{:S(2)}) copy-start(f32[512]{0:T(512)} %skip.1) | copy-start | bytes 6148
  2.8 28.0 %all-to-all-start = ((bf16[64,16,128]{2,1,0:T(8,128)(2,1)}), bf16[64,16,128]{2,1,0:T(8,128)(2,1)S(1)}, u32[]{:S(2)}, u32[]{:S(2)}) async-start(bf16[64,16,128]{2,1,0:T(8,128)(2,1)} %bitcast), calls=%async_computation | async-start | bytes 524288 | tf_op jit(solution)/shard_map/all_to_all | solution.py:279
  18.9 23.6 %collective-permute-start.2 = (bf16[384,512]{1,0:T(8,128)(2,1)S(1)}, bf16[384,512]{1,0:T(8,128)(2,1)S(1)}, u32[]{:S(2)}, u32[]{:S(2)}) collective-permute-start(bf16[384,512]{1,0:T(8,128)(2,1)S(1)} %get-tuple-element.19), channel_id=1, source_target_pairs={{0,1},{1,0},{2,3},{3,2},{4,5},{5,4},{6,7},{7,6},{8,9},{9,8},{10,11... | collective-permute-start | bytes 1179656 | tf_op jit(solution)/shard_map/ppermute | solution.py:292
  22.1 20.3 %collective-permute-start = (bf16[256,512]{1,0:T(8,128)(2,1)S(1)}, bf16[256,512]{1,0:T(8,128)(2,1)S(1)}, u32[]{:S(2)}, u32[]{:S(2)}) collective-permute-start(bf16[256,512]{1,0:T(8,128)(2,1)S(1)} %get-tuple-element.17), channel_id=1, source_target_pairs={{0,1},{1,0},{2,3},{3,2},{4,5},{5,4},{6,7},{7,6},{8,9},{9,8},{10,11... | collective-permute-start | bytes 786440 | tf_op jit(solution)/shard_map/ppermute | solution.py:292
  24.2 18.3 %collective-permute-start.1 = (bf16[256,512]{1,0:T(8,128)(2,1)S(1)}, bf16[256,512]{1,0:T(8,128)(2,1)S(1)}, u32[]{:S(2)}, u32[]{:S(2)}) collective-permute-start(bf16[256,512]{1,0:T(8,128)(2,1)S(1)} %get-tuple-element.18), channel_id=1, source_target_pairs={{0,1},{1,0},{2,3},{3,2},{4,5},{5,4},{6,7},{7,6},{8,9},{9,8},{10,11... | collective-permute-start | bytes 786440 | tf_op jit(solution)/shard_map/ppermute | solution.py:292
  33.9 22.1 %all-to-all-start.1 = ((bf16[128,8,128]{2,1,0:T(8,128)(2,1)}), bf16[128,8,128]{2,1,0:T(8,128)(2,1)S(1)}, u32[]{:S(2)}, u32[]{:S(2)}) async-start(bf16[128,8,128]{2,1,0:T(8,128)(2,1)} %bitcast.2), calls=%async_computation.1 | async-start | bytes 524288 | tf_op jit(solution)/shard_map/all_to_all | solution.py:309
  42.5 8.5 %collective-permute-start.5 = (bf16[384,512]{1,0:T(8,128)(2,1)S(1)}, bf16[384,512]{1,0:T(8,128)(2,1)S(1)}, u32[]{:S(2)}, u32[]{:S(2)}) collective-permute-start(bf16[384,512]{1,0:T(8,128)(2,1)S(1)} %get-tuple-element.22.rest_2_), channel_id=1, source_target_pairs={{0,8},{8,0},{1,9},{9,1},{2,10},{10,2},{3,11},{11,3},{4,12},{12,4},... | collective-permute-start | bytes 1179656 | tf_op jit(solution)/shard_map/ppermute | solution.py:256
  45.4 4.3 %collective-permute-start.3 = (bf16[256,512]{1,0:T(8,128)(2,1)S(1)}, bf16[256,512]{1,0:T(8,128)(2,1)S(1)}, u32[]{:S(2)}, u32[]{:S(2)}) collective-permute-start(bf16[256,512]{1,0:T(8,128)(2,1)S(1)} %get-tuple-element.20.rest_0_), channel_id=1, source_target_pairs={{0,8},{8,0},{1,9},{9,1},{2,10},{10,2},{3,11},{11,3},{4,12},{12,4},... | collective-permute-start | bytes 786440 | tf_op jit(solution)/shard_map/ppermute | solution.py:256
  47.4 3.6 %collective-permute-start.4 = (bf16[256,512]{1,0:T(8,128)(2,1)S(1)}, bf16[256,512]{1,0:T(8,128)(2,1)S(1)}, u32[]{:S(2)}, u32[]{:S(2)}) collective-permute-start(bf16[256,512]{1,0:T(8,128)(2,1)S(1)} %get-tuple-element.21.rest_1_), channel_id=1, source_target_pairs={{0,8},{8,0},{1,9},{9,1},{2,10},{10,2},{3,11},{11,3},{4,12},{12,4},... | collective-permute-start | bytes 786440 | tf_op jit(solution)/shard_map/ppermute | solution.py:256
  58.0 17.5 %collective-permute-start.6 = (bf16[128,512]{1,0:T(8,128)(2,1)S(1)}, bf16[128,512]{1,0:T(8,128)(2,1)S(1)}, u32[]{:S(2)}, u32[]{:S(2)}) collective-permute-start(bf16[128,512]{1,0:T(8,128)(2,1)S(1)} %get-tuple-element.28), channel_id=1, source_target_pairs={{0,5},{1,4},{2,7},{3,6},{4,1},{5,0},{6,3},{7,2},{8,13},{9,12},{10,... | collective-permute-start | bytes 393224 | tf_op jit(solution)/shard_map/ppermute | solution.py:330
  65.3 10.2 %collective-permute-start.7 = (bf16[128,512]{1,0:T(8,128)(2,1)S(1)}, bf16[128,512]{1,0:T(8,128)(2,1)S(1)}, u32[]{:S(2)}, u32[]{:S(2)}) collective-permute-start(bf16[128,512]{1,0:T(8,128)(2,1)S(1)} %get-tuple-element.29), channel_id=1, source_target_pairs={{0,6},{1,3},{2,0},{3,5},{4,2},{5,7},{6,4},{7,1},{8,14},{9,11},{10,... | collective-permute-start | bytes 393224 | tf_op jit(solution)/shard_map/ppermute | solution.py:330
  67.4 8.7 %collective-permute-start.8 = (bf16[128,512]{1,0:T(8,128)(2,1)S(1)}, bf16[128,512]{1,0:T(8,128)(2,1)S(1)}, u32[]{:S(2)}, u32[]{:S(2)}) collective-permute-start(bf16[128,512]{1,0:T(8,128)(2,1)S(1)} %get-tuple-element.30), channel_id=1, source_target_pairs={{0,7},{1,2},{2,1},{3,4},{4,3},{5,6},{6,5},{7,0},{8,15},{9,10},{10,... | collective-permute-start | bytes 393224 | tf_op jit(solution)/shard_map/ppermute | solution.py:330
  71.9 5.7 %collective-permute-start.9 = (bf16[128,512]{1,0:T(8,128)(2,1)S(1)}, bf16[128,512]{1,0:T(8,128)(2,1)S(1)}, u32[]{:S(2)}, u32[]{:S(2)}) collective-permute-start(bf16[128,512]{1,0:T(8,128)(2,1)S(1)} %get-tuple-element.31), channel_id=1, source_target_pairs={{0,1},{1,0},{2,3},{3,2},{4,5},{5,4},{6,7},{7,6},{8,9},{9,8},{10,11... | collective-permute-start | bytes 393224 | tf_op jit(solution)/shard_map/ppermute | solution.py:331

commit v3 on v2

--- a/solution.py
+++ b/solution.py
@@ -152,16 +152,39 @@
         out_ref[i] = out
 
 
-def ship_kernel(steps, planes, query_ref, weight_ref, packed_ref, *rest):
+def segments(steps, half, rows):
+    middle = len(steps) // 2
+    found, at = [], [0, 0]
+
+    def put(piece, index, row, count):
+        found.append((piece, at[piece], index, row, count))
+        at[piece] += count
+
+    for index in range(middle):
+        put(0, index, 0, half)
+    put(0, middle, 0, half // 2)
+    put(1, middle, half // 2, half // 2)
+    for index in range(middle + 1, len(steps)):
+        put(1, index, 0, half)
+    for piece in range(2):
+        put(piece, len(steps), piece * rows // 2, rows // 2)
+    return at[0], found
+
+
+def ship_kernel(steps, planes, found, query_ref, weight_ref, packed_ref, *rest):
     del packed_ref
     *out_refs, sems = rest
     partner = place()[1]
-    count, width = out_refs[0].shape
-    rows = pl.ds(pl.multiple_of(lax.axis_index("core") * count, count), count)
-    pairs = [(query_ref, out_refs[-1].at[pl.ds(count, query_ref.shape[0])])]
-    for step, out_ref in zip(steps, out_refs, strict=True):
-        columns = columns_of(served(partner, step, planes), width)
-        pairs.append((weight_ref.at[rows, columns], out_ref.at[pl.ds(0, count)]))
+    width = out_refs[0].shape[1]
+    base = lax.axis_index("core") * (weight_ref.shape[0] // 2)
+    pairs = []
+    for piece, at, index, row, count in found:
+        if index < len(steps):
+            rows = pl.ds(pl.multiple_of(base + row, 16), count)
+            source = weight_ref.at[rows, columns_of(served(partner, steps[index], planes), width)]
+        else:
+            source = query_ref.at[pl.ds(row, count)]
+        pairs.append((source, out_refs[piece].at[pl.ds(at, count)]))
     wait_all(fetch(pairs, sems))
 
 
@@ -169,38 +192,53 @@
     del refs
 
 
-def stage_kernel(query_ref, *rest):
-    *piece_refs, weight_ref, queries_ref, sems = rest
-    count = len(piece_refs) // 2
-    near_refs, far_refs = piece_refs[:count], piece_refs[count:]
-    core = lax.axis_index("core")
-    half = weight_ref.shape[1] // 2
-    near = pl.ds(pl.multiple_of(core * half, half), half)
-    far = pl.ds(pl.multiple_of((1 - core) * half, half), half)
-    rows = pl.ds(half, query_ref.shape[0])
-    pairs = [(query_ref, queries_ref.at[0]), (near_refs[-1].at[rows], queries_ref.at[1])]
-    for i in range(count):
-        pairs.append((near_refs[i].at[pl.ds(0, half)], weight_ref.at[i, near]))
-        pairs.append((far_refs[i].at[pl.ds(0, half)], weight_ref.at[i, far]))
+def stage_kernel(steps, planes, query_ref, weight_ref, after_ref, early_ref, query_out, late_ref, sems):
+    del after_ref
+    plane, partner = place()
+    width = early_ref.shape[2]
+    early = early_ref.shape[0]
+    targets = [served(plane, step, planes) for step in steps] + [partner]
+    pairs = [(query_ref, query_out)]
+    for i, target in enumerate(targets):
+        held = early_ref.at[i] if i < early else late_ref.at[i - early]
+        pairs.append((weight_ref.at[:, columns_of(target, width)], held))
     wait_all(fetch(pairs, sems))
 
 
-def gate_kernel(steps, planes, turned_ref, queries_ref, other_weight, weight_ref, own_ref, *rest):
-    *partial_refs, partner_ref, held, sems = rest
-    plane, partner = place()
-    width = held.shape[2]
-    targets = [served(plane, step, planes) for step in steps] + [partner]
-    copies = fetch([(weight_ref.at[:, columns_of(t, width)], held.at[i]) for i, t in enumerate(targets)], sems)
+def across(found, index, other, near_refs, far_refs):
+    half = other.shape[1] // 2
+    low, high = other[:, :half], other[:, half:]
+    first = lax.axis_index("core") == 0
+    near, far = jnp.where(first, low, high), jnp.where(first, high, low)
+    total = None
+    for piece, at, owner, row, count in found:
+        if owner == index:
+            rows = pl.ds(at, count)
+            part = dot(near[:, row : row + count], near_refs[piece][rows, :])
+            part = part + dot(far[:, row : row + count], far_refs[piece][rows, :])
+            total = part if total is None else total + part
+    return total
+
+
+def gate_kernel(found, turned_ref, query_ref, early_ref, *rest):
+    near_refs, far_refs, (own_ref, other_ref, *partial_refs) = rest[:2], rest[2:4], rest[4:]
     side = lax.axis_index("side")
-    other = (queries_ref[1].astype(f32) * turned_ref[1 - side].astype(f32).T).astype(bf16)
-    own = (queries_ref[0].astype(f32) * turned_ref[side].astype(f32).T).astype(bf16)
+    count = max(index for _, _, index, _, _ in found)
+    passed = [near_refs[piece][pl.ds(at, size), :] for piece, at, index, _, size in found if index == count]
+    passed = jnp.concatenate(passed, axis=0)
+    other = (passed.astype(f32) * turned_ref[1 - side].astype(f32).T).astype(bf16)
+    own = (query_ref[...].astype(f32) * turned_ref[side].astype(f32).T).astype(bf16)
     own_ref[...] = own
-    across = [dot(other, other_weight[i]) for i in range(len(steps))]
+    other_ref[...] = other
     for i, partial_ref in enumerate(partial_refs):
-        copies[i].wait()
-        partial_ref[...] = (dot(own, held[i]) + across[i]).astype(bf16)
-    copies[-1].wait()
-    partner_ref[...] = dot(own, held[len(steps)]).astype(bf16)
+        partial_ref[...] = (dot(own, early_ref[i]) + across(found, i, other, near_refs, far_refs)).astype(bf16)
+
+
+def near_kernel(found, index, own_ref, other_ref, late_ref, *rest):
+    near_refs, far_refs, (served_ref, partner_ref) = rest[:2], rest[2:4], rest[4:]
+    own = own_ref[...]
+    served_ref[...] = (dot(own, late_ref[0]) + across(found, index, other_ref[...], near_refs, far_refs)).astype(bf16)
+    partner_ref[...] = dot(own, late_ref[1]).astype(bf16)
 
 
 def keep_kernel(own_ref, weight_ref, out_ref, kept_ref, held, sems):
@@ -243,17 +281,16 @@
     return [pltpu.with_memory_space_constraint(x, pltpu.VMEM) for x in arrays]
 
 
-def permuted_after(arrays, after, axis, pairs):
-    count = len(arrays)
-    arrays = call(
+def permuted_after(array, after, axis, pairs):
+    (array,) = call(
         hold_kernel,
         "hold",
-        [jax.ShapeDtypeStruct(x.shape, x.dtype) for x in arrays],
-        [ANY] * (count + 1),
-        out_specs=[ANY] * count,
-        input_output_aliases={i: i for i in range(count)},
-    )(*arrays, after)
-    return arrays, [lax.ppermute(x, axis, pairs) for x in arrays]
+        [jax.ShapeDtypeStruct(array.shape, array.dtype)],
+        [ANY] * 2,
+        out_specs=[ANY],
+        input_output_aliases={0: 0},
+    )(array, after)
+    return array, lax.ppermute(array, axis, pairs)
 
 
 def shards(key_branch, value_branch, query_branch, long_filter, skip_scale, out_weight):
@@ -280,14 +317,13 @@
         packed.reshape(seq_count, 2 * group, rows), seq, split_axis=0, concat_axis=0, tiled=True
     ).reshape(2 * chans, rows)
     swap = [(0, 1), (1, 0)]
-    half = chans // 2
-    piece_rows = [half] * (len(steps) - 1) + [half + rows]
+    size, found = segments(steps, chans // 2, rows)
     near = call(
-        functools.partial(ship_kernel, steps, planes),
+        functools.partial(ship_kernel, steps, planes, found),
         "ship",
-        [pltpu.VMEM((count, width), bf16) for count in piece_rows],
+        [pltpu.VMEM((size, width), bf16)] * 2,
         [ANY] * 3,
-        [dma((1 + len(steps),))],
+        [dma((len(found),))],
     )(query_branch, out_weight, packed)
     near = [lax.ppermute(x, "side", swap) for x in near]
     (turned,) = call(
@@ -297,26 +333,36 @@
         [SMEM] + [VMEM] * (1 + len(tables)),
         [pltpu.VMEM((2 * chans, rows), f32), pltpu.VMEM((chans, rows), f32)],
     )(skip_scale, arrived, *[jnp.asarray(t) for t in tables])
-    near, far = permuted_after(near, turned, "core", swap)
-    staged = call(
-        stage_kernel,
+    near, far = zip(*[permuted_after(x, turned, "core", swap) for x in near], strict=True)
+    early = len(steps) - 1
+    early_weight, query, late_weight = call(
+        functools.partial(stage_kernel, steps, planes),
         "stage",
-        [pltpu.VMEM((len(steps), chans, width), bf16), pltpu.VMEM((PAIR, rows, chans), bf16)],
-        [ANY] * (1 + 2 * len(steps)),
-        [dma((2 * len(steps) + 2,))],
-    )(query_branch, *near, *far)
-    other_weight, queries = in_vmem(*staged)
+        [
+            pltpu.VMEM((early, chans, width), bf16),
+            pltpu.VMEM((rows, chans), bf16),
+            pltpu.HBM((2, chans, width), bf16),
+        ],
+        [ANY] * 3,
+        [dma((len(steps) + 2,))],
+    )(query_branch, out_weight, turned)
+    early_weight, query = in_vmem(early_weight, query)
+    pieces = in_vmem(*near, *far)
     turned = lax.all_to_all(
         turned.reshape(PAIR * seq_count, group, rows), ("side",) + seq, split_axis=0, concat_axis=0, tiled=True
     ).reshape(PAIR, chans, rows)
     block = pltpu.VMEM((rows, width), bf16)
-    own, *sent, partner = call(
-        functools.partial(gate_kernel, steps, planes),
+    gated = pltpu.VMEM((rows, chans), bf16)
+    own, other, *sent = call(
+        functools.partial(gate_kernel, found),
         "gate",
-        [pltpu.VMEM((rows, chans), bf16)] + [block] * (len(steps) + 1),
-        [VMEM] * 3 + [ANY],
-        [pltpu.VMEM((len(steps) + 1, chans, width), bf16), dma((len(steps) + 1,))],
-    )(turned, queries, other_weight, out_weight)
+        [gated] * 2 + [block] * early,
+        [VMEM] * 7,
+        cost_estimate=pl.CostEstimate(flops=4 * 10**9, bytes_accessed=16 * 2**20, transcendentals=0),
+    )(turned, query, early_weight, *pieces)
+    last, partner = call(
+        functools.partial(near_kernel, found, early), "near", [block] * 2, [VMEM] * 7
+    )(own, other, late_weight, *pieces)
     operator_out, kept = call(
         keep_kernel,
         "keep",
@@ -325,7 +371,7 @@
         [pltpu.VMEM((chans, width), bf16), dma((1,))],
     )(own, out_weight)
     parts = [kept]
-    for part, step in zip(sent, steps, strict=True):
+    for part, step in zip((*sent, last), steps, strict=True):
         pairs = [(i, (i + (step if i % PAIR else planes - step)) % planes) for i in range(planes)]
         parts.append(lax.ppermute(part, chan, pairs))
     parts.append(lax.ppermute(partner, "side", swap))

time: 79.3 us -> 75.4 us (0.951)
  starting transfers between devices: 54.9 us -> 47.3 us
  waiting for transfers between devices: 10.7 us -> 14 us
    ppermute x3 -> x2, starting transfers between devices: 8.49 us -> 5.28 us  [shards(): near = [lax.ppermute(x, 'side', swap) for x in near]]
    all_to_all x1, waiting for transfers between devices: 3.42 us -> 6.62 us  [shards(): lax.all_to_all(packed.reshape(seq_count, 2 * group, rows), seq, split_axi...]
    all_to_all x1, starting transfers between devices: 8.53 us -> 6.51 us  [shards(): lax.all_to_all(turned.reshape(PAIR * seq_count, group, rows), ('side',) +...]
    ppermute x3 -> x2, starting transfers between devices: 7.3 us -> 5.37 us  [permuted_after(): return (array, lax.ppermute(array, axis, pairs))]
    all_to_all x1, waiting for transfers between devices: 4.06 us -> 5.44 us  [shards(): lax.all_to_all(turned.reshape(PAIR * seq_count, group, rows), ('side',) +...]
    ppermute x3 -> x2, waiting for transfers between devices: 1.13 us -> 0.01 us  [permuted_after(): return (array, lax.ppermute(array, axis, pairs))]
    pallas_call x4 -> x6, Pallas kernels: 4.27 us -> 4.85 us  [the longest x1 2.67 us: shards(): call(functools.partial(stage_kernel, steps, planes), 'stage', [pltpu.VMEM...]
  transfers between devices with their start and end apart: 12 -> 10, of which waited for: 5 -> 4; matrix products, arithmetic and copies ran while one was open for 0% -> 0% of each run, Pallas kernels for 9% -> 12%
where the time goes in v3:
time: 75.4 us; the launch traced here: 74.7 us
  starting transfers between devices  47.3 us (63%)
  waiting for transfers between devices  14 us (19%)
  Pallas kernels  12.4 us (16%)
  between operations  0.95 us (1%)
    all_to_all x1, starting transfers between devices, shards(): lax.all_to_all(packed.reshape(seq_count, 2 * group, rows), seq, split_axi...  14.8 us
    ppermute x3, starting transfers between devices, shards(): parts.append(lax.ppermute(part, chan, pairs))  13.3 us
    all_to_all x1, waiting for transfers between devices, shards(): lax.all_to_all(packed.reshape(seq_count, 2 * group, rows), seq, split_axi...  6.62 us
    all_to_all x1, starting transfers between devices, shards(): lax.all_to_all(turned.reshape(PAIR * seq_count, group, rows), ('side',) +...  6.51 us
    all_to_all x1, waiting for transfers between devices, shards(): lax.all_to_all(turned.reshape(PAIR * seq_count, group, rows), ('side',) +...  5.44 us
    ppermute x2, starting transfers between devices, permuted_after(): return (array, lax.ppermute(array, axis, pairs))  5.37 us
    ppermute x2, starting transfers between devices, shards(): near = [lax.ppermute(x, 'side', swap) for x in near]  5.28 us
    pallas_call x1, Pallas kernels, shards(): call(functools.partial(convolve_kernel, group, seq_count), 'convolve', [p...  3.03 us
  transfers between devices with their start and end apart: 10, of which 4 were waited for; matrix products, arithmetic and copies ran while one was open for 0% of the time, Pallas kernels for 12%

profile of v3, /device:TPU:1, one launch (start us, length us, event | category | flops | bytes accessed | tf_op | source)
XLA Modules:
  0.0 74.7 jit_solution(6758668663961738305)
XLA Ops:
  0.6 0.0 copy-start.6
  0.6 0.0 copy-start.1
  0.7 0.0 copy-start.2
  0.7 0.0 copy-start.3
  0.7 0.0 copy-start.4
  0.7 0.0 copy-start.7
  0.7 0.0 copy-start.8
  0.7 0.0 copy-start.5
  0.7 0.0 copy-start.9
  0.7 2.0 %pack.1.packed_ref = bf16[1024,128]{1,0:T(8,128)(2,1)} custom-call(bf16[128,512]{1,0:T(8,128)(2,1)} %key_ref.1, bf16[128,512]{1,0:T(8,128)(2,1)} %value_ref.1, bf16[128,512]{1,0:T(8,128)(2,1)} %filter_ref.1), custom_call_target="tpu_custom_call" | custom-call | tf_op jit(solution)/shard_map/pack/pallas_call | solution.py:309
  2.8 14.8 %all-to-all-start = ((bf16[64,16,128]{2,1,0:T(8,128)(2,1)}), bf16[64,16,128]{2,1,0:T(8,128)(2,1)S(1)}, u32[]{:S(2)}, u32[]{:S(2)}) async-start(bf16[64,16,128]{2,1,0:T(8,128)(2,1)} %bitcast), calls=%async_computation | async-start | bytes 524288 | tf_op jit(solution)/shard_map/all_to_all | solution.py:316
  17.6 1.2 %ship.1 = (bf16[448,512]{1,0:T(8,128)(2,1)S(1)}, bf16[448,512]{1,0:T(8,128)(2,1)S(1)}) custom-call(bf16[128,512]{1,0:T(8,128)(2,1)} %query_ref.3, bf16[512,4096]{1,0:T(8,128)(2,1)} %weight_ref.5, bf16[1024,128]{1,0:T(8,128)(2,1)} %pack.1.packed_ref), custom_call_target="tpu_custom_call" | custom-call | tf_op jit(solution)/shard_map/ship/pallas_call | solution.py:321
  18.9 3.2 %collective-permute-start = (bf16[448,512]{1,0:T(8,128)(2,1)S(1)}, bf16[448,512]{1,0:T(8,128)(2,1)S(1)}, u32[]{:S(2)}, u32[]{:S(2)}) collective-permute-start(bf16[448,512]{1,0:T(8,128)(2,1)S(1)} %get-tuple-element.17), channel_id=1, source_target_pairs={{0,1},{1,0},{2,3},{3,2},{4,5},{5,4},{6,7},{7,6},{8,9},{9,8},{10,11... | collective-permute-start | bytes 1376264 | tf_op jit(solution)/shard_map/ppermute | solution.py:328
  22.1 2.1 %collective-permute-start.1 = (bf16[448,512]{1,0:T(8,128)(2,1)S(1)}, bf16[448,512]{1,0:T(8,128)(2,1)S(1)}, u32[]{:S(2)}, u32[]{:S(2)}) collective-permute-start(bf16[448,512]{1,0:T(8,128)(2,1)S(1)} %get-tuple-element.18), channel_id=1, source_target_pairs={{0,1},{1,0},{2,3},{3,2},{4,5},{5,4},{6,7},{7,6},{8,9},{9,8},{10,11... | collective-permute-start | bytes 1376264 | tf_op jit(solution)/shard_map/ppermute | solution.py:328
  24.2 6.6 %all-to-all-done = bf16[64,16,128]{2,1,0:T(8,128)(2,1)S(1)} async-done(((bf16[64,16,128]{2,1,0:T(8,128)(2,1)}), bf16[64,16,128]{2,1,0:T(8,128)(2,1)S(1)}, u32[]{:S(2)}, u32[]{:S(2)}) %all-to-all-start) | async-done | bytes 262176 | tf_op jit(solution)/shard_map/all_to_all | solution.py:316
  30.8 0.0 copy-done.6
  30.8 0.0 copy-done.1
  30.8 0.0 copy-done.2
  30.8 0.0 copy-done.3
  30.8 0.0 copy-done.4
  30.8 0.0 copy-done.7
  30.8 0.0 copy-done.8
  30.9 0.0 copy-done.5
  30.9 0.0 copy-done.9
  30.9 3.0 %convolve.1.after_ref.refs_1_ = bf16[2,512,128]{2,1,0:T(8,128)(2,1)} custom-call(f32[512]{0:T(512)S(1)} %copy-done.9, bf16[1024,128]{1,0:T(8,128)(2,1)S(1)} %bitcast.4, bf16[128,192]{1,0:T(8,128)(2,1)S(1)} %copy-done.5, f32[64,128]{1,0:T(8,128)S(1)} %copy-done.8, f32[64,128]{1,0:T(8,128)S(1)} %copy-done.7, bf16[256,256]{1,0:T(8,128)(2,1)S(1)} %copy-done.4, ...), custom_call_target="tpu_custom_call" | custom-call | tf_op jit(solution)/shard_map/convolve/pallas_call | solution.py:329
  33.9 6.5 %all-to-all-start.1 = ((bf16[128,8,128]{2,1,0:T(8,128)(2,1)}), bf16[128,8,128]{2,1,0:T(8,128)(2,1)S(1)}, u32[]{:S(2)}, u32[]{:S(2)}) async-start(bf16[128,8,128]{2,1,0:T(8,128)(2,1)} %bitcast.2), calls=%async_computation.1 | async-start | bytes 524288 | tf_op jit(solution)/shard_map/all_to_all | solution.py:351
  40.4 0.0 collective-permute-done.refs_0_
  40.4 2.8 %collective-permute-start.2 = (bf16[448,512]{1,0:T(8,128)(2,1)S(1)}, bf16[448,512]{1,0:T(8,128)(2,1)S(1)}, u32[]{:S(2)}, u32[]{:S(2)}) collective-permute-start(bf16[448,512]{1,0:T(8,128)(2,1)S(1)} %hold.2.rest_0_), channel_id=1, source_target_pairs={{0,8},{8,0},{1,9},{9,1},{2,10},{10,2},{3,11},{11,3},{4,12},{12,4},... | collective-permute-start | bytes 1376264 | tf_op jit(solution)/shard_map/ppermute | solution.py:293
  43.2 0.0 collective-permute-done.1.refs_0_
  43.3 2.6 %collective-permute-start.3 = (bf16[448,512]{1,0:T(8,128)(2,1)S(1)}, bf16[448,512]{1,0:T(8,128)(2,1)S(1)}, u32[]{:S(2)}, u32[]{:S(2)}) collective-permute-start(bf16[448,512]{1,0:T(8,128)(2,1)S(1)} %hold.3.rest_1_), channel_id=1, source_target_pairs={{0,8},{8,0},{1,9},{9,1},{2,10},{10,2},{3,11},{11,3},{4,12},{12,4},... | collective-permute-start | bytes 1376264 | tf_op jit(solution)/shard_map/ppermute | solution.py:293
  45.8 2.7 %stage.1 = (bf16[2,512,512]{2,1,0:T(8,128)(2,1)S(1)}, bf16[128,512]{1,0:T(8,128)(2,1)S(1)}, bf16[2,512,512]{2,1,0:T(8,128)(2,1)}) custom-call(bf16[128,512]{1,0:T(8,128)(2,1)} %query_ref.3, bf16[512,4096]{1,0:T(8,128)(2,1)} %weight_ref.5, bf16[2,512,128]{2,1,0:T(8,128)(2,1)} %convolve.1.after_ref.refs_1_), custom_call_target="tpu_custom_call" | custom-call | tf_op jit(solution)/shard_map/stage/pallas_call | solution.py:338
  48.5 0.0 collective-permute-done.2.rest_2_
  48.5 0.0 collective-permute-done.3.rest_3_
  48.5 5.4 %all-to-all-done.1 = bf16[128,8,128]{2,1,0:T(8,128)(2,1)S(1)} async-done(((bf16[128,8,128]{2,1,0:T(8,128)(2,1)}), bf16[128,8,128]{2,1,0:T(8,128)(2,1)S(1)}, u32[]{:S(2)}, u32[]{:S(2)}) %all-to-all-start.1) | async-done | bytes 262176 | tf_op jit(solution)/shard_map/all_to_all | solution.py:351
  54.0 0.0 copy-start
  54.0 0.6 gate.1
  54.6 6.9 %collective-permute-start.4 = (bf16[128,512]{1,0:T(8,128)(2,1)S(1)}, bf16[128,512]{1,0:T(8,128)(2,1)S(1)}, u32[]{:S(2)}, u32[]{:S(2)}) collective-permute-start(bf16[128,512]{1,0:T(8,128)(2,1)S(1)} %get-tuple-element.22), channel_id=1, source_target_pairs={{0,5},{1,4},{2,7},{3,6},{4,1},{5,0},{6,3},{7,2},{8,13},{9,12},{10,... | collective-permute-start | bytes 393224 | tf_op jit(solution)/shard_map/ppermute | solution.py:376
  61.5 2.9 %collective-permute-start.5 = (bf16[128,512]{1,0:T(8,128)(2,1)S(1)}, bf16[128,512]{1,0:T(8,128)(2,1)S(1)}, u32[]{:S(2)}, u32[]{:S(2)}) collective-permute-start(bf16[128,512]{1,0:T(8,128)(2,1)S(1)} %get-tuple-element.23), channel_id=1, source_target_pairs={{0,6},{1,3},{2,0},{3,5},{4,2},{5,7},{6,4},{7,1},{8,14},{9,11},{10,... | collective-permute-start | bytes 393224 | tf_op jit(solution)/shard_map/ppermute | solution.py:376
  64.4 0.0 copy-done
  64.4 0.4 near.1
  64.8 3.5 %collective-permute-start.6 = (bf16[128,512]{1,0:T(8,128)(2,1)S(1)}, bf16[128,512]{1,0:T(8,128)(2,1)S(1)}, u32[]{:S(2)}, u32[]{:S(2)}) collective-permute-start(bf16[128,512]{1,0:T(8,128)(2,1)S(1)} %get-tuple-element.26), channel_id=1, source_target_pairs={{0,7},{1,2},{2,1},{3,4},{4,3},{5,6},{6,5},{7,0},{8,15},{9,10},{10,... | collective-permute-start | bytes 393224 | tf_op jit(solution)/shard_map/ppermute | solution.py:376
  68.3 2.0 %collective-permute-start.7 = (bf16[128,512]{1,0:T(8,128)(2,1)S(1)}, bf16[128,512]{1,0:T(8,128)(2,1)S(1)}, u32[]{:S(2)}, u32[]{:S(2)}) collective-permute-start(bf16[128,512]{1,0:T(8,128)(2,1)S(1)} %get-tuple-element.27), channel_id=1, source_target_pairs={{0,1},{1,0},{2,3},{3,2},{4,5},{5,4},{6,7},{7,6},{8,9},{9,8},{10,11... | collective-permute-start | bytes 393224 | tf_op jit(solution)/shard_map/ppermute | solution.py:377
  70.3 1.7 %keep.1 = (bf16[128,512]{1,0:T(8,128)(2,1)}, f32[128,512]{1,0:T(8,128)S(1)}) custom-call(bf16[128,512]{1,0:T(8,128)(2,1)S(1)} %get-tuple-element.19.own_ref, bf16[512,4096]{1,0:T(8,128)(2,1)} %weight_ref.5), custom_call_target="tpu_custom_call" | custom-call | tf_op jit(solution)/shard_map/keep/pallas_call | solution.py:366
  72.0 0.0 collective-permute-done.4.refs_1_
  72.0 0.0 collective-permute-done.5.refs_2_
  72.0 0.9 %collective-permute-done.6.refs_3_ = bf16[128,512]{1,0:T(8,128)(2,1)S(1)} collective-permute-done((bf16[128,512]{1,0:T(8,128)(2,1)S(1)}, bf16[128,512]{1,0:T(8,128)(2,1)S(1)}, u32[]{:S(2)}, u32[]{:S(2)}) %collective-permute-start.6) | collective-permute-done | bytes 131104 | tf_op jit(solution)/shard_map/ppermute | solution.py:376
  72.9 1.1 %collective-permute-done.7.refs_4_ = bf16[128,512]{1,0:T(8,128)(2,1)S(1)} collective-permute-done((bf16[128,512]{1,0:T(8,128)(2,1)S(1)}, bf16[128,512]{1,0:T(8,128)(2,1)S(1)}, u32[]{:S(2)}, u32[]{:S(2)}) %collective-permute-start.7) | collective-permute-done | bytes 131104 | tf_op jit(solution)/shard_map/ppermute | solution.py:377
  74.0 0.7 sum.1
  (2 shorter events, 0.0 us)
Async XLA Ops:
  0.6 30.2 %copy-start.6 = (bf16[64,384]{1,0:T(8,128)(2,1)S(1)}, bf16[64,384]{1,0:T(8,128)(2,1)}, u32[]{:S(2)}) copy-start(bf16[64,384]{1,0:T(8,128)(2,1)} %constant.23.clone.last_ref) | copy-start | bytes 147460
  0.6 30.2 %copy-start.1 = (bf16[256,256]{1,0:T(8,128)(2,1)S(1)}, bf16[256,256]{1,0:T(8,128)(2,1)}, u32[]{:S(2)}) copy-start(bf16[256,256]{1,0:T(8,128)(2,1)} %constant.22.clone.back_low) | copy-start | bytes 393220
  0.7 30.2 %copy-start.2 = (bf16[256,256]{1,0:T(8,128)(2,1)S(1)}, bf16[256,256]{1,0:T(8,128)(2,1)}, u32[]{:S(2)}) copy-start(bf16[256,256]{1,0:T(8,128)(2,1)} %constant.21.clone.back_high) | copy-start | bytes 393220
  0.7 30.2 %copy-start.3 = (bf16[256,256]{1,0:T(8,128)(2,1)S(1)}, bf16[256,256]{1,0:T(8,128)(2,1)}, u32[]{:S(2)}) copy-start(bf16[256,256]{1,0:T(8,128)(2,1)} %constant.20.clone.second_low) | copy-start | bytes 393220
  0.7 30.1 %copy-start.4 = (bf16[256,256]{1,0:T(8,128)(2,1)S(1)}, bf16[256,256]{1,0:T(8,128)(2,1)}, u32[]{:S(2)}) copy-start(bf16[256,256]{1,0:T(8,128)(2,1)} %constant.19.clone.second_high) | copy-start | bytes 393220
  0.7 30.1 %copy-start.7 = (f32[64,128]{1,0:T(8,128)S(1)}, f32[64,128]{1,0:T(8,128)}, u32[]{:S(2)}) copy-start(f32[64,128]{1,0:T(8,128)} %constant.18.clone.sin_ref) | copy-start | bytes 98308
  0.7 30.1 %copy-start.8 = (f32[64,128]{1,0:T(8,128)S(1)}, f32[64,128]{1,0:T(8,128)}, u32[]{:S(2)}) copy-start(f32[64,128]{1,0:T(8,128)} %constant.17.clone.cos_ref) | copy-start | bytes 98308
  0.7 30.1 %copy-start.5 = (bf16[128,192]{1,0:T(8,128)(2,1)S(1)}, bf16[128,192]{1,0:T(8,128)(2,1)}, u32[]{:S(2)}) copy-start(bf16[128,192]{1,0:T(8,128)(2,1)} %constant.16.clone.first_ref) | copy-start | bytes 147460
  0.7 30.1 %copy-start.9 = (f32[512]{0:T(512)S(1)}, f32[512]{0:T(512)}, u32[]{:S(2)}) copy-start(f32[512]{0:T(512)} %skip.1) | copy-start | bytes 6148
  2.8 28.0 %all-to-all-start = ((bf16[64,16,128]{2,1,0:T(8,128)(2,1)}), bf16[64,16,128]{2,1,0:T(8,128)(2,1)S(1)}, u32[]{:S(2)}, u32[]{:S(2)}) async-start(bf16[64,16,128]{2,1,0:T(8,128)(2,1)} %bitcast), calls=%async_computation | async-start | bytes 524288 | tf_op jit(solution)/shard_map/all_to_all | solution.py:316
  18.9 21.5 %collective-permute-start = (bf16[448,512]{1,0:T(8,128)(2,1)S(1)}, bf16[448,512]{1,0:T(8,128)(2,1)S(1)}, u32[]{:S(2)}, u32[]{:S(2)}) collective-permute-start(bf16[448,512]{1,0:T(8,128)(2,1)S(1)} %get-tuple-element.17), channel_id=1, source_target_pairs={{0,1},{1,0},{2,3},{3,2},{4,5},{5,4},{6,7},{7,6},{8,9},{9,8},{10,11... | collective-permute-start | bytes 1376264 | tf_op jit(solution)/shard_map/ppermute | solution.py:328
  22.1 21.1 %collective-permute-start.1 = (bf16[448,512]{1,0:T(8,128)(2,1)S(1)}, bf16[448,512]{1,0:T(8,128)(2,1)S(1)}, u32[]{:S(2)}, u32[]{:S(2)}) collective-permute-start(bf16[448,512]{1,0:T(8,128)(2,1)S(1)} %get-tuple-element.18), channel_id=1, source_target_pairs={{0,1},{1,0},{2,3},{3,2},{4,5},{5,4},{6,7},{7,6},{8,9},{9,8},{10,11... | collective-permute-start | bytes 1376264 | tf_op jit(solution)/shard_map/ppermute | solution.py:328
  33.9 20.1 %all-to-all-start.1 = ((bf16[128,8,128]{2,1,0:T(8,128)(2,1)}), bf16[128,8,128]{2,1,0:T(8,128)(2,1)S(1)}, u32[]{:S(2)}, u32[]{:S(2)}) async-start(bf16[128,8,128]{2,1,0:T(8,128)(2,1)} %bitcast.2), calls=%async_computation.1 | async-start | bytes 524288 | tf_op jit(solution)/shard_map/all_to_all | solution.py:351
  40.4 8.1 %collective-permute-start.2 = (bf16[448,512]{1,0:T(8,128)(2,1)S(1)}, bf16[448,512]{1,0:T(8,128)(2,1)S(1)}, u32[]{:S(2)}, u32[]{:S(2)}) collective-permute-start(bf16[448,512]{1,0:T(8,128)(2,1)S(1)} %hold.2.rest_0_), channel_id=1, source_target_pairs={{0,8},{8,0},{1,9},{9,1},{2,10},{10,2},{3,11},{11,3},{4,12},{12,4},... | collective-permute-start | bytes 1376264 | tf_op jit(solution)/shard_map/ppermute | solution.py:293
  43.3 5.3 %collective-permute-start.3 = (bf16[448,512]{1,0:T(8,128)(2,1)S(1)}, bf16[448,512]{1,0:T(8,128)(2,1)S(1)}, u32[]{:S(2)}, u32[]{:S(2)}) collective-permute-start(bf16[448,512]{1,0:T(8,128)(2,1)S(1)} %hold.3.rest_1_), channel_id=1, source_target_pairs={{0,8},{8,0},{1,9},{9,1},{2,10},{10,2},{3,11},{11,3},{4,12},{12,4},... | collective-permute-start | bytes 1376264 | tf_op jit(solution)/shard_map/ppermute | solution.py:293
  54.0 10.4 %copy-start = (bf16[2,512,512]{2,1,0:T(8,128)(2,1)S(1)}, bf16[2,512,512]{2,1,0:T(8,128)(2,1)}, u32[]{:S(2)}) copy-start(bf16[2,512,512]{2,1,0:T(8,128)(2,1)} %get-tuple-element.25.late_ref) | copy-start | bytes 3145732
  54.6 17.5 %collective-permute-start.4 = (bf16[128,512]{1,0:T(8,128)(2,1)S(1)}, bf16[128,512]{1,0:T(8,128)(2,1)S(1)}, u32[]{:S(2)}, u32[]{:S(2)}) collective-permute-start(bf16[128,512]{1,0:T(8,128)(2,1)S(1)} %get-tuple-element.22), channel_id=1, source_target_pairs={{0,5},{1,4},{2,7},{3,6},{4,1},{5,0},{6,3},{7,2},{8,13},{9,12},{10,... | collective-permute-start | bytes 393224 | tf_op jit(solution)/shard_map/ppermute | solution.py:376
  61.5 10.5 %collective-permute-start.5 = (bf16[128,512]{1,0:T(8,128)(2,1)S(1)}, bf16[128,512]{1,0:T(8,128)(2,1)S(1)}, u32[]{:S(2)}, u32[]{:S(2)}) collective-permute-start(bf16[128,512]{1,0:T(8,128)(2,1)S(1)} %get-tuple-element.23), channel_id=1, source_target_pairs={{0,6},{1,3},{2,0},{3,5},{4,2},{5,7},{6,4},{7,1},{8,14},{9,11},{10,... | collective-permute-start | bytes 393224 | tf_op jit(solution)/shard_map/ppermute | solution.py:376
  64.8 8.2 %collective-permute-start.6 = (bf16[128,512]{1,0:T(8,128)(2,1)S(1)}, bf16[128,512]{1,0:T(8,128)(2,1)S(1)}, u32[]{:S(2)}, u32[]{:S(2)}) collective-permute-start(bf16[128,512]{1,0:T(8,128)(2,1)S(1)} %get-tuple-element.26), channel_id=1, source_target_pairs={{0,7},{1,2},{2,1},{3,4},{4,3},{5,6},{6,5},{7,0},{8,15},{9,10},{10,... | collective-permute-start | bytes 393224 | tf_op jit(solution)/shard_map/ppermute | solution.py:376
  68.3 5.7 %collective-permute-start.7 = (bf16[128,512]{1,0:T(8,128)(2,1)S(1)}, bf16[128,512]{1,0:T(8,128)(2,1)S(1)}, u32[]{:S(2)}, u32[]{:S(2)}) collective-permute-start(bf16[128,512]{1,0:T(8,128)(2,1)S(1)} %get-tuple-element.27), channel_id=1, source_target_pairs={{0,1},{1,0},{2,3},{3,2},{4,5},{5,4},{6,7},{7,6},{8,9},{9,8},{10,11... | collective-permute-start | bytes 393224 | tf_op jit(solution)/shard_map/ppermute | solution.py:377

commit v4 on v3

--- a/solution.py
+++ b/solution.py
@@ -297,7 +297,8 @@
     seq, chan = ("zx", "core"), ("quad", "side")
     seq_count = lax.axis_size("zx") * lax.axis_size("core")
     planes = PAIR * lax.axis_size("quad")
-    steps = tuple(range(planes // PAIR - 1, 0, -1))
+    steps = (2, 3, 1)
+    assert planes == PAIR * (len(steps) + 1)
     rows, chans = key_branch.shape
     group = chans // seq_count
     width = out_weight.shape[1] // planes

time: 75.4 us -> 74.1 us (0.983)
  starting transfers between devices: 47.3 us -> 46 us
    ppermute x3, starting transfers between devices: 13.3 us -> 11.3 us  [shards(): parts.append(lax.ppermute(part, chan, pairs))]
    ppermute x3, waiting for transfers between devices: 0.89 us -> 1.82 us  [shards(): parts.append(lax.ppermute(part, chan, pairs))]
    ppermute x1, waiting for transfers between devices: 1.08 us -> 0.27 us  [shards(): parts.append(lax.ppermute(partner, 'side', swap))]
where the time goes in v4:
time: 74.1 us; the launch traced here: 73.5 us
  starting transfers between devices  46 us (62%)
  waiting for transfers between devices  14.2 us (19%)
  Pallas kernels  12.4 us (17%)
  between operations  0.95 us (1%)
    all_to_all x1, starting transfers between devices, shards(): lax.all_to_all(packed.reshape(seq_count, 2 * group, rows), seq, split_axi...  14.8 us
    ppermute x3, starting transfers between devices, shards(): parts.append(lax.ppermute(part, chan, pairs))  11.3 us
    all_to_all x1, waiting for transfers between devices, shards(): lax.all_to_all(packed.reshape(seq_count, 2 * group, rows), seq, split_axi...  6.61 us
    all_to_all x1, starting transfers between devices, shards(): lax.all_to_all(turned.reshape(PAIR * seq_count, group, rows), ('side',) +...  6.51 us
    all_to_all x1, waiting for transfers between devices, shards(): lax.all_to_all(turned.reshape(PAIR * seq_count, group, rows), ('side',) +...  5.44 us
    ppermute x2, starting transfers between devices, permuted_after(): return (array, lax.ppermute(array, axis, pairs))  5.37 us
    ppermute x2, starting transfers between devices, shards(): near = [lax.ppermute(x, 'side', swap) for x in near]  5.28 us
    pallas_call x1, Pallas kernels, shards(): call(functools.partial(convolve_kernel, group, seq_count), 'convolve', [p...  3.03 us
  transfers between devices with their start and end apart: 10, of which 4 were waited for; matrix products, arithmetic and copies ran while one was open for 0% of the time, Pallas kernels for 12%

profile of v4, /device:TPU:1, one launch (start us, length us, event | category | flops | bytes accessed | tf_op | source)
XLA Modules:
  0.0 73.5 jit_solution(4934802307292286923)
XLA Ops:
  0.6 0.0 copy-start.6
  0.6 0.0 copy-start.1
  0.7 0.0 copy-start.2
  0.7 0.0 copy-start.3
  0.7 0.0 copy-start.4
  0.7 0.0 copy-start.7
  0.7 0.0 copy-start.8
  0.7 0.0 copy-start.5
  0.7 0.0 copy-start.9
  0.7 2.0 %pack.1.packed_ref = bf16[1024,128]{1,0:T(8,128)(2,1)} custom-call(bf16[128,512]{1,0:T(8,128)(2,1)} %key_ref.1, bf16[128,512]{1,0:T(8,128)(2,1)} %value_ref.1, bf16[128,512]{1,0:T(8,128)(2,1)} %filter_ref.1), custom_call_target="tpu_custom_call" | custom-call | tf_op jit(solution)/shard_map/pack/pallas_call | solution.py:310
  2.8 14.8 %all-to-all-start = ((bf16[64,16,128]{2,1,0:T(8,128)(2,1)}), bf16[64,16,128]{2,1,0:T(8,128)(2,1)S(1)}, u32[]{:S(2)}, u32[]{:S(2)}) async-start(bf16[64,16,128]{2,1,0:T(8,128)(2,1)} %bitcast), calls=%async_computation | async-start | bytes 524288 | tf_op jit(solution)/shard_map/all_to_all | solution.py:317
  17.6 1.2 %ship.1 = (bf16[448,512]{1,0:T(8,128)(2,1)S(1)}, bf16[448,512]{1,0:T(8,128)(2,1)S(1)}) custom-call(bf16[128,512]{1,0:T(8,128)(2,1)} %query_ref.3, bf16[512,4096]{1,0:T(8,128)(2,1)} %weight_ref.5, bf16[1024,128]{1,0:T(8,128)(2,1)} %pack.1.packed_ref), custom_call_target="tpu_custom_call" | custom-call | tf_op jit(solution)/shard_map/ship/pallas_call | solution.py:322
  18.9 3.2 %collective-permute-start = (bf16[448,512]{1,0:T(8,128)(2,1)S(1)}, bf16[448,512]{1,0:T(8,128)(2,1)S(1)}, u32[]{:S(2)}, u32[]{:S(2)}) collective-permute-start(bf16[448,512]{1,0:T(8,128)(2,1)S(1)} %get-tuple-element.17), channel_id=1, source_target_pairs={{0,1},{1,0},{2,3},{3,2},{4,5},{5,4},{6,7},{7,6},{8,9},{9,8},{10,11... | collective-permute-start | bytes 1376264 | tf_op jit(solution)/shard_map/ppermute | solution.py:329
  22.1 2.1 %collective-permute-start.1 = (bf16[448,512]{1,0:T(8,128)(2,1)S(1)}, bf16[448,512]{1,0:T(8,128)(2,1)S(1)}, u32[]{:S(2)}, u32[]{:S(2)}) collective-permute-start(bf16[448,512]{1,0:T(8,128)(2,1)S(1)} %get-tuple-element.18), channel_id=1, source_target_pairs={{0,1},{1,0},{2,3},{3,2},{4,5},{5,4},{6,7},{7,6},{8,9},{9,8},{10,11... | collective-permute-start | bytes 1376264 | tf_op jit(solution)/shard_map/ppermute | solution.py:329
  24.2 6.6 %all-to-all-done = bf16[64,16,128]{2,1,0:T(8,128)(2,1)S(1)} async-done(((bf16[64,16,128]{2,1,0:T(8,128)(2,1)}), bf16[64,16,128]{2,1,0:T(8,128)(2,1)S(1)}, u32[]{:S(2)}, u32[]{:S(2)}) %all-to-all-start) | async-done | bytes 262176 | tf_op jit(solution)/shard_map/all_to_all | solution.py:317
  30.8 0.0 copy-done.6
  30.8 0.0 copy-done.1
  30.8 0.0 copy-done.2
  30.8 0.0 copy-done.3
  30.8 0.0 copy-done.4
  30.8 0.0 copy-done.7
  30.8 0.0 copy-done.8
  30.9 0.0 copy-done.5
  30.9 0.0 copy-done.9
  30.9 3.0 %convolve.1.after_ref.refs_1_ = bf16[2,512,128]{2,1,0:T(8,128)(2,1)} custom-call(f32[512]{0:T(512)S(1)} %copy-done.9, bf16[1024,128]{1,0:T(8,128)(2,1)S(1)} %bitcast.4, bf16[128,192]{1,0:T(8,128)(2,1)S(1)} %copy-done.5, f32[64,128]{1,0:T(8,128)S(1)} %copy-done.8, f32[64,128]{1,0:T(8,128)S(1)} %copy-done.7, bf16[256,256]{1,0:T(8,128)(2,1)S(1)} %copy-done.4, ...), custom_call_target="tpu_custom_call" | custom-call | tf_op jit(solution)/shard_map/convolve/pallas_call | solution.py:330
  33.9 6.5 %all-to-all-start.1 = ((bf16[128,8,128]{2,1,0:T(8,128)(2,1)}), bf16[128,8,128]{2,1,0:T(8,128)(2,1)S(1)}, u32[]{:S(2)}, u32[]{:S(2)}) async-start(bf16[128,8,128]{2,1,0:T(8,128)(2,1)} %bitcast.2), calls=%async_computation.1 | async-start | bytes 524288 | tf_op jit(solution)/shard_map/all_to_all | solution.py:352
  40.4 0.0 collective-permute-done.refs_0_
  40.4 2.8 %collective-permute-start.2 = (bf16[448,512]{1,0:T(8,128)(2,1)S(1)}, bf16[448,512]{1,0:T(8,128)(2,1)S(1)}, u32[]{:S(2)}, u32[]{:S(2)}) collective-permute-start(bf16[448,512]{1,0:T(8,128)(2,1)S(1)} %hold.2.rest_0_), channel_id=1, source_target_pairs={{0,8},{8,0},{1,9},{9,1},{2,10},{10,2},{3,11},{11,3},{4,12},{12,4},... | collective-permute-start | bytes 1376264 | tf_op jit(solution)/shard_map/ppermute | solution.py:293
  43.2 0.0 collective-permute-done.1.refs_0_
  43.3 2.6 %collective-permute-start.3 = (bf16[448,512]{1,0:T(8,128)(2,1)S(1)}, bf16[448,512]{1,0:T(8,128)(2,1)S(1)}, u32[]{:S(2)}, u32[]{:S(2)}) collective-permute-start(bf16[448,512]{1,0:T(8,128)(2,1)S(1)} %hold.3.rest_1_), channel_id=1, source_target_pairs={{0,8},{8,0},{1,9},{9,1},{2,10},{10,2},{3,11},{11,3},{4,12},{12,4},... | collective-permute-start | bytes 1376264 | tf_op jit(solution)/shard_map/ppermute | solution.py:293
  45.8 2.7 %stage.1 = (bf16[2,512,512]{2,1,0:T(8,128)(2,1)S(1)}, bf16[128,512]{1,0:T(8,128)(2,1)S(1)}, bf16[2,512,512]{2,1,0:T(8,128)(2,1)}) custom-call(bf16[128,512]{1,0:T(8,128)(2,1)} %query_ref.3, bf16[512,4096]{1,0:T(8,128)(2,1)} %weight_ref.5, bf16[2,512,128]{2,1,0:T(8,128)(2,1)} %convolve.1.after_ref.refs_1_), custom_call_target="tpu_custom_call" | custom-call | tf_op jit(solution)/shard_map/stage/pallas_call | solution.py:339
  48.5 0.0 collective-permute-done.2.rest_2_
  48.5 0.0 collective-permute-done.3.rest_3_
  48.5 5.4 %all-to-all-done.1 = bf16[128,8,128]{2,1,0:T(8,128)(2,1)S(1)} async-done(((bf16[128,8,128]{2,1,0:T(8,128)(2,1)}), bf16[128,8,128]{2,1,0:T(8,128)(2,1)S(1)}, u32[]{:S(2)}, u32[]{:S(2)}) %all-to-all-start.1) | async-done | bytes 262176 | tf_op jit(solution)/shard_map/all_to_all | solution.py:352
  54.0 0.0 copy-start
  54.0 0.6 gate.1
  54.6 5.3 %collective-permute-start.4 = (bf16[128,512]{1,0:T(8,128)(2,1)S(1)}, bf16[128,512]{1,0:T(8,128)(2,1)S(1)}, u32[]{:S(2)}, u32[]{:S(2)}) collective-permute-start(bf16[128,512]{1,0:T(8,128)(2,1)S(1)} %get-tuple-element.22), channel_id=1, source_target_pairs={{0,6},{1,3},{2,0},{3,5},{4,2},{5,7},{6,4},{7,1},{8,14},{9,11},{10,... | collective-permute-start | bytes 393224 | tf_op jit(solution)/shard_map/ppermute | solution.py:377
  59.8 4.1 %collective-permute-start.5 = (bf16[128,512]{1,0:T(8,128)(2,1)S(1)}, bf16[128,512]{1,0:T(8,128)(2,1)S(1)}, u32[]{:S(2)}, u32[]{:S(2)}) collective-permute-start(bf16[128,512]{1,0:T(8,128)(2,1)S(1)} %get-tuple-element.23), channel_id=1, source_target_pairs={{0,5},{1,4},{2,7},{3,6},{4,1},{5,0},{6,3},{7,2},{8,13},{9,12},{10,... | collective-permute-start | bytes 393224 | tf_op jit(solution)/shard_map/ppermute | solution.py:377
  63.9 0.0 copy-done
  63.9 0.4 near.1
  64.3 1.9 %collective-permute-start.6 = (bf16[128,512]{1,0:T(8,128)(2,1)S(1)}, bf16[128,512]{1,0:T(8,128)(2,1)S(1)}, u32[]{:S(2)}, u32[]{:S(2)}) collective-permute-start(bf16[128,512]{1,0:T(8,128)(2,1)S(1)} %get-tuple-element.26), channel_id=1, source_target_pairs={{0,7},{1,2},{2,1},{3,4},{4,3},{5,6},{6,5},{7,0},{8,15},{9,10},{10,... | collective-permute-start | bytes 393224 | tf_op jit(solution)/shard_map/ppermute | solution.py:377
  66.2 2.7 %collective-permute-start.7 = (bf16[128,512]{1,0:T(8,128)(2,1)S(1)}, bf16[128,512]{1,0:T(8,128)(2,1)S(1)}, u32[]{:S(2)}, u32[]{:S(2)}) collective-permute-start(bf16[128,512]{1,0:T(8,128)(2,1)S(1)} %get-tuple-element.27), channel_id=1, source_target_pairs={{0,1},{1,0},{2,3},{3,2},{4,5},{5,4},{6,7},{7,6},{8,9},{9,8},{10,11... | collective-permute-start | bytes 393224 | tf_op jit(solution)/shard_map/ppermute | solution.py:378
  68.9 1.7 %keep.1 = (bf16[128,512]{1,0:T(8,128)(2,1)}, f32[128,512]{1,0:T(8,128)S(1)}) custom-call(bf16[128,512]{1,0:T(8,128)(2,1)S(1)} %get-tuple-element.19.own_ref, bf16[512,4096]{1,0:T(8,128)(2,1)} %weight_ref.5), custom_call_target="tpu_custom_call" | custom-call | tf_op jit(solution)/shard_map/keep/pallas_call | solution.py:367
  70.7 0.0 collective-permute-done.4.refs_1_
  70.7 0.0 collective-permute-done.5.refs_2_
  70.7 1.8 %collective-permute-done.6.refs_3_ = bf16[128,512]{1,0:T(8,128)(2,1)S(1)} collective-permute-done((bf16[128,512]{1,0:T(8,128)(2,1)S(1)}, bf16[128,512]{1,0:T(8,128)(2,1)S(1)}, u32[]{:S(2)}, u32[]{:S(2)}) %collective-permute-start.6) | collective-permute-done | bytes 131104 | tf_op jit(solution)/shard_map/ppermute | solution.py:377
  72.5 0.3 collective-permute-done.7.refs_4_
  72.8 0.7 sum.1
  (2 shorter events, 0.0 us)
Async XLA Ops:
  0.6 30.2 %copy-start.6 = (bf16[64,384]{1,0:T(8,128)(2,1)S(1)}, bf16[64,384]{1,0:T(8,128)(2,1)}, u32[]{:S(2)}) copy-start(bf16[64,384]{1,0:T(8,128)(2,1)} %constant.23.clone.last_ref) | copy-start | bytes 147460
  0.6 30.2 %copy-start.1 = (bf16[256,256]{1,0:T(8,128)(2,1)S(1)}, bf16[256,256]{1,0:T(8,128)(2,1)}, u32[]{:S(2)}) copy-start(bf16[256,256]{1,0:T(8,128)(2,1)} %constant.22.clone.back_low) | copy-start | bytes 393220
  0.7 30.2 %copy-start.2 = (bf16[256,256]{1,0:T(8,128)(2,1)S(1)}, bf16[256,256]{1,0:T(8,128)(2,1)}, u32[]{:S(2)}) copy-start(bf16[256,256]{1,0:T(8,128)(2,1)} %constant.21.clone.back_high) | copy-start | bytes 393220
  0.7 30.2 %copy-start.3 = (bf16[256,256]{1,0:T(8,128)(2,1)S(1)}, bf16[256,256]{1,0:T(8,128)(2,1)}, u32[]{:S(2)}) copy-start(bf16[256,256]{1,0:T(8,128)(2,1)} %constant.20.clone.second_low) | copy-start | bytes 393220
  0.7 30.1 %copy-start.4 = (bf16[256,256]{1,0:T(8,128)(2,1)S(1)}, bf16[256,256]{1,0:T(8,128)(2,1)}, u32[]{:S(2)}) copy-start(bf16[256,256]{1,0:T(8,128)(2,1)} %constant.19.clone.second_high) | copy-start | bytes 393220
  0.7 30.1 %copy-start.7 = (f32[64,128]{1,0:T(8,128)S(1)}, f32[64,128]{1,0:T(8,128)}, u32[]{:S(2)}) copy-start(f32[64,128]{1,0:T(8,128)} %constant.18.clone.sin_ref) | copy-start | bytes 98308
  0.7 30.1 %copy-start.8 = (f32[64,128]{1,0:T(8,128)S(1)}, f32[64,128]{1,0:T(8,128)}, u32[]{:S(2)}) copy-start(f32[64,128]{1,0:T(8,128)} %constant.17.clone.cos_ref) | copy-start | bytes 98308
  0.7 30.1 %copy-start.5 = (bf16[128,192]{1,0:T(8,128)(2,1)S(1)}, bf16[128,192]{1,0:T(8,128)(2,1)}, u32[]{:S(2)}) copy-start(bf16[128,192]{1,0:T(8,128)(2,1)} %constant.16.clone.first_ref) | copy-start | bytes 147460
  0.7 30.1 %copy-start.9 = (f32[512]{0:T(512)S(1)}, f32[512]{0:T(512)}, u32[]{:S(2)}) copy-start(f32[512]{0:T(512)} %skip.1) | copy-start | bytes 6148
  2.8 28.0 %all-to-all-start = ((bf16[64,16,128]{2,1,0:T(8,128)(2,1)}), bf16[64,16,128]{2,1,0:T(8,128)(2,1)S(1)}, u32[]{:S(2)}, u32[]{:S(2)}) async-start(bf16[64,16,128]{2,1,0:T(8,128)(2,1)} %bitcast), calls=%async_computation | async-start | bytes 524288 | tf_op jit(solution)/shard_map/all_to_all | solution.py:317
  18.9 21.5 %collective-permute-start = (bf16[448,512]{1,0:T(8,128)(2,1)S(1)}, bf16[448,512]{1,0:T(8,128)(2,1)S(1)}, u32[]{:S(2)}, u32[]{:S(2)}) collective-permute-start(bf16[448,512]{1,0:T(8,128)(2,1)S(1)} %get-tuple-element.17), channel_id=1, source_target_pairs={{0,1},{1,0},{2,3},{3,2},{4,5},{5,4},{6,7},{7,6},{8,9},{9,8},{10,11... | collective-permute-start | bytes 1376264 | tf_op jit(solution)/shard_map/ppermute | solution.py:329
  22.1 21.1 %collective-permute-start.1 = (bf16[448,512]{1,0:T(8,128)(2,1)S(1)}, bf16[448,512]{1,0:T(8,128)(2,1)S(1)}, u32[]{:S(2)}, u32[]{:S(2)}) collective-permute-start(bf16[448,512]{1,0:T(8,128)(2,1)S(1)} %get-tuple-element.18), channel_id=1, source_target_pairs={{0,1},{1,0},{2,3},{3,2},{4,5},{5,4},{6,7},{7,6},{8,9},{9,8},{10,11... | collective-permute-start | bytes 1376264 | tf_op jit(solution)/shard_map/ppermute | solution.py:329
  33.9 20.1 %all-to-all-start.1 = ((bf16[128,8,128]{2,1,0:T(8,128)(2,1)}), bf16[128,8,128]{2,1,0:T(8,128)(2,1)S(1)}, u32[]{:S(2)}, u32[]{:S(2)}) async-start(bf16[128,8,128]{2,1,0:T(8,128)(2,1)} %bitcast.2), calls=%async_computation.1 | async-start | bytes 524288 | tf_op jit(solution)/shard_map/all_to_all | solution.py:352
  40.4 8.1 %collective-permute-start.2 = (bf16[448,512]{1,0:T(8,128)(2,1)S(1)}, bf16[448,512]{1,0:T(8,128)(2,1)S(1)}, u32[]{:S(2)}, u32[]{:S(2)}) collective-permute-start(bf16[448,512]{1,0:T(8,128)(2,1)S(1)} %hold.2.rest_0_), channel_id=1, source_target_pairs={{0,8},{8,0},{1,9},{9,1},{2,10},{10,2},{3,11},{11,3},{4,12},{12,4},... | collective-permute-start | bytes 1376264 | tf_op jit(solution)/shard_map/ppermute | solution.py:293
  43.3 5.3 %collective-permute-start.3 = (bf16[448,512]{1,0:T(8,128)(2,1)S(1)}, bf16[448,512]{1,0:T(8,128)(2,1)S(1)}, u32[]{:S(2)}, u32[]{:S(2)}) collective-permute-start(bf16[448,512]{1,0:T(8,128)(2,1)S(1)} %hold.3.rest_1_), channel_id=1, source_target_pairs={{0,8},{8,0},{1,9},{9,1},{2,10},{10,2},{3,11},{11,3},{4,12},{12,4},... | collective-permute-start | bytes 1376264 | tf_op jit(solution)/shard_map/ppermute | solution.py:293
  54.0 9.9 %copy-start = (bf16[2,512,512]{2,1,0:T(8,128)(2,1)S(1)}, bf16[2,512,512]{2,1,0:T(8,128)(2,1)}, u32[]{:S(2)}) copy-start(bf16[2,512,512]{2,1,0:T(8,128)(2,1)} %get-tuple-element.25.late_ref) | copy-start | bytes 3145732
  54.6 16.1 %collective-permute-start.4 = (bf16[128,512]{1,0:T(8,128)(2,1)S(1)}, bf16[128,512]{1,0:T(8,128)(2,1)S(1)}, u32[]{:S(2)}, u32[]{:S(2)}) collective-permute-start(bf16[128,512]{1,0:T(8,128)(2,1)S(1)} %get-tuple-element.22), channel_id=1, source_target_pairs={{0,6},{1,3},{2,0},{3,5},{4,2},{5,7},{6,4},{7,1},{8,14},{9,11},{10,... | collective-permute-start | bytes 393224 | tf_op jit(solution)/shard_map/ppermute | solution.py:377
  59.8 10.9 %collective-permute-start.5 = (bf16[128,512]{1,0:T(8,128)(2,1)S(1)}, bf16[128,512]{1,0:T(8,128)(2,1)S(1)}, u32[]{:S(2)}, u32[]{:S(2)}) collective-permute-start(bf16[128,512]{1,0:T(8,128)(2,1)S(1)} %get-tuple-element.23), channel_id=1, source_target_pairs={{0,5},{1,4},{2,7},{3,6},{4,1},{5,0},{6,3},{7,2},{8,13},{9,12},{10,... | collective-permute-start | bytes 393224 | tf_op jit(solution)/shard_map/ppermute | solution.py:377
  64.3 8.2 %collective-permute-start.6 = (bf16[128,512]{1,0:T(8,128)(2,1)S(1)}, bf16[128,512]{1,0:T(8,128)(2,1)S(1)}, u32[]{:S(2)}, u32[]{:S(2)}) collective-permute-start(bf16[128,512]{1,0:T(8,128)(2,1)S(1)} %get-tuple-element.26), channel_id=1, source_target_pairs={{0,7},{1,2},{2,1},{3,4},{4,3},{5,6},{6,5},{7,0},{8,15},{9,10},{10,... | collective-permute-start | bytes 393224 | tf_op jit(solution)/shard_map/ppermute | solution.py:377
  66.2 6.5 %collective-permute-start.7 = (bf16[128,512]{1,0:T(8,128)(2,1)S(1)}, bf16[128,512]{1,0:T(8,128)(2,1)S(1)}, u32[]{:S(2)}, u32[]{:S(2)}) collective-permute-start(bf16[128,512]{1,0:T(8,128)(2,1)S(1)} %get-tuple-element.27), channel_id=1, source_target_pairs={{0,1},{1,0},{2,3},{3,2},{4,5},{5,4},{6,7},{7,6},{8,9},{9,8},{10,11... | collective-permute-start | bytes 393224 | tf_op jit(solution)/shard_map/ppermute | solution.py:378

commit v5 on v4

--- a/solution.py
+++ b/solution.py
@@ -23,17 +23,19 @@
     return pieces
 
 
-def transform_tables(outer, inner):
+def transform_tables(order, inner):
+    outer = len(order)
     length = outer * inner
     row = np.arange(outer, dtype=np.float64)
+    block = np.asarray(order, np.float64)
     lane = np.arange(inner, dtype=np.float64)
-    angle = 2.0 * np.pi * np.outer(row + 0.25, row) / outer
+    angle = 2.0 * np.pi * np.outer(row + 0.25, block) / outer
     first = np.concatenate([np.cos(angle), -np.sin(angle)], axis=0)
     twist = 2.0 * np.pi * np.outer(row + 0.25, lane) / length
     angle = 2.0 * np.pi * np.outer(lane, lane) / inner
     cos, sin = np.cos(angle), np.sin(angle)
     second = np.block([[cos, -sin], [sin, cos]])
-    angle = 2.0 * np.pi * np.outer(row, row + 0.25) / outer
+    angle = 2.0 * np.pi * np.outer(block, row + 0.25) / outer
     last = np.concatenate([np.cos(angle), -np.sin(angle)], axis=1) / length
     first_parts = np.concatenate(split(first, 3), axis=1)
     second_parts = split(second, 2)
@@ -62,10 +64,22 @@
 
 
 PAIR = 2
+FIRST = (6, 2)
 
 
 def served(plane, step, planes):
     return lax.rem(plane + planes + step * (PAIR * lax.rem(plane, PAIR) - 1), planes)
+
+
+def ranked():
+    z, x, core = np.meshgrid(np.arange(8), np.arange(4), np.arange(2), indexing="ij")
+    return [int(i) for i in (((z + FIRST[0]) % 8 * 4 + (x + FIRST[1]) % 4) * 2 + core).reshape(-1)]
+
+
+def rank():
+    zx = lax.axis_index("zx")
+    z, x = lax.rem(zx // 4 + 8 - FIRST[0], 8), lax.rem(lax.rem(zx, 4) + 4 - FIRST[1], 4)
+    return (z * 4 + x) * 2 + lax.axis_index("core")
 
 
 def place():
@@ -143,7 +157,7 @@
         columns.append(jnp.concatenate([re * cos - im * sin, re * sin + im * cos], axis=0))
     high, low = halves(jnp.concatenate(columns, axis=1))
     result = dot(last_ref[...], jnp.concatenate([high, high, low], axis=0))
-    base = (lax.axis_index("zx") * 2 + lax.axis_index("core")) * group
+    base = rank() * group
     for i in range(group):
         summed = result[:, i * inner : (i + 1) * inner] + skip[base + i] * taken[i]
         turned[pl.ds(i, outer, stride=group), :] = summed
@@ -302,7 +316,9 @@
     rows, chans = key_branch.shape
     group = chans // seq_count
     width = out_weight.shape[1] // planes
-    tables = transform_tables(seq_count, rows)
+    order = ranked()
+    assert sorted(order) == list(range(seq_count))
+    tables = transform_tables(order, rows)
     key_branch, value_branch, query_branch, long_filter, out_weight = [
         pltpu.with_memory_space_constraint(x, pltpu.HBM)
         for x in (key_branch, value_branch, query_branch, long_filter, out_weight)
@@ -315,7 +331,12 @@
         [pltpu.VMEM((3, rows, chans), bf16), dma((3,))],
     )(key_branch, value_branch, long_filter)
     arrived = lax.all_to_all(
-        packed.reshape(seq_count, 2 * group, rows), seq, split_axis=0, concat_axis=0, tiled=True
+        packed.reshape(seq_count, 2 * group, rows),
+        seq,
+        split_axis=0,
+        concat_axis=0,
+        axis_index_groups=[order],
+        tiled=True,
     ).reshape(2 * chans, rows)
     swap = [(0, 1), (1, 0)]
     size, found = segments(steps, chans // 2, rows)
@@ -350,7 +371,12 @@
     early_weight, query = in_vmem(early_weight, query)
     pieces = in_vmem(*near, *far)
     turned = lax.all_to_all(
-        turned.reshape(PAIR * seq_count, group, rows), ("side",) + seq, split_axis=0, concat_axis=0, tiled=True
+        turned.reshape(PAIR * seq_count, group, rows),
+        ("side",) + seq,
+        split_axis=0,
+        concat_axis=0,
+        axis_index_groups=[[side * seq_count + i for side in range(PAIR) for i in order]],
+        tiled=True,
     ).reshape(PAIR, chans, rows)
     block = pltpu.VMEM((rows, width), bf16)
     gated = pltpu.VMEM((rows, chans), bf16)

time: 74.1 us -> 71.1 us (0.960)
  waiting for transfers between devices: 14.2 us -> 3.52 us
  starting transfers between devices: 46 us -> 53.6 us
    all_to_all x1, waiting for transfers between devices: 6.61 us -> 1.07 us  [shards(): lax.all_to_all(packed.reshape(seq_count, 2 * group, rows), seq, split_axi...]
    all_to_all x1, starting transfers between devices: 6.51 us -> 12 us  [shards(): lax.all_to_all(turned.reshape(PAIR * seq_count, group, rows), ('side',) +...]
    all_to_all x1, waiting for transfers between devices: 5.44 us -> 0.01 us  [shards(): lax.all_to_all(turned.reshape(PAIR * seq_count, group, rows), ('side',) +...]
    all_to_all x1, starting transfers between devices: 14.8 us -> 16.8 us  [shards(): lax.all_to_all(packed.reshape(seq_count, 2 * group, rows), seq, split_axi...]
  transfers between devices with their start and end apart: 10 -> 10, of which waited for: 4 -> 3; matrix products, arithmetic and copies ran while one was open for 0% -> 0% of each run, Pallas kernels for 12% -> 13%
where the time goes in v5:
time: 71.1 us; the launch traced here: 70.5 us
  starting transfers between devices  53.6 us (75%)
  Pallas kernels  12.4 us (17%)
  waiting for transfers between devices  3.52 us (5%)
  between operations  0.96 us (1%)
    all_to_all x1, starting transfers between devices, shards(): lax.all_to_all(packed.reshape(seq_count, 2 * group, rows), seq, split_axi...  16.8 us
    all_to_all x1, starting transfers between devices, shards(): lax.all_to_all(turned.reshape(PAIR * seq_count, group, rows), ('side',) +...  12 us
    ppermute x3, starting transfers between devices, shards(): parts.append(lax.ppermute(part, chan, pairs))  11.2 us
    ppermute x2, starting transfers between devices, permuted_after(): return (array, lax.ppermute(array, axis, pairs))  5.62 us
    ppermute x2, starting transfers between devices, shards(): near = [lax.ppermute(x, 'side', swap) for x in near]  5.28 us
    pallas_call x1, Pallas kernels, shards(): call(functools.partial(convolve_kernel, group, seq_count), 'convolve', [p...  3.03 us
    ppermute x1, starting transfers between devices, shards(): parts.append(lax.ppermute(partner, 'side', swap))  2.68 us
    pallas_call x1, Pallas kernels, shards(): call(functools.partial(stage_kernel, steps, planes), 'stage', [pltpu.VMEM...  2.67 us
  transfers between devices with their start and end apart: 10, of which 3 were waited for; matrix products, arithmetic and copies ran while one was open for 0% of the time, Pallas kernels for 13%

profile of v5, /device:TPU:1, one launch (start us, length us, event | category | flops | bytes accessed | tf_op | source)
XLA Modules:
  0.0 70.5 jit_solution(12663603132286012374)
XLA Ops:
  0.6 0.0 copy-start.6
  0.6 0.0 copy-start.1
  0.7 0.0 copy-start.2
  0.7 0.0 copy-start.3
  0.7 0.0 copy-start.4
  0.7 0.0 copy-start.7
  0.7 0.0 copy-start.8
  0.7 0.0 copy-start.5
  0.7 0.0 copy-start.9
  0.7 2.0 %pack.1.packed_ref = bf16[1024,128]{1,0:T(8,128)(2,1)} custom-call(bf16[128,512]{1,0:T(8,128)(2,1)} %key_ref.1, bf16[128,512]{1,0:T(8,128)(2,1)} %value_ref.1, bf16[128,512]{1,0:T(8,128)(2,1)} %filter_ref.1), custom_call_target="tpu_custom_call" | custom-call | tf_op jit(solution)/shard_map/pack/pallas_call | solution.py:326
  2.8 16.8 %all-to-all-start = ((bf16[64,16,128]{2,1,0:T(8,128)(2,1)}), bf16[64,16,128]{2,1,0:T(8,128)(2,1)S(1)}, u32[]{:S(2)}, u32[]{:S(2)}) async-start(bf16[64,16,128]{2,1,0:T(8,128)(2,1)} %bitcast), calls=%async_computation | async-start | bytes 524288 | tf_op jit(solution)/shard_map/all_to_all | solution.py:333
  19.6 1.2 %ship.1 = (bf16[448,512]{1,0:T(8,128)(2,1)S(1)}, bf16[448,512]{1,0:T(8,128)(2,1)S(1)}) custom-call(bf16[128,512]{1,0:T(8,128)(2,1)} %query_ref.3, bf16[512,4096]{1,0:T(8,128)(2,1)} %weight_ref.5, bf16[1024,128]{1,0:T(8,128)(2,1)} %pack.1.packed_ref), custom_call_target="tpu_custom_call" | custom-call | tf_op jit(solution)/shard_map/ship/pallas_call | solution.py:343
  20.9 3.2 %collective-permute-start = (bf16[448,512]{1,0:T(8,128)(2,1)S(1)}, bf16[448,512]{1,0:T(8,128)(2,1)S(1)}, u32[]{:S(2)}, u32[]{:S(2)}) collective-permute-start(bf16[448,512]{1,0:T(8,128)(2,1)S(1)} %get-tuple-element.17), channel_id=1, source_target_pairs={{0,1},{1,0},{2,3},{3,2},{4,5},{5,4},{6,7},{7,6},{8,9},{9,8},{10,11... | collective-permute-start | bytes 1376264 | tf_op jit(solution)/shard_map/ppermute | solution.py:350
  24.1 2.1 %collective-permute-start.1 = (bf16[448,512]{1,0:T(8,128)(2,1)S(1)}, bf16[448,512]{1,0:T(8,128)(2,1)S(1)}, u32[]{:S(2)}, u32[]{:S(2)}) collective-permute-start(bf16[448,512]{1,0:T(8,128)(2,1)S(1)} %get-tuple-element.18), channel_id=1, source_target_pairs={{0,1},{1,0},{2,3},{3,2},{4,5},{5,4},{6,7},{7,6},{8,9},{9,8},{10,11... | collective-permute-start | bytes 1376264 | tf_op jit(solution)/shard_map/ppermute | solution.py:350
  26.2 1.1 %all-to-all-done = bf16[64,16,128]{2,1,0:T(8,128)(2,1)S(1)} async-done(((bf16[64,16,128]{2,1,0:T(8,128)(2,1)}), bf16[64,16,128]{2,1,0:T(8,128)(2,1)S(1)}, u32[]{:S(2)}, u32[]{:S(2)}) %all-to-all-start) | async-done | bytes 262176 | tf_op jit(solution)/shard_map/all_to_all | solution.py:333
  27.2 0.0 copy-done.6
  27.2 0.0 copy-done.1
  27.2 0.0 copy-done.2
  27.3 0.0 copy-done.3
  27.3 0.0 copy-done.4
  27.3 0.0 copy-done.7
  27.3 0.0 copy-done.8
  27.3 0.0 copy-done.5
  27.3 0.0 copy-done.9
  27.3 3.0 %convolve.1.after_ref.refs_1_ = bf16[2,512,128]{2,1,0:T(8,128)(2,1)} custom-call(f32[512]{0:T(512)S(1)} %copy-done.9, bf16[1024,128]{1,0:T(8,128)(2,1)S(1)} %bitcast.4, bf16[128,192]{1,0:T(8,128)(2,1)S(1)} %copy-done.5, f32[64,128]{1,0:T(8,128)S(1)} %copy-done.8, f32[64,128]{1,0:T(8,128)S(1)} %copy-done.7, bf16[256,256]{1,0:T(8,128)(2,1)S(1)} %copy-done.4, ...), custom_call_target="tpu_custom_call" | custom-call | tf_op jit(solution)/shard_map/convolve/pallas_call | solution.py:351
  30.3 12.0 %all-to-all-start.1 = ((bf16[128,8,128]{2,1,0:T(8,128)(2,1)}), bf16[128,8,128]{2,1,0:T(8,128)(2,1)S(1)}, u32[]{:S(2)}, u32[]{:S(2)}) async-start(bf16[128,8,128]{2,1,0:T(8,128)(2,1)} %bitcast.2), calls=%async_computation.1 | async-start | bytes 524288 | tf_op jit(solution)/shard_map/all_to_all | solution.py:373
  42.3 0.0 collective-permute-done.refs_0_
  42.3 2.3 %collective-permute-start.2 = (bf16[448,512]{1,0:T(8,128)(2,1)S(1)}, bf16[448,512]{1,0:T(8,128)(2,1)S(1)}, u32[]{:S(2)}, u32[]{:S(2)}) collective-permute-start(bf16[448,512]{1,0:T(8,128)(2,1)S(1)} %hold.2.rest_0_), channel_id=1, source_target_pairs={{0,8},{8,0},{1,9},{9,1},{2,10},{10,2},{3,11},{11,3},{4,12},{12,4},... | collective-permute-start | bytes 1376264 | tf_op jit(solution)/shard_map/ppermute | solution.py:307
  44.6 0.0 collective-permute-done.1.refs_0_
  44.6 3.4 %collective-permute-start.3 = (bf16[448,512]{1,0:T(8,128)(2,1)S(1)}, bf16[448,512]{1,0:T(8,128)(2,1)S(1)}, u32[]{:S(2)}, u32[]{:S(2)}) collective-permute-start(bf16[448,512]{1,0:T(8,128)(2,1)S(1)} %hold.3.rest_1_), channel_id=1, source_target_pairs={{0,8},{8,0},{1,9},{9,1},{2,10},{10,2},{3,11},{11,3},{4,12},{12,4},... | collective-permute-start | bytes 1376264 | tf_op jit(solution)/shard_map/ppermute | solution.py:307
  48.0 2.7 %stage.1 = (bf16[2,512,512]{2,1,0:T(8,128)(2,1)S(1)}, bf16[128,512]{1,0:T(8,128)(2,1)S(1)}, bf16[2,512,512]{2,1,0:T(8,128)(2,1)}) custom-call(bf16[128,512]{1,0:T(8,128)(2,1)} %query_ref.3, bf16[512,4096]{1,0:T(8,128)(2,1)} %weight_ref.5, bf16[2,512,128]{2,1,0:T(8,128)(2,1)} %convolve.1.after_ref.refs_1_), custom_call_target="tpu_custom_call" | custom-call | tf_op jit(solution)/shard_map/stage/pallas_call | solution.py:360
  50.7 0.0 collective-permute-done.2.rest_2_
  50.7 0.0 collective-permute-done.3.rest_3_
  50.7 0.0 all-to-all-done.1
  50.7 0.0 copy-start
  50.7 0.6 gate.1
  51.3 6.1 %collective-permute-start.4 = (bf16[128,512]{1,0:T(8,128)(2,1)S(1)}, bf16[128,512]{1,0:T(8,128)(2,1)S(1)}, u32[]{:S(2)}, u32[]{:S(2)}) collective-permute-start(bf16[128,512]{1,0:T(8,128)(2,1)S(1)} %get-tuple-element.22), channel_id=1, source_target_pairs={{0,6},{1,3},{2,0},{3,5},{4,2},{5,7},{6,4},{7,1},{8,14},{9,11},{10,... | collective-permute-start | bytes 393224 | tf_op jit(solution)/shard_map/ppermute | solution.py:403
  57.4 3.2 %collective-permute-start.5 = (bf16[128,512]{1,0:T(8,128)(2,1)S(1)}, bf16[128,512]{1,0:T(8,128)(2,1)S(1)}, u32[]{:S(2)}, u32[]{:S(2)}) collective-permute-start(bf16[128,512]{1,0:T(8,128)(2,1)S(1)} %get-tuple-element.23), channel_id=1, source_target_pairs={{0,5},{1,4},{2,7},{3,6},{4,1},{5,0},{6,3},{7,2},{8,13},{9,12},{10,... | collective-permute-start | bytes 393224 | tf_op jit(solution)/shard_map/ppermute | solution.py:403
  60.6 0.0 copy-done
  60.6 0.4 near.1
  61.0 1.9 %collective-permute-start.6 = (bf16[128,512]{1,0:T(8,128)(2,1)S(1)}, bf16[128,512]{1,0:T(8,128)(2,1)S(1)}, u32[]{:S(2)}, u32[]{:S(2)}) collective-permute-start(bf16[128,512]{1,0:T(8,128)(2,1)S(1)} %get-tuple-element.26), channel_id=1, source_target_pairs={{0,7},{1,2},{2,1},{3,4},{4,3},{5,6},{6,5},{7,0},{8,15},{9,10},{10,... | collective-permute-start | bytes 393224 | tf_op jit(solution)/shard_map/ppermute | solution.py:403
  62.9 2.7 %collective-permute-start.7 = (bf16[128,512]{1,0:T(8,128)(2,1)S(1)}, bf16[128,512]{1,0:T(8,128)(2,1)S(1)}, u32[]{:S(2)}, u32[]{:S(2)}) collective-permute-start(bf16[128,512]{1,0:T(8,128)(2,1)S(1)} %get-tuple-element.27), channel_id=1, source_target_pairs={{0,1},{1,0},{2,3},{3,2},{4,5},{5,4},{6,7},{7,6},{8,9},{9,8},{10,11... | collective-permute-start | bytes 393224 | tf_op jit(solution)/shard_map/ppermute | solution.py:404
  65.6 1.7 %keep.1 = (bf16[128,512]{1,0:T(8,128)(2,1)}, f32[128,512]{1,0:T(8,128)S(1)}) custom-call(bf16[128,512]{1,0:T(8,128)(2,1)S(1)} %get-tuple-element.19.own_ref, bf16[512,4096]{1,0:T(8,128)(2,1)} %weight_ref.5), custom_call_target="tpu_custom_call" | custom-call | tf_op jit(solution)/shard_map/keep/pallas_call | solution.py:393
  67.4 0.0 collective-permute-done.4.refs_1_
  67.4 2.0 %collective-permute-done.5.refs_2_ = bf16[128,512]{1,0:T(8,128)(2,1)S(1)} collective-permute-done((bf16[128,512]{1,0:T(8,128)(2,1)S(1)}, bf16[128,512]{1,0:T(8,128)(2,1)S(1)}, u32[]{:S(2)}, u32[]{:S(2)}) %collective-permute-start.5) | collective-permute-done | bytes 131104 | tf_op jit(solution)/shard_map/ppermute | solution.py:403
  69.4 0.0 collective-permute-done.6.refs_3_
  69.4 0.4 collective-permute-done.7.refs_4_
  69.8 0.7 %sum.1 = bf16[128,512]{1,0:T(8,128)(2,1)} custom-call(f32[128,512]{1,0:T(8,128)S(1)} %get-tuple-element.21.refs_0_, bf16[128,512]{1,0:T(8,128)(2,1)S(1)} %collective-permute-done.4.refs_1_, bf16[128,512]{1,0:T(8,128)(2,1)S(1)} %collective-permute-done.5.refs_2_, bf16[128,512]{1,0:T(8,128)(2,1)S(1)} %collective-permute-done.6.refs_3_, ...), custom_call_target="tpu_custom_call" | custom-call | tf_op jit(solution)/shard_map/sum/pallas_call | solution.py:405
  (2 shorter events, 0.0 us)
Async XLA Ops:
  0.6 26.6 %copy-start.6 = (bf16[64,384]{1,0:T(8,128)(2,1)S(1)}, bf16[64,384]{1,0:T(8,128)(2,1)}, u32[]{:S(2)}) copy-start(bf16[64,384]{1,0:T(8,128)(2,1)} %constant.23.clone.last_ref) | copy-start | bytes 147460
  0.6 26.6 %copy-start.1 = (bf16[256,256]{1,0:T(8,128)(2,1)S(1)}, bf16[256,256]{1,0:T(8,128)(2,1)}, u32[]{:S(2)}) copy-start(bf16[256,256]{1,0:T(8,128)(2,1)} %constant.22.clone.back_low) | copy-start | bytes 393220
  0.7 26.6 %copy-start.2 = (bf16[256,256]{1,0:T(8,128)(2,1)S(1)}, bf16[256,256]{1,0:T(8,128)(2,1)}, u32[]{:S(2)}) copy-start(bf16[256,256]{1,0:T(8,128)(2,1)} %constant.21.clone.back_high) | copy-start | bytes 393220
  0.7 26.6 %copy-start.3 = (bf16[256,256]{1,0:T(8,128)(2,1)S(1)}, bf16[256,256]{1,0:T(8,128)(2,1)}, u32[]{:S(2)}) copy-start(bf16[256,256]{1,0:T(8,128)(2,1)} %constant.20.clone.second_low) | copy-start | bytes 393220
  0.7 26.6 %copy-start.4 = (bf16[256,256]{1,0:T(8,128)(2,1)S(1)}, bf16[256,256]{1,0:T(8,128)(2,1)}, u32[]{:S(2)}) copy-start(bf16[256,256]{1,0:T(8,128)(2,1)} %constant.19.clone.second_high) | copy-start | bytes 393220
  0.7 26.6 %copy-start.7 = (f32[64,128]{1,0:T(8,128)S(1)}, f32[64,128]{1,0:T(8,128)}, u32[]{:S(2)}) copy-start(f32[64,128]{1,0:T(8,128)} %constant.18.clone.sin_ref) | copy-start | bytes 98308
  0.7 26.6 %copy-start.8 = (f32[64,128]{1,0:T(8,128)S(1)}, f32[64,128]{1,0:T(8,128)}, u32[]{:S(2)}) copy-start(f32[64,128]{1,0:T(8,128)} %constant.17.clone.cos_ref) | copy-start | bytes 98308
  0.7 26.6 %copy-start.5 = (bf16[128,192]{1,0:T(8,128)(2,1)S(1)}, bf16[128,192]{1,0:T(8,128)(2,1)}, u32[]{:S(2)}) copy-start(bf16[128,192]{1,0:T(8,128)(2,1)} %constant.16.clone.first_ref) | copy-start | bytes 147460
  0.7 26.6 %copy-start.9 = (f32[512]{0:T(512)S(1)}, f32[512]{0:T(512)}, u32[]{:S(2)}) copy-start(f32[512]{0:T(512)} %skip.1) | copy-start | bytes 6148
  2.8 24.4 %all-to-all-start = ((bf16[64,16,128]{2,1,0:T(8,128)(2,1)}), bf16[64,16,128]{2,1,0:T(8,128)(2,1)S(1)}, u32[]{:S(2)}, u32[]{:S(2)}) async-start(bf16[64,16,128]{2,1,0:T(8,128)(2,1)} %bitcast), calls=%async_computation | async-start | bytes 524288 | tf_op jit(solution)/shard_map/all_to_all | solution.py:333
  20.9 21.4 %collective-permute-start = (bf16[448,512]{1,0:T(8,128)(2,1)S(1)}, bf16[448,512]{1,0:T(8,128)(2,1)S(1)}, u32[]{:S(2)}, u32[]{:S(2)}) collective-permute-start(bf16[448,512]{1,0:T(8,128)(2,1)S(1)} %get-tuple-element.17), channel_id=1, source_target_pairs={{0,1},{1,0},{2,3},{3,2},{4,5},{5,4},{6,7},{7,6},{8,9},{9,8},{10,11... | collective-permute-start | bytes 1376264 | tf_op jit(solution)/shard_map/ppermute | solution.py:350
  24.1 20.5 %collective-permute-start.1 = (bf16[448,512]{1,0:T(8,128)(2,1)S(1)}, bf16[448,512]{1,0:T(8,128)(2,1)S(1)}, u32[]{:S(2)}, u32[]{:S(2)}) collective-permute-start(bf16[448,512]{1,0:T(8,128)(2,1)S(1)} %get-tuple-element.18), channel_id=1, source_target_pairs={{0,1},{1,0},{2,3},{3,2},{4,5},{5,4},{6,7},{7,6},{8,9},{9,8},{10,11... | collective-permute-start | bytes 1376264 | tf_op jit(solution)/shard_map/ppermute | solution.py:350
  30.3 20.4 %all-to-all-start.1 = ((bf16[128,8,128]{2,1,0:T(8,128)(2,1)}), bf16[128,8,128]{2,1,0:T(8,128)(2,1)S(1)}, u32[]{:S(2)}, u32[]{:S(2)}) async-start(bf16[128,8,128]{2,1,0:T(8,128)(2,1)} %bitcast.2), calls=%async_computation.1 | async-start | bytes 524288 | tf_op jit(solution)/shard_map/all_to_all | solution.py:373
  42.3 8.3 %collective-permute-start.2 = (bf16[448,512]{1,0:T(8,128)(2,1)S(1)}, bf16[448,512]{1,0:T(8,128)(2,1)S(1)}, u32[]{:S(2)}, u32[]{:S(2)}) collective-permute-start(bf16[448,512]{1,0:T(8,128)(2,1)S(1)} %hold.2.rest_0_), channel_id=1, source_target_pairs={{0,8},{8,0},{1,9},{9,1},{2,10},{10,2},{3,11},{11,3},{4,12},{12,4},... | collective-permute-start | bytes 1376264 | tf_op jit(solution)/shard_map/ppermute | solution.py:307
  44.6 6.0 %collective-permute-start.3 = (bf16[448,512]{1,0:T(8,128)(2,1)S(1)}, bf16[448,512]{1,0:T(8,128)(2,1)S(1)}, u32[]{:S(2)}, u32[]{:S(2)}) collective-permute-start(bf16[448,512]{1,0:T(8,128)(2,1)S(1)} %hold.3.rest_1_), channel_id=1, source_target_pairs={{0,8},{8,0},{1,9},{9,1},{2,10},{10,2},{3,11},{11,3},{4,12},{12,4},... | collective-permute-start | bytes 1376264 | tf_op jit(solution)/shard_map/ppermute | solution.py:307
  50.7 9.9 %copy-start = (bf16[2,512,512]{2,1,0:T(8,128)(2,1)S(1)}, bf16[2,512,512]{2,1,0:T(8,128)(2,1)}, u32[]{:S(2)}) copy-start(bf16[2,512,512]{2,1,0:T(8,128)(2,1)} %get-tuple-element.25.late_ref) | copy-start | bytes 3145732
  51.3 16.1 %collective-permute-start.4 = (bf16[128,512]{1,0:T(8,128)(2,1)S(1)}, bf16[128,512]{1,0:T(8,128)(2,1)S(1)}, u32[]{:S(2)}, u32[]{:S(2)}) collective-permute-start(bf16[128,512]{1,0:T(8,128)(2,1)S(1)} %get-tuple-element.22), channel_id=1, source_target_pairs={{0,6},{1,3},{2,0},{3,5},{4,2},{5,7},{6,4},{7,1},{8,14},{9,11},{10,... | collective-permute-start | bytes 393224 | tf_op jit(solution)/shard_map/ppermute | solution.py:403
  57.4 12.0 %collective-permute-start.5 = (bf16[128,512]{1,0:T(8,128)(2,1)S(1)}, bf16[128,512]{1,0:T(8,128)(2,1)S(1)}, u32[]{:S(2)}, u32[]{:S(2)}) collective-permute-start(bf16[128,512]{1,0:T(8,128)(2,1)S(1)} %get-tuple-element.23), channel_id=1, source_target_pairs={{0,5},{1,4},{2,7},{3,6},{4,1},{5,0},{6,3},{7,2},{8,13},{9,12},{10,... | collective-permute-start | bytes 393224 | tf_op jit(solution)/shard_map/ppermute | solution.py:403
  61.0 8.4 %collective-permute-start.6 = (bf16[128,512]{1,0:T(8,128)(2,1)S(1)}, bf16[128,512]{1,0:T(8,128)(2,1)S(1)}, u32[]{:S(2)}, u32[]{:S(2)}) collective-permute-start(bf16[128,512]{1,0:T(8,128)(2,1)S(1)} %get-tuple-element.26), channel_id=1, source_target_pairs={{0,7},{1,2},{2,1},{3,4},{4,3},{5,6},{6,5},{7,0},{8,15},{9,10},{10,... | collective-permute-start | bytes 393224 | tf_op jit(solution)/shard_map/ppermute | solution.py:403
  62.9 6.9 %collective-permute-start.7 = (bf16[128,512]{1,0:T(8,128)(2,1)S(1)}, bf16[128,512]{1,0:T(8,128)(2,1)S(1)}, u32[]{:S(2)}, u32[]{:S(2)}) collective-permute-start(bf16[128,512]{1,0:T(8,128)(2,1)S(1)} %get-tuple-element.27), channel_id=1, source_target_pairs={{0,1},{1,0},{2,3},{3,2},{4,5},{5,4},{6,7},{7,6},{8,9},{9,8},{10,11... | collective-permute-start | bytes 393224 | tf_op jit(solution)/shard_map/ppermute | solution.py:404

commit v6 on v5

--- a/solution.py
+++ b/solution.py
@@ -64,7 +64,7 @@
 
 
 PAIR = 2
-FIRST = (6, 2)
+FIRST = (6, 3)
 
 
 def served(plane, step, planes):
@@ -73,13 +73,13 @@
 
 def ranked():
     z, x, core = np.meshgrid(np.arange(8), np.arange(4), np.arange(2), indexing="ij")
-    return [int(i) for i in (((z + FIRST[0]) % 8 * 4 + (x + FIRST[1]) % 4) * 2 + core).reshape(-1)]
+    return [int(i) for i in (((z + FIRST[0]) % 8 * 4 + (x + FIRST[1]) % 4) * 2 + 1 - core).reshape(-1)]
 
 
 def rank():
     zx = lax.axis_index("zx")
     z, x = lax.rem(zx // 4 + 8 - FIRST[0], 8), lax.rem(lax.rem(zx, 4) + 4 - FIRST[1], 4)
-    return (z * 4 + x) * 2 + lax.axis_index("core")
+    return (z * 4 + x) * 2 + 1 - lax.axis_index("core")
 
 
 def place():

time: 71.1 us -> 70.8 us (level)
  starting transfers between devices: 53.6 us -> 51.7 us
  waiting for transfers between devices: 3.52 us -> 5.11 us
    all_to_all x1, starting transfers between devices: 12 us -> 10.4 us  [shards(): lax.all_to_all(turned.reshape(PAIR * seq_count, group, rows), ('side',) +...]
    all_to_all x1, waiting for transfers between devices: 1.07 us -> 2.51 us  [shards(): lax.all_to_all(packed.reshape(seq_count, 2 * group, rows), seq, split_axi...]
where the time goes in v6:
time: 70.8 us; the launch traced here: 70.2 us
  starting transfers between devices  51.7 us (73%)
  Pallas kernels  12.4 us (18%)
  waiting for transfers between devices  5.11 us (7%)
  between operations  0.96 us (1%)
    all_to_all x1, starting transfers between devices, shards(): lax.all_to_all(packed.reshape(seq_count, 2 * group, rows), seq, split_axi...  16.2 us
    ppermute x3, starting transfers between devices, shards(): parts.append(lax.ppermute(part, chan, pairs))  11.2 us
    all_to_all x1, starting transfers between devices, shards(): lax.all_to_all(turned.reshape(PAIR * seq_count, group, rows), ('side',) +...  10.4 us
    ppermute x2, starting transfers between devices, permuted_after(): return (array, lax.ppermute(array, axis, pairs))  5.92 us
    ppermute x2, starting transfers between devices, shards(): near = [lax.ppermute(x, 'side', swap) for x in near]  5.28 us
    pallas_call x1, Pallas kernels, shards(): call(functools.partial(convolve_kernel, group, seq_count), 'convolve', [p...  3.03 us
    ppermute x1, starting transfers between devices, shards(): parts.append(lax.ppermute(partner, 'side', swap))  2.69 us
    pallas_call x1, Pallas kernels, shards(): call(functools.partial(stage_kernel, steps, planes), 'stage', [pltpu.VMEM...  2.67 us
  transfers between devices with their start and end apart: 10, of which 3 were waited for; matrix products, arithmetic and copies ran while one was open for 0% of the time, Pallas kernels for 13%

profile of v6, /device:TPU:1, one launch (start us, length us, event | category | flops | bytes accessed | tf_op | source)
XLA Modules:
  0.0 70.2 jit_solution(4135727465529138659)
XLA Ops:
  0.6 0.0 copy-start.6
  0.6 0.0 copy-start.1
  0.7 0.0 copy-start.2
  0.7 0.0 copy-start.3
  0.7 0.0 copy-start.4
  0.7 0.0 copy-start.7
  0.7 0.0 copy-start.8
  0.7 0.0 copy-start.5
  0.7 0.0 copy-start.9
  0.7 2.0 %pack.1.packed_ref = bf16[1024,128]{1,0:T(8,128)(2,1)} custom-call(bf16[128,512]{1,0:T(8,128)(2,1)} %key_ref.1, bf16[128,512]{1,0:T(8,128)(2,1)} %value_ref.1, bf16[128,512]{1,0:T(8,128)(2,1)} %filter_ref.1), custom_call_target="tpu_custom_call" | custom-call | tf_op jit(solution)/shard_map/pack/pallas_call | solution.py:326
  2.8 16.2 %all-to-all-start = ((bf16[64,16,128]{2,1,0:T(8,128)(2,1)}), bf16[64,16,128]{2,1,0:T(8,128)(2,1)S(1)}, u32[]{:S(2)}, u32[]{:S(2)}) async-start(bf16[64,16,128]{2,1,0:T(8,128)(2,1)} %bitcast), calls=%async_computation | async-start | bytes 524288 | tf_op jit(solution)/shard_map/all_to_all | solution.py:333
  19.0 1.2 %ship.1 = (bf16[448,512]{1,0:T(8,128)(2,1)S(1)}, bf16[448,512]{1,0:T(8,128)(2,1)S(1)}) custom-call(bf16[128,512]{1,0:T(8,128)(2,1)} %query_ref.3, bf16[512,4096]{1,0:T(8,128)(2,1)} %weight_ref.5, bf16[1024,128]{1,0:T(8,128)(2,1)} %pack.1.packed_ref), custom_call_target="tpu_custom_call" | custom-call | tf_op jit(solution)/shard_map/ship/pallas_call | solution.py:343
  20.3 3.2 %collective-permute-start = (bf16[448,512]{1,0:T(8,128)(2,1)S(1)}, bf16[448,512]{1,0:T(8,128)(2,1)S(1)}, u32[]{:S(2)}, u32[]{:S(2)}) collective-permute-start(bf16[448,512]{1,0:T(8,128)(2,1)S(1)} %get-tuple-element.17), channel_id=1, source_target_pairs={{0,1},{1,0},{2,3},{3,2},{4,5},{5,4},{6,7},{7,6},{8,9},{9,8},{10,11... | collective-permute-start | bytes 1376264 | tf_op jit(solution)/shard_map/ppermute | solution.py:350
  23.5 2.1 %collective-permute-start.1 = (bf16[448,512]{1,0:T(8,128)(2,1)S(1)}, bf16[448,512]{1,0:T(8,128)(2,1)S(1)}, u32[]{:S(2)}, u32[]{:S(2)}) collective-permute-start(bf16[448,512]{1,0:T(8,128)(2,1)S(1)} %get-tuple-element.18), channel_id=1, source_target_pairs={{0,1},{1,0},{2,3},{3,2},{4,5},{5,4},{6,7},{7,6},{8,9},{9,8},{10,11... | collective-permute-start | bytes 1376264 | tf_op jit(solution)/shard_map/ppermute | solution.py:350
  25.6 2.5 %all-to-all-done = bf16[64,16,128]{2,1,0:T(8,128)(2,1)S(1)} async-done(((bf16[64,16,128]{2,1,0:T(8,128)(2,1)}), bf16[64,16,128]{2,1,0:T(8,128)(2,1)S(1)}, u32[]{:S(2)}, u32[]{:S(2)}) %all-to-all-start) | async-done | bytes 262176 | tf_op jit(solution)/shard_map/all_to_all | solution.py:333
  28.1 0.0 copy-done.6
  28.1 0.0 copy-done.1
  28.1 0.0 copy-done.2
  28.1 0.0 copy-done.3
  28.1 0.0 copy-done.4
  28.1 0.0 copy-done.7
  28.1 0.0 copy-done.8
  28.1 0.0 copy-done.5
  28.1 0.0 copy-done.9
  28.1 3.0 %convolve.1.after_ref.refs_1_ = bf16[2,512,128]{2,1,0:T(8,128)(2,1)} custom-call(f32[512]{0:T(512)S(1)} %copy-done.9, bf16[1024,128]{1,0:T(8,128)(2,1)S(1)} %bitcast.4, bf16[128,192]{1,0:T(8,128)(2,1)S(1)} %copy-done.5, f32[64,128]{1,0:T(8,128)S(1)} %copy-done.8, f32[64,128]{1,0:T(8,128)S(1)} %copy-done.7, bf16[256,256]{1,0:T(8,128)(2,1)S(1)} %copy-done.4, ...), custom_call_target="tpu_custom_call" | custom-call | tf_op jit(solution)/shard_map/convolve/pallas_call | solution.py:351
  31.2 10.4 %all-to-all-start.1 = ((bf16[128,8,128]{2,1,0:T(8,128)(2,1)}), bf16[128,8,128]{2,1,0:T(8,128)(2,1)S(1)}, u32[]{:S(2)}, u32[]{:S(2)}) async-start(bf16[128,8,128]{2,1,0:T(8,128)(2,1)} %bitcast.2), calls=%async_computation.1 | async-start | bytes 524288 | tf_op jit(solution)/shard_map/all_to_all | solution.py:373
  41.6 0.0 collective-permute-done.refs_0_
  41.6 2.3 %collective-permute-start.2 = (bf16[448,512]{1,0:T(8,128)(2,1)S(1)}, bf16[448,512]{1,0:T(8,128)(2,1)S(1)}, u32[]{:S(2)}, u32[]{:S(2)}) collective-permute-start(bf16[448,512]{1,0:T(8,128)(2,1)S(1)} %hold.2.rest_0_), channel_id=1, source_target_pairs={{0,8},{8,0},{1,9},{9,1},{2,10},{10,2},{3,11},{11,3},{4,12},{12,4},... | collective-permute-start | bytes 1376264 | tf_op jit(solution)/shard_map/ppermute | solution.py:307
  43.9 0.0 collective-permute-done.1.refs_0_
  43.9 3.6 %collective-permute-start.3 = (bf16[448,512]{1,0:T(8,128)(2,1)S(1)}, bf16[448,512]{1,0:T(8,128)(2,1)S(1)}, u32[]{:S(2)}, u32[]{:S(2)}) collective-permute-start(bf16[448,512]{1,0:T(8,128)(2,1)S(1)} %hold.3.rest_1_), channel_id=1, source_target_pairs={{0,8},{8,0},{1,9},{9,1},{2,10},{10,2},{3,11},{11,3},{4,12},{12,4},... | collective-permute-start | bytes 1376264 | tf_op jit(solution)/shard_map/ppermute | solution.py:307
  47.5 2.7 %stage.1 = (bf16[2,512,512]{2,1,0:T(8,128)(2,1)S(1)}, bf16[128,512]{1,0:T(8,128)(2,1)S(1)}, bf16[2,512,512]{2,1,0:T(8,128)(2,1)}) custom-call(bf16[128,512]{1,0:T(8,128)(2,1)} %query_ref.3, bf16[512,4096]{1,0:T(8,128)(2,1)} %weight_ref.5, bf16[2,512,128]{2,1,0:T(8,128)(2,1)} %convolve.1.after_ref.refs_1_), custom_call_target="tpu_custom_call" | custom-call | tf_op jit(solution)/shard_map/stage/pallas_call | solution.py:360
  50.2 0.0 collective-permute-done.2.rest_2_
  50.2 0.0 collective-permute-done.3.rest_3_
  50.2 0.0 all-to-all-done.1
  50.2 0.0 copy-start
  50.3 0.6 gate.1
  50.8 6.0 %collective-permute-start.4 = (bf16[128,512]{1,0:T(8,128)(2,1)S(1)}, bf16[128,512]{1,0:T(8,128)(2,1)S(1)}, u32[]{:S(2)}, u32[]{:S(2)}) collective-permute-start(bf16[128,512]{1,0:T(8,128)(2,1)S(1)} %get-tuple-element.22), channel_id=1, source_target_pairs={{0,6},{1,3},{2,0},{3,5},{4,2},{5,7},{6,4},{7,1},{8,14},{9,11},{10,... | collective-permute-start | bytes 393224 | tf_op jit(solution)/shard_map/ppermute | solution.py:403
  56.9 3.2 %collective-permute-start.5 = (bf16[128,512]{1,0:T(8,128)(2,1)S(1)}, bf16[128,512]{1,0:T(8,128)(2,1)S(1)}, u32[]{:S(2)}, u32[]{:S(2)}) collective-permute-start(bf16[128,512]{1,0:T(8,128)(2,1)S(1)} %get-tuple-element.23), channel_id=1, source_target_pairs={{0,5},{1,4},{2,7},{3,6},{4,1},{5,0},{6,3},{7,2},{8,13},{9,12},{10,... | collective-permute-start | bytes 393224 | tf_op jit(solution)/shard_map/ppermute | solution.py:403
  60.1 0.0 copy-done
  60.1 0.4 near.1
  60.5 1.9 %collective-permute-start.6 = (bf16[128,512]{1,0:T(8,128)(2,1)S(1)}, bf16[128,512]{1,0:T(8,128)(2,1)S(1)}, u32[]{:S(2)}, u32[]{:S(2)}) collective-permute-start(bf16[128,512]{1,0:T(8,128)(2,1)S(1)} %get-tuple-element.26), channel_id=1, source_target_pairs={{0,7},{1,2},{2,1},{3,4},{4,3},{5,6},{6,5},{7,0},{8,15},{9,10},{10,... | collective-permute-start | bytes 393224 | tf_op jit(solution)/shard_map/ppermute | solution.py:403
  62.4 2.7 %collective-permute-start.7 = (bf16[128,512]{1,0:T(8,128)(2,1)S(1)}, bf16[128,512]{1,0:T(8,128)(2,1)S(1)}, u32[]{:S(2)}, u32[]{:S(2)}) collective-permute-start(bf16[128,512]{1,0:T(8,128)(2,1)S(1)} %get-tuple-element.27), channel_id=1, source_target_pairs={{0,1},{1,0},{2,3},{3,2},{4,5},{5,4},{6,7},{7,6},{8,9},{9,8},{10,11... | collective-permute-start | bytes 393224 | tf_op jit(solution)/shard_map/ppermute | solution.py:404
  65.1 1.7 %keep.1 = (bf16[128,512]{1,0:T(8,128)(2,1)}, f32[128,512]{1,0:T(8,128)S(1)}) custom-call(bf16[128,512]{1,0:T(8,128)(2,1)S(1)} %get-tuple-element.19.own_ref, bf16[512,4096]{1,0:T(8,128)(2,1)} %weight_ref.5), custom_call_target="tpu_custom_call" | custom-call | tf_op jit(solution)/shard_map/keep/pallas_call | solution.py:393
  66.8 0.0 collective-permute-done.4.refs_1_
  66.9 1.9 %collective-permute-done.5.refs_2_ = bf16[128,512]{1,0:T(8,128)(2,1)S(1)} collective-permute-done((bf16[128,512]{1,0:T(8,128)(2,1)S(1)}, bf16[128,512]{1,0:T(8,128)(2,1)S(1)}, u32[]{:S(2)}, u32[]{:S(2)}) %collective-permute-start.5) | collective-permute-done | bytes 131104 | tf_op jit(solution)/shard_map/ppermute | solution.py:403
  68.7 0.0 collective-permute-done.6.refs_3_
  68.7 0.7 %collective-permute-done.7.refs_4_ = bf16[128,512]{1,0:T(8,128)(2,1)S(1)} collective-permute-done((bf16[128,512]{1,0:T(8,128)(2,1)S(1)}, bf16[128,512]{1,0:T(8,128)(2,1)S(1)}, u32[]{:S(2)}, u32[]{:S(2)}) %collective-permute-start.7) | collective-permute-done | bytes 131104 | tf_op jit(solution)/shard_map/ppermute | solution.py:404
  69.4 0.7 %sum.1 = bf16[128,512]{1,0:T(8,128)(2,1)} custom-call(f32[128,512]{1,0:T(8,128)S(1)} %get-tuple-element.21.refs_0_, bf16[128,512]{1,0:T(8,128)(2,1)S(1)} %collective-permute-done.4.refs_1_, bf16[128,512]{1,0:T(8,128)(2,1)S(1)} %collective-permute-done.5.refs_2_, bf16[128,512]{1,0:T(8,128)(2,1)S(1)} %collective-permute-done.6.refs_3_, ...), custom_call_target="tpu_custom_call" | custom-call | tf_op jit(solution)/shard_map/sum/pallas_call | solution.py:405
  (2 shorter events, 0.0 us)
Async XLA Ops:
  0.6 27.4 %copy-start.6 = (bf16[64,384]{1,0:T(8,128)(2,1)S(1)}, bf16[64,384]{1,0:T(8,128)(2,1)}, u32[]{:S(2)}) copy-start(bf16[64,384]{1,0:T(8,128)(2,1)} %constant.23.clone.last_ref) | copy-start | bytes 147460
  0.6 27.4 %copy-start.1 = (bf16[256,256]{1,0:T(8,128)(2,1)S(1)}, bf16[256,256]{1,0:T(8,128)(2,1)}, u32[]{:S(2)}) copy-start(bf16[256,256]{1,0:T(8,128)(2,1)} %constant.22.clone.back_low) | copy-start | bytes 393220
  0.7 27.4 %copy-start.2 = (bf16[256,256]{1,0:T(8,128)(2,1)S(1)}, bf16[256,256]{1,0:T(8,128)(2,1)}, u32[]{:S(2)}) copy-start(bf16[256,256]{1,0:T(8,128)(2,1)} %constant.21.clone.back_high) | copy-start | bytes 393220
  0.7 27.4 %copy-start.3 = (bf16[256,256]{1,0:T(8,128)(2,1)S(1)}, bf16[256,256]{1,0:T(8,128)(2,1)}, u32[]{:S(2)}) copy-start(bf16[256,256]{1,0:T(8,128)(2,1)} %constant.20.clone.second_low) | copy-start | bytes 393220
  0.7 27.4 %copy-start.4 = (bf16[256,256]{1,0:T(8,128)(2,1)S(1)}, bf16[256,256]{1,0:T(8,128)(2,1)}, u32[]{:S(2)}) copy-start(bf16[256,256]{1,0:T(8,128)(2,1)} %constant.19.clone.second_high) | copy-start | bytes 393220
  0.7 27.4 %copy-start.7 = (f32[64,128]{1,0:T(8,128)S(1)}, f32[64,128]{1,0:T(8,128)}, u32[]{:S(2)}) copy-start(f32[64,128]{1,0:T(8,128)} %constant.18.clone.sin_ref) | copy-start | bytes 98308
  0.7 27.4 %copy-start.8 = (f32[64,128]{1,0:T(8,128)S(1)}, f32[64,128]{1,0:T(8,128)}, u32[]{:S(2)}) copy-start(f32[64,128]{1,0:T(8,128)} %constant.17.clone.cos_ref) | copy-start | bytes 98308
  0.7 27.4 %copy-start.5 = (bf16[128,192]{1,0:T(8,128)(2,1)S(1)}, bf16[128,192]{1,0:T(8,128)(2,1)}, u32[]{:S(2)}) copy-start(bf16[128,192]{1,0:T(8,128)(2,1)} %constant.16.clone.first_ref) | copy-start | bytes 147460
  0.7 27.4 %copy-start.9 = (f32[512]{0:T(512)S(1)}, f32[512]{0:T(512)}, u32[]{:S(2)}) copy-start(f32[512]{0:T(512)} %skip.1) | copy-start | bytes 6148
  2.8 25.3 %all-to-all-start = ((bf16[64,16,128]{2,1,0:T(8,128)(2,1)}), bf16[64,16,128]{2,1,0:T(8,128)(2,1)S(1)}, u32[]{:S(2)}, u32[]{:S(2)}) async-start(bf16[64,16,128]{2,1,0:T(8,128)(2,1)} %bitcast), calls=%async_computation | async-start | bytes 524288 | tf_op jit(solution)/shard_map/all_to_all | solution.py:333
  20.3 21.3 %collective-permute-start = (bf16[448,512]{1,0:T(8,128)(2,1)S(1)}, bf16[448,512]{1,0:T(8,128)(2,1)S(1)}, u32[]{:S(2)}, u32[]{:S(2)}) collective-permute-start(bf16[448,512]{1,0:T(8,128)(2,1)S(1)} %get-tuple-element.17), channel_id=1, source_target_pairs={{0,1},{1,0},{2,3},{3,2},{4,5},{5,4},{6,7},{7,6},{8,9},{9,8},{10,11... | collective-permute-start | bytes 1376264 | tf_op jit(solution)/shard_map/ppermute | solution.py:350
  23.5 20.5 %collective-permute-start.1 = (bf16[448,512]{1,0:T(8,128)(2,1)S(1)}, bf16[448,512]{1,0:T(8,128)(2,1)S(1)}, u32[]{:S(2)}, u32[]{:S(2)}) collective-permute-start(bf16[448,512]{1,0:T(8,128)(2,1)S(1)} %get-tuple-element.18), channel_id=1, source_target_pairs={{0,1},{1,0},{2,3},{3,2},{4,5},{5,4},{6,7},{7,6},{8,9},{9,8},{10,11... | collective-permute-start | bytes 1376264 | tf_op jit(solution)/shard_map/ppermute | solution.py:350
  31.2 19.1 %all-to-all-start.1 = ((bf16[128,8,128]{2,1,0:T(8,128)(2,1)}), bf16[128,8,128]{2,1,0:T(8,128)(2,1)S(1)}, u32[]{:S(2)}, u32[]{:S(2)}) async-start(bf16[128,8,128]{2,1,0:T(8,128)(2,1)} %bitcast.2), calls=%async_computation.1 | async-start | bytes 524288 | tf_op jit(solution)/shard_map/all_to_all | solution.py:373
  41.6 8.6 %collective-permute-start.2 = (bf16[448,512]{1,0:T(8,128)(2,1)S(1)}, bf16[448,512]{1,0:T(8,128)(2,1)S(1)}, u32[]{:S(2)}, u32[]{:S(2)}) collective-permute-start(bf16[448,512]{1,0:T(8,128)(2,1)S(1)} %hold.2.rest_0_), channel_id=1, source_target_pairs={{0,8},{8,0},{1,9},{9,1},{2,10},{10,2},{3,11},{11,3},{4,12},{12,4},... | collective-permute-start | bytes 1376264 | tf_op jit(solution)/shard_map/ppermute | solution.py:307
  43.9 6.3 %collective-permute-start.3 = (bf16[448,512]{1,0:T(8,128)(2,1)S(1)}, bf16[448,512]{1,0:T(8,128)(2,1)S(1)}, u32[]{:S(2)}, u32[]{:S(2)}) collective-permute-start(bf16[448,512]{1,0:T(8,128)(2,1)S(1)} %hold.3.rest_1_), channel_id=1, source_target_pairs={{0,8},{8,0},{1,9},{9,1},{2,10},{10,2},{3,11},{11,3},{4,12},{12,4},... | collective-permute-start | bytes 1376264 | tf_op jit(solution)/shard_map/ppermute | solution.py:307
  50.2 9.9 %copy-start = (bf16[2,512,512]{2,1,0:T(8,128)(2,1)S(1)}, bf16[2,512,512]{2,1,0:T(8,128)(2,1)}, u32[]{:S(2)}) copy-start(bf16[2,512,512]{2,1,0:T(8,128)(2,1)} %get-tuple-element.25.late_ref) | copy-start | bytes 3145732
  50.8 16.0 %collective-permute-start.4 = (bf16[128,512]{1,0:T(8,128)(2,1)S(1)}, bf16[128,512]{1,0:T(8,128)(2,1)S(1)}, u32[]{:S(2)}, u32[]{:S(2)}) collective-permute-start(bf16[128,512]{1,0:T(8,128)(2,1)S(1)} %get-tuple-element.22), channel_id=1, source_target_pairs={{0,6},{1,3},{2,0},{3,5},{4,2},{5,7},{6,4},{7,1},{8,14},{9,11},{10,... | collective-permute-start | bytes 393224 | tf_op jit(solution)/shard_map/ppermute | solution.py:403
  56.9 11.8 %collective-permute-start.5 = (bf16[128,512]{1,0:T(8,128)(2,1)S(1)}, bf16[128,512]{1,0:T(8,128)(2,1)S(1)}, u32[]{:S(2)}, u32[]{:S(2)}) collective-permute-start(bf16[128,512]{1,0:T(8,128)(2,1)S(1)} %get-tuple-element.23), channel_id=1, source_target_pairs={{0,5},{1,4},{2,7},{3,6},{4,1},{5,0},{6,3},{7,2},{8,13},{9,12},{10,... | collective-permute-start | bytes 393224 | tf_op jit(solution)/shard_map/ppermute | solution.py:403
  60.5 8.2 %collective-permute-start.6 = (bf16[128,512]{1,0:T(8,128)(2,1)S(1)}, bf16[128,512]{1,0:T(8,128)(2,1)S(1)}, u32[]{:S(2)}, u32[]{:S(2)}) collective-permute-start(bf16[128,512]{1,0:T(8,128)(2,1)S(1)} %get-tuple-element.26), channel_id=1, source_target_pairs={{0,7},{1,2},{2,1},{3,4},{4,3},{5,6},{6,5},{7,0},{8,15},{9,10},{10,... | collective-permute-start | bytes 393224 | tf_op jit(solution)/shard_map/ppermute | solution.py:403
  62.4 7.0 %collective-permute-start.7 = (bf16[128,512]{1,0:T(8,128)(2,1)S(1)}, bf16[128,512]{1,0:T(8,128)(2,1)S(1)}, u32[]{:S(2)}, u32[]{:S(2)}) collective-permute-start(bf16[128,512]{1,0:T(8,128)(2,1)S(1)} %get-tuple-element.27), channel_id=1, source_target_pairs={{0,1},{1,0},{2,3},{3,2},{4,5},{5,4},{6,7},{7,6},{8,9},{9,8},{10,11... | collective-permute-start | bytes 393224 | tf_op jit(solution)/shard_map/ppermute | solution.py:404

commit v7 on v6

--- a/solution.py
+++ b/solution.py
@@ -240,8 +240,8 @@
     count = max(index for _, _, index, _, _ in found)
     passed = [near_refs[piece][pl.ds(at, size), :] for piece, at, index, _, size in found if index == count]
     passed = jnp.concatenate(passed, axis=0)
-    other = (passed.astype(f32) * turned_ref[1 - side].astype(f32).T).astype(bf16)
-    own = (query_ref[...].astype(f32) * turned_ref[side].astype(f32).T).astype(bf16)
+    other = (passed.astype(f32) * turned_ref[side].astype(f32).T).astype(bf16)
+    own = (query_ref[...].astype(f32) * turned_ref[1 - side].astype(f32).T).astype(bf16)
     own_ref[...] = own
     other_ref[...] = other
     for i, partial_ref in enumerate(partial_refs):
@@ -375,7 +375,7 @@
         ("side",) + seq,
         split_axis=0,
         concat_axis=0,
-        axis_index_groups=[[side * seq_count + i for side in range(PAIR) for i in order]],
+        axis_index_groups=[[side * seq_count + i for side in (1, 0) for i in order]],
         tiled=True,
     ).reshape(PAIR, chans, rows)
     block = pltpu.VMEM((rows, width), bf16)

time: 70.8 us -> 70.8 us (level)
  no operation moved by 1% of the time
where the time goes in v7:
time: 70.8 us; the launch traced here: 70.2 us
  starting transfers between devices  51.7 us (73%)
  Pallas kernels  12.4 us (18%)
  waiting for transfers between devices  5.15 us (7%)
  between operations  0.96 us (1%)
    all_to_all x1, starting transfers between devices, shards(): lax.all_to_all(packed.reshape(seq_count, 2 * group, rows), seq, split_axi...  16.2 us
    ppermute x3, starting transfers between devices, shards(): parts.append(lax.ppermute(part, chan, pairs))  11 us
    all_to_all x1, starting transfers between devices, shards(): lax.all_to_all(turned.reshape(PAIR * seq_count, group, rows), ('side',) +...  10.9 us
    ppermute x2, starting transfers between devices, permuted_after(): return (array, lax.ppermute(array, axis, pairs))  5.6 us
    ppermute x2, starting transfers between devices, shards(): near = [lax.ppermute(x, 'side', swap) for x in near]  5.28 us
    pallas_call x1, Pallas kernels, shards(): call(functools.partial(convolve_kernel, group, seq_count), 'convolve', [p...  3.03 us
    ppermute x1, starting transfers between devices, shards(): parts.append(lax.ppermute(partner, 'side', swap))  2.68 us
    pallas_call x1, Pallas kernels, shards(): call(functools.partial(stage_kernel, steps, planes), 'stage', [pltpu.VMEM...  2.67 us
  transfers between devices with their start and end apart: 10, of which 3 were waited for; matrix products, arithmetic and copies ran while one was open for 0% of the time, Pallas kernels for 13%

profile of v7, /device:TPU:1, one launch (start us, length us, event | category | flops | bytes accessed | tf_op | source)
XLA Modules:
  0.0 70.2 jit_solution(1764482054856323222)
XLA Ops:
  0.6 0.0 copy-start.6
  0.6 0.0 copy-start.1
  0.7 0.0 copy-start.2
  0.7 0.0 copy-start.3
  0.7 0.0 copy-start.4
  0.7 0.0 copy-start.7
  0.7 0.0 copy-start.8
  0.7 0.0 copy-start.5
  0.7 0.0 copy-start.9
  0.7 2.0 %pack.1.packed_ref = bf16[1024,128]{1,0:T(8,128)(2,1)} custom-call(bf16[128,512]{1,0:T(8,128)(2,1)} %key_ref.1, bf16[128,512]{1,0:T(8,128)(2,1)} %value_ref.1, bf16[128,512]{1,0:T(8,128)(2,1)} %filter_ref.1), custom_call_target="tpu_custom_call" | custom-call | tf_op jit(solution)/shard_map/pack/pallas_call | solution.py:326
  2.8 16.2 %all-to-all-start = ((bf16[64,16,128]{2,1,0:T(8,128)(2,1)}), bf16[64,16,128]{2,1,0:T(8,128)(2,1)S(1)}, u32[]{:S(2)}, u32[]{:S(2)}) async-start(bf16[64,16,128]{2,1,0:T(8,128)(2,1)} %bitcast), calls=%async_computation | async-start | bytes 524288 | tf_op jit(solution)/shard_map/all_to_all | solution.py:333
  19.0 1.2 %ship.1 = (bf16[448,512]{1,0:T(8,128)(2,1)S(1)}, bf16[448,512]{1,0:T(8,128)(2,1)S(1)}) custom-call(bf16[128,512]{1,0:T(8,128)(2,1)} %query_ref.3, bf16[512,4096]{1,0:T(8,128)(2,1)} %weight_ref.5, bf16[1024,128]{1,0:T(8,128)(2,1)} %pack.1.packed_ref), custom_call_target="tpu_custom_call" | custom-call | tf_op jit(solution)/shard_map/ship/pallas_call | solution.py:343
  20.3 3.2 %collective-permute-start = (bf16[448,512]{1,0:T(8,128)(2,1)S(1)}, bf16[448,512]{1,0:T(8,128)(2,1)S(1)}, u32[]{:S(2)}, u32[]{:S(2)}) collective-permute-start(bf16[448,512]{1,0:T(8,128)(2,1)S(1)} %get-tuple-element.17), channel_id=1, source_target_pairs={{0,1},{1,0},{2,3},{3,2},{4,5},{5,4},{6,7},{7,6},{8,9},{9,8},{10,11... | collective-permute-start | bytes 1376264 | tf_op jit(solution)/shard_map/ppermute | solution.py:350
  23.5 2.1 %collective-permute-start.1 = (bf16[448,512]{1,0:T(8,128)(2,1)S(1)}, bf16[448,512]{1,0:T(8,128)(2,1)S(1)}, u32[]{:S(2)}, u32[]{:S(2)}) collective-permute-start(bf16[448,512]{1,0:T(8,128)(2,1)S(1)} %get-tuple-element.18), channel_id=1, source_target_pairs={{0,1},{1,0},{2,3},{3,2},{4,5},{5,4},{6,7},{7,6},{8,9},{9,8},{10,11... | collective-permute-start | bytes 1376264 | tf_op jit(solution)/shard_map/ppermute | solution.py:350
  25.6 2.5 %all-to-all-done = bf16[64,16,128]{2,1,0:T(8,128)(2,1)S(1)} async-done(((bf16[64,16,128]{2,1,0:T(8,128)(2,1)}), bf16[64,16,128]{2,1,0:T(8,128)(2,1)S(1)}, u32[]{:S(2)}, u32[]{:S(2)}) %all-to-all-start) | async-done | bytes 262176 | tf_op jit(solution)/shard_map/all_to_all | solution.py:333
  28.1 0.0 copy-done.6
  28.1 0.0 copy-done.1
  28.1 0.0 copy-done.2
  28.1 0.0 copy-done.3
  28.1 0.0 copy-done.4
  28.1 0.0 copy-done.7
  28.1 0.0 copy-done.8
  28.1 0.0 copy-done.5
  28.1 0.0 copy-done.9
  28.1 3.0 %convolve.1.after_ref.refs_1_ = bf16[2,512,128]{2,1,0:T(8,128)(2,1)} custom-call(f32[512]{0:T(512)S(1)} %copy-done.9, bf16[1024,128]{1,0:T(8,128)(2,1)S(1)} %bitcast.4, bf16[128,192]{1,0:T(8,128)(2,1)S(1)} %copy-done.5, f32[64,128]{1,0:T(8,128)S(1)} %copy-done.8, f32[64,128]{1,0:T(8,128)S(1)} %copy-done.7, bf16[256,256]{1,0:T(8,128)(2,1)S(1)} %copy-done.4, ...), custom_call_target="tpu_custom_call" | custom-call | tf_op jit(solution)/shard_map/convolve/pallas_call | solution.py:351
  31.2 10.9 %all-to-all-start.1 = ((bf16[128,8,128]{2,1,0:T(8,128)(2,1)}), bf16[128,8,128]{2,1,0:T(8,128)(2,1)S(1)}, u32[]{:S(2)}, u32[]{:S(2)}) async-start(bf16[128,8,128]{2,1,0:T(8,128)(2,1)} %bitcast.2), calls=%async_computation.1 | async-start | bytes 524288 | tf_op jit(solution)/shard_map/all_to_all | solution.py:373
  42.0 0.0 collective-permute-done.refs_0_
  42.1 2.3 %collective-permute-start.2 = (bf16[448,512]{1,0:T(8,128)(2,1)S(1)}, bf16[448,512]{1,0:T(8,128)(2,1)S(1)}, u32[]{:S(2)}, u32[]{:S(2)}) collective-permute-start(bf16[448,512]{1,0:T(8,128)(2,1)S(1)} %hold.2.rest_0_), channel_id=1, source_target_pairs={{0,8},{8,0},{1,9},{9,1},{2,10},{10,2},{3,11},{11,3},{4,12},{12,4},... | collective-permute-start | bytes 1376264 | tf_op jit(solution)/shard_map/ppermute | solution.py:307
  44.4 0.0 collective-permute-done.1.refs_0_
  44.4 3.3 %collective-permute-start.3 = (bf16[448,512]{1,0:T(8,128)(2,1)S(1)}, bf16[448,512]{1,0:T(8,128)(2,1)S(1)}, u32[]{:S(2)}, u32[]{:S(2)}) collective-permute-start(bf16[448,512]{1,0:T(8,128)(2,1)S(1)} %hold.3.rest_1_), channel_id=1, source_target_pairs={{0,8},{8,0},{1,9},{9,1},{2,10},{10,2},{3,11},{11,3},{4,12},{12,4},... | collective-permute-start | bytes 1376264 | tf_op jit(solution)/shard_map/ppermute | solution.py:307
  47.7 2.7 %stage.1 = (bf16[2,512,512]{2,1,0:T(8,128)(2,1)S(1)}, bf16[128,512]{1,0:T(8,128)(2,1)S(1)}, bf16[2,512,512]{2,1,0:T(8,128)(2,1)}) custom-call(bf16[128,512]{1,0:T(8,128)(2,1)} %query_ref.3, bf16[512,4096]{1,0:T(8,128)(2,1)} %weight_ref.5, bf16[2,512,128]{2,1,0:T(8,128)(2,1)} %convolve.1.after_ref.refs_1_), custom_call_target="tpu_custom_call" | custom-call | tf_op jit(solution)/shard_map/stage/pallas_call | solution.py:360
  50.4 0.0 collective-permute-done.2.rest_2_
  50.4 0.0 collective-permute-done.3.rest_3_
  50.4 0.0 all-to-all-done.1
  50.4 0.0 copy-start
  50.4 0.6 gate.1
  51.0 5.9 %collective-permute-start.4 = (bf16[128,512]{1,0:T(8,128)(2,1)S(1)}, bf16[128,512]{1,0:T(8,128)(2,1)S(1)}, u32[]{:S(2)}, u32[]{:S(2)}) collective-permute-start(bf16[128,512]{1,0:T(8,128)(2,1)S(1)} %get-tuple-element.22), channel_id=1, source_target_pairs={{0,6},{1,3},{2,0},{3,5},{4,2},{5,7},{6,4},{7,1},{8,14},{9,11},{10,... | collective-permute-start | bytes 393224 | tf_op jit(solution)/shard_map/ppermute | solution.py:403
  56.9 3.2 %collective-permute-start.5 = (bf16[128,512]{1,0:T(8,128)(2,1)S(1)}, bf16[128,512]{1,0:T(8,128)(2,1)S(1)}, u32[]{:S(2)}, u32[]{:S(2)}) collective-permute-start(bf16[128,512]{1,0:T(8,128)(2,1)S(1)} %get-tuple-element.23), channel_id=1, source_target_pairs={{0,5},{1,4},{2,7},{3,6},{4,1},{5,0},{6,3},{7,2},{8,13},{9,12},{10,... | collective-permute-start | bytes 393224 | tf_op jit(solution)/shard_map/ppermute | solution.py:403
  60.1 0.0 copy-done
  60.1 0.4 near.1
  60.5 1.9 %collective-permute-start.6 = (bf16[128,512]{1,0:T(8,128)(2,1)S(1)}, bf16[128,512]{1,0:T(8,128)(2,1)S(1)}, u32[]{:S(2)}, u32[]{:S(2)}) collective-permute-start(bf16[128,512]{1,0:T(8,128)(2,1)S(1)} %get-tuple-element.26), channel_id=1, source_target_pairs={{0,7},{1,2},{2,1},{3,4},{4,3},{5,6},{6,5},{7,0},{8,15},{9,10},{10,... | collective-permute-start | bytes 393224 | tf_op jit(solution)/shard_map/ppermute | solution.py:403
  62.4 2.7 %collective-permute-start.7 = (bf16[128,512]{1,0:T(8,128)(2,1)S(1)}, bf16[128,512]{1,0:T(8,128)(2,1)S(1)}, u32[]{:S(2)}, u32[]{:S(2)}) collective-permute-start(bf16[128,512]{1,0:T(8,128)(2,1)S(1)} %get-tuple-element.27), channel_id=1, source_target_pairs={{0,1},{1,0},{2,3},{3,2},{4,5},{5,4},{6,7},{7,6},{8,9},{9,8},{10,11... | collective-permute-start | bytes 393224 | tf_op jit(solution)/shard_map/ppermute | solution.py:404
  65.1 1.7 %keep.1 = (bf16[128,512]{1,0:T(8,128)(2,1)}, f32[128,512]{1,0:T(8,128)S(1)}) custom-call(bf16[128,512]{1,0:T(8,128)(2,1)S(1)} %get-tuple-element.19.own_ref, bf16[512,4096]{1,0:T(8,128)(2,1)} %weight_ref.5), custom_call_target="tpu_custom_call" | custom-call | tf_op jit(solution)/shard_map/keep/pallas_call | solution.py:393
  66.8 0.0 collective-permute-done.4.refs_1_
  66.9 1.9 %collective-permute-done.5.refs_2_ = bf16[128,512]{1,0:T(8,128)(2,1)S(1)} collective-permute-done((bf16[128,512]{1,0:T(8,128)(2,1)S(1)}, bf16[128,512]{1,0:T(8,128)(2,1)S(1)}, u32[]{:S(2)}, u32[]{:S(2)}) %collective-permute-start.5) | collective-permute-done | bytes 131104 | tf_op jit(solution)/shard_map/ppermute | solution.py:403
  68.8 0.0 collective-permute-done.6.refs_3_
  68.8 0.7 collective-permute-done.7.refs_4_
  69.5 0.7 %sum.1 = bf16[128,512]{1,0:T(8,128)(2,1)} custom-call(f32[128,512]{1,0:T(8,128)S(1)} %get-tuple-element.21.refs_0_, bf16[128,512]{1,0:T(8,128)(2,1)S(1)} %collective-permute-done.4.refs_1_, bf16[128,512]{1,0:T(8,128)(2,1)S(1)} %collective-permute-done.5.refs_2_, bf16[128,512]{1,0:T(8,128)(2,1)S(1)} %collective-permute-done.6.refs_3_, ...), custom_call_target="tpu_custom_call" | custom-call | tf_op jit(solution)/shard_map/sum/pallas_call | solution.py:405
  (2 shorter events, 0.0 us)
Async XLA Ops:
  0.6 27.4 %copy-start.6 = (bf16[64,384]{1,0:T(8,128)(2,1)S(1)}, bf16[64,384]{1,0:T(8,128)(2,1)}, u32[]{:S(2)}) copy-start(bf16[64,384]{1,0:T(8,128)(2,1)} %constant.23.clone.last_ref) | copy-start | bytes 147460
  0.6 27.4 %copy-start.1 = (bf16[256,256]{1,0:T(8,128)(2,1)S(1)}, bf16[256,256]{1,0:T(8,128)(2,1)}, u32[]{:S(2)}) copy-start(bf16[256,256]{1,0:T(8,128)(2,1)} %constant.22.clone.back_low) | copy-start | bytes 393220
  0.7 27.4 %copy-start.2 = (bf16[256,256]{1,0:T(8,128)(2,1)S(1)}, bf16[256,256]{1,0:T(8,128)(2,1)}, u32[]{:S(2)}) copy-start(bf16[256,256]{1,0:T(8,128)(2,1)} %constant.21.clone.back_high) | copy-start | bytes 393220
  0.7 27.4 %copy-start.3 = (bf16[256,256]{1,0:T(8,128)(2,1)S(1)}, bf16[256,256]{1,0:T(8,128)(2,1)}, u32[]{:S(2)}) copy-start(bf16[256,256]{1,0:T(8,128)(2,1)} %constant.20.clone.second_low) | copy-start | bytes 393220
  0.7 27.4 %copy-start.4 = (bf16[256,256]{1,0:T(8,128)(2,1)S(1)}, bf16[256,256]{1,0:T(8,128)(2,1)}, u32[]{:S(2)}) copy-start(bf16[256,256]{1,0:T(8,128)(2,1)} %constant.19.clone.second_high) | copy-start | bytes 393220
  0.7 27.4 %copy-start.7 = (f32[64,128]{1,0:T(8,128)S(1)}, f32[64,128]{1,0:T(8,128)}, u32[]{:S(2)}) copy-start(f32[64,128]{1,0:T(8,128)} %constant.18.clone.sin_ref) | copy-start | bytes 98308
  0.7 27.4 %copy-start.8 = (f32[64,128]{1,0:T(8,128)S(1)}, f32[64,128]{1,0:T(8,128)}, u32[]{:S(2)}) copy-start(f32[64,128]{1,0:T(8,128)} %constant.17.clone.cos_ref) | copy-start | bytes 98308
  0.7 27.4 %copy-start.5 = (bf16[128,192]{1,0:T(8,128)(2,1)S(1)}, bf16[128,192]{1,0:T(8,128)(2,1)}, u32[]{:S(2)}) copy-start(bf16[128,192]{1,0:T(8,128)(2,1)} %constant.16.clone.first_ref) | copy-start | bytes 147460
  0.7 27.4 %copy-start.9 = (f32[512]{0:T(512)S(1)}, f32[512]{0:T(512)}, u32[]{:S(2)}) copy-start(f32[512]{0:T(512)} %skip.1) | copy-start | bytes 6148
  2.8 25.3 %all-to-all-start = ((bf16[64,16,128]{2,1,0:T(8,128)(2,1)}), bf16[64,16,128]{2,1,0:T(8,128)(2,1)S(1)}, u32[]{:S(2)}, u32[]{:S(2)}) async-start(bf16[64,16,128]{2,1,0:T(8,128)(2,1)} %bitcast), calls=%async_computation | async-start | bytes 524288 | tf_op jit(solution)/shard_map/all_to_all | solution.py:333
  20.3 21.8 %collective-permute-start = (bf16[448,512]{1,0:T(8,128)(2,1)S(1)}, bf16[448,512]{1,0:T(8,128)(2,1)S(1)}, u32[]{:S(2)}, u32[]{:S(2)}) collective-permute-start(bf16[448,512]{1,0:T(8,128)(2,1)S(1)} %get-tuple-element.17), channel_id=1, source_target_pairs={{0,1},{1,0},{2,3},{3,2},{4,5},{5,4},{6,7},{7,6},{8,9},{9,8},{10,11... | collective-permute-start | bytes 1376264 | tf_op jit(solution)/shard_map/ppermute | solution.py:350
  23.5 20.9 %collective-permute-start.1 = (bf16[448,512]{1,0:T(8,128)(2,1)S(1)}, bf16[448,512]{1,0:T(8,128)(2,1)S(1)}, u32[]{:S(2)}, u32[]{:S(2)}) collective-permute-start(bf16[448,512]{1,0:T(8,128)(2,1)S(1)} %get-tuple-element.18), channel_id=1, source_target_pairs={{0,1},{1,0},{2,3},{3,2},{4,5},{5,4},{6,7},{7,6},{8,9},{9,8},{10,11... | collective-permute-start | bytes 1376264 | tf_op jit(solution)/shard_map/ppermute | solution.py:350
  31.2 19.2 %all-to-all-start.1 = ((bf16[128,8,128]{2,1,0:T(8,128)(2,1)}), bf16[128,8,128]{2,1,0:T(8,128)(2,1)S(1)}, u32[]{:S(2)}, u32[]{:S(2)}) async-start(bf16[128,8,128]{2,1,0:T(8,128)(2,1)} %bitcast.2), calls=%async_computation.1 | async-start | bytes 524288 | tf_op jit(solution)/shard_map/all_to_all | solution.py:373
  42.1 8.3 %collective-permute-start.2 = (bf16[448,512]{1,0:T(8,128)(2,1)S(1)}, bf16[448,512]{1,0:T(8,128)(2,1)S(1)}, u32[]{:S(2)}, u32[]{:S(2)}) collective-permute-start(bf16[448,512]{1,0:T(8,128)(2,1)S(1)} %hold.2.rest_0_), channel_id=1, source_target_pairs={{0,8},{8,0},{1,9},{9,1},{2,10},{10,2},{3,11},{11,3},{4,12},{12,4},... | collective-permute-start | bytes 1376264 | tf_op jit(solution)/shard_map/ppermute | solution.py:307
  44.4 6.0 %collective-permute-start.3 = (bf16[448,512]{1,0:T(8,128)(2,1)S(1)}, bf16[448,512]{1,0:T(8,128)(2,1)S(1)}, u32[]{:S(2)}, u32[]{:S(2)}) collective-permute-start(bf16[448,512]{1,0:T(8,128)(2,1)S(1)} %hold.3.rest_1_), channel_id=1, source_target_pairs={{0,8},{8,0},{1,9},{9,1},{2,10},{10,2},{3,11},{11,3},{4,12},{12,4},... | collective-permute-start | bytes 1376264 | tf_op jit(solution)/shard_map/ppermute | solution.py:307
  50.4 9.7 %copy-start = (bf16[2,512,512]{2,1,0:T(8,128)(2,1)S(1)}, bf16[2,512,512]{2,1,0:T(8,128)(2,1)}, u32[]{:S(2)}) copy-start(bf16[2,512,512]{2,1,0:T(8,128)(2,1)} %get-tuple-element.25.late_ref) | copy-start | bytes 3145732
  51.0 15.9 %collective-permute-start.4 = (bf16[128,512]{1,0:T(8,128)(2,1)S(1)}, bf16[128,512]{1,0:T(8,128)(2,1)S(1)}, u32[]{:S(2)}, u32[]{:S(2)}) collective-permute-start(bf16[128,512]{1,0:T(8,128)(2,1)S(1)} %get-tuple-element.22), channel_id=1, source_target_pairs={{0,6},{1,3},{2,0},{3,5},{4,2},{5,7},{6,4},{7,1},{8,14},{9,11},{10,... | collective-permute-start | bytes 393224 | tf_op jit(solution)/shard_map/ppermute | solution.py:403
  56.9 11.9 %collective-permute-start.5 = (bf16[128,512]{1,0:T(8,128)(2,1)S(1)}, bf16[128,512]{1,0:T(8,128)(2,1)S(1)}, u32[]{:S(2)}, u32[]{:S(2)}) collective-permute-start(bf16[128,512]{1,0:T(8,128)(2,1)S(1)} %get-tuple-element.23), channel_id=1, source_target_pairs={{0,5},{1,4},{2,7},{3,6},{4,1},{5,0},{6,3},{7,2},{8,13},{9,12},{10,... | collective-permute-start | bytes 393224 | tf_op jit(solution)/shard_map/ppermute | solution.py:403
  60.5 8.3 %collective-permute-start.6 = (bf16[128,512]{1,0:T(8,128)(2,1)S(1)}, bf16[128,512]{1,0:T(8,128)(2,1)S(1)}, u32[]{:S(2)}, u32[]{:S(2)}) collective-permute-start(bf16[128,512]{1,0:T(8,128)(2,1)S(1)} %get-tuple-element.26), channel_id=1, source_target_pairs={{0,7},{1,2},{2,1},{3,4},{4,3},{5,6},{6,5},{7,0},{8,15},{9,10},{10,... | collective-permute-start | bytes 393224 | tf_op jit(solution)/shard_map/ppermute | solution.py:403
  62.4 7.1 %collective-permute-start.7 = (bf16[128,512]{1,0:T(8,128)(2,1)S(1)}, bf16[128,512]{1,0:T(8,128)(2,1)S(1)}, u32[]{:S(2)}, u32[]{:S(2)}) collective-permute-start(bf16[128,512]{1,0:T(8,128)(2,1)S(1)} %get-tuple-element.27), channel_id=1, source_target_pairs={{0,1},{1,0},{2,3},{3,2},{4,5},{5,4},{6,7},{7,6},{8,9},{9,8},{10,11... | collective-permute-start | bytes 393224 | tf_op jit(solution)/shard_map/ppermute | solution.py:404
